TPU v7x, 32 devices: a whole 2x2x4 slice. The times are simulated.
32 devices in a mesh: groups: 2 (over x), dp: 16 (over z, y, core).
Axes of the slice: x: 2, y: 2, z: 4, core: 2. Of those that a mesh axis runs over, the one named last changes fastest.
Arguments:
- teacher_hidden: bfloat16 [256, 4096], P(('groups', 'dp')), parts along dimension 0, may hold values from -128 to 128
- student_hidden: bfloat16 [256, 4096], P(('groups', 'dp')), parts along dimension 0, may hold values from -128 to 128
- teacher_head: bfloat16 [4096, 8192], P(None, 'dp'), may hold values from -0.09375 to 0.09375
- student_head: bfloat16 [4096, 8192], P(None, 'dp'), may hold values from -0.09375 to 0.09375
- labels: int32 [256], P('groups'), parts along dimension 0, may hold values from 0 to 8191
- order: int32 [256], P('groups'), parts along dimension 0, may hold values from 0 to 127, each once
Outputs:
- row_loss: float32 [256], P(('groups', 'dp')), parts along dimension 0
- grad_hidden: float32 [256, 4096], P(('groups', 'dp')), parts along dimension 0
- grad_head: bfloat16 [8192, 8192], P('groups', 'dp'), parts along dimension 0
There are 2 independent parts, one for each index of `groups`. A program takes and returns all parts, laid end to end along the dimension named above; an argument that names none is the same for every part. Nothing has to cross between parts.
Inputs may be any that keep to these rules, and one draw needn't show every extreme that they name: `order`: a permutation of the rows.
All inputs are finite; a program needn't handle non-finite values.
Results may differ from a plain program's by a relative error of at most 0.0044.
Values may be sent and summed in bfloat16 or wider, within the bound.
No kernel may reach another device: no remote copies, remote signals or barrier semaphores. Data moves between devices by JAX's collectives and lax.ppermute only.
A program may use at most 128 MiB of HBM per device.

v0:
```python
import jax
import jax.numpy as jnp
from jax import lax
from jax.sharding import PartitionSpec as P

CE_WEIGHT = 0.5


def per_device(teacher_hidden, student_hidden, teacher_head, student_head, labels, order):
    rows_local = student_hidden.shape[0]
    vocab_local = student_head.shape[1]
    teacher_unordered = jnp.dot(
        lax.all_gather(teacher_hidden, "dp", axis=0, tiled=True),
        teacher_head,
        preferred_element_type=jnp.float32,
    )
    teacher_logits = jnp.take(teacher_unordered, order, axis=0)
    student_all = lax.all_gather(student_hidden, "dp", axis=0, tiled=True)
    student_logits = jnp.dot(student_all, student_head, preferred_element_type=jnp.float32)
    columns = lax.axis_index("dp") * vocab_local + lax.iota(jnp.int32, vocab_local)
    is_label = labels[:, None] == columns[None, :]
    label_part = jnp.sum(
        jnp.where(is_label, student_logits, jnp.zeros_like(student_logits)), axis=1
    )
    teacher_local = jnp.max(teacher_logits, axis=1)
    student_local = jnp.max(student_logits, axis=1)
    teacher_max, student_max = lax.pmax((teacher_local, student_local), "dp")
    teacher_exp = jnp.exp(teacher_logits - teacher_max[:, None])
    student_exp = jnp.exp(student_logits - student_max[:, None])
    teacher_total, student_total, cross, label_logit = lax.psum(
        (
            jnp.sum(teacher_exp, axis=1),
            jnp.sum(student_exp, axis=1),
            jnp.sum(teacher_exp * (teacher_logits - student_logits), axis=1),
            label_part,
        ),
        "dp",
    )
    teacher_norm = teacher_max + jnp.log(teacher_total)
    student_norm = student_max + jnp.log(student_total)
    loss_all = (
        cross / teacher_total
        - teacher_norm
        + student_norm
        + CE_WEIGHT * (student_norm - label_logit)
    )
    row_loss = lax.dynamic_slice_in_dim(loss_all, lax.axis_index("dp") * rows_local, rows_local, 0)
    onehot = jnp.where(is_label, 1.0, 0.0).astype(jnp.float32)
    logit_grad = (
        (1.0 + CE_WEIGHT) * jnp.exp(student_logits - student_norm[:, None])
        - jnp.exp(teacher_logits - teacher_norm[:, None])
        - CE_WEIGHT * onehot
    ).astype(jnp.bfloat16)
    grad_head = lax.dot_general(
        student_all, logit_grad, (((0,), (0,)), ((), ())), preferred_element_type=jnp.float32
    ).astype(jnp.bfloat16)
    grad_hidden = lax.psum_scatter(
        lax.dot_general(
            logit_grad, student_head, (((1,), (1,)), ((), ())), preferred_element_type=jnp.float32
        ),
        "dp",
        scatter_dimension=0,
        tiled=True,
    )
    return (row_loss, grad_hidden, grad_head)


def solution(mesh):
    in_specs = (
        P(("groups", "dp"), None),
        P(("groups", "dp"), None),
        P(None, "dp"),
        P(None, "dp"),
        P("groups"),
        P("groups"),
    )
    out_specs = (P(("groups", "dp")), P(("groups", "dp"), None), P("groups", "dp"))
    return jax.shard_map(
        per_device, mesh=mesh, in_specs=in_specs, out_specs=out_specs, check_vma=False
    )
```

profile of v0, /device:TPU:0, one launch (start us, length us, event | category | flops | bytes accessed | tf_op | source)
XLA Modules:
  0.0 225.3 jit_solution(967322349798619806)
XLA Ops:
  7.2 0.0 all-gather.3.cloned.1.call-start
  7.2 0.7 all-gather.3.cloned.1.call-update
  7.9 0.0 all-gather.5.cloned.1.call-start
  7.9 0.7 all-gather.5.cloned.1.call-update
  8.6 0.0 reduce-scatter.2.cloned.1.call-start
  8.7 0.7 compare_select_fusion.2
  9.4 0.7 compare_and_fusion
  10.0 40.8 %all-gather.3.cloned.1.call-done = bf16[128,4096]{1,0:T(8,128)(2,1)} async-done(((bf16[8,4096]{1,0:T(8,128)(2,1)}), bf16[128,4096]{1,0:T(8,128)(2,1)}) %all-gather.3.cloned.1.call-update) | async-done | bytes 1048592 | tf_op jit(solution)/shard_map/all_gather | solution.py:13
  50.8 3.2 %fusion.10 = f32[128,512]{1,0:T(8,128)S(1)} fusion(bf16[128,4096]{1,0:T(8,128)(2,1)} %all-gather.3.cloned.1.call-done, bf16[4096,512]{1,0:T(8,128)(2,1)} %param.8), kind=kOutput, calls=%fused_computation.23 | convolution fusion | flops 536870912 | bytes 5505024 | tf_op jit(solution)/shard_map/dot_general | solution.py:12
  54.1 0.0 copy-start.1
  54.1 0.8 gather_fusion
  54.8 0.2 select_reduce_fusion
  55.0 34.9 %all-gather.5.cloned.1.call-done = bf16[128,4096]{1,0:T(8,128)(2,1)} async-done(((bf16[8,4096]{1,0:T(8,128)(2,1)}), bf16[128,4096]{1,0:T(8,128)(2,1)}) %all-gather.5.cloned.1.call-update) | async-done | bytes 1048592 | tf_op jit(solution)/shard_map/all_gather | solution.py:18
  89.9 3.3 %fusion.9 = (f32[128]{0:T(128)S(1)}, f32[128,512]{1,0:T(8,128)S(1)}) fusion(bf16[128,4096]{1,0:T(8,128)(2,1)} %all-gather.5.cloned.1.call-done, bf16[4096,512]{1,0:T(8,128)(2,1)} %param.9), kind=kOutput, calls=%fused_computation.22 | convolution fusion | flops 536936320 | bytes 5505536 | tf_op jit(solution)/shard_map/dot_general | solution.py:19
  93.2 31.6 %all-reduce.1 = (f32[128]{0:T(128)S(1)}, f32[128]{0:T(128)S(1)}) all-reduce(f32[128]{0:T(128)S(1)} %get-tuple-element.19, f32[128]{0:T(128)S(1)} %select_reduce_fusion), channel_id=1, replica_groups=mesh['groups'=2,'dp'=16] {'dp'}, use_global_device_ids=true, to_apply=%region_7.8 | all-reduce | flops 256 | bytes 2048 | tf_op jit(solution)/shard_map/pmax | solution.py:27
  124.8 0.0 copy-done.1
  124.8 0.3 fusion.5
  125.1 29.5 %all-reduce = (f32[128]{0:T(128)S(1)}, f32[128]{0:T(128)S(1)}, f32[128]{0:T(128)S(1)}, f32[128]{0:T(128)S(1)}) all-reduce(f32[128]{0:T(128)S(1)} %get-tuple-element.9, f32[128]{0:T(128)S(1)} %get-tuple-element.8, f32[128]{0:T(128)S(1)} %get-tuple-element.7, f32[128]{0:T(128)S(1)} %get-tuple-element.6), channel_id=1, replica_groups=mesh['groups'=2,'dp'=16] {'dp'}, use_global_device_ids=true, to_apply=%region_9.10 | all-reduce | flops 512 | bytes 4096 | tf_op jit(solution)/shard_map/psum | solution.py:30
  154.6 0.0 copy-start
  154.6 5.1 %fusion.7 = f32[128,4096]{1,0:T(8,128)} fusion(bf16[4096,512]{1,0:T(8,128)(2,1)} %param.9, f32[128,512]{1,0:T(8,128)S(1)} %get-tuple-element.20, f32[128,512]{1,0:T(8,128)S(1)} %gather_fusion, f32[128]{0:T(128)S(1)} %get-tuple-element.18, f32[128]{0:T(128)S(1)} %get-tuple-element.17, s32[512]{0:T(512)S(1)} %iota_add_fusion, s32[128]{0:T(128)S(1)} %copy-done.1, ...), kind=kOutput, calls=%fused_computation.21 | convolution fusion | flops 537526272 | bytes 6819456 | tf_op jit(solution)/shard_map/dot_general | solution.py:58
  159.8 0.0 reduce-scatter.2.cloned.1.call-update
  159.8 0.0 copy-done
  159.8 3.4 %fusion = bf16[4096,512]{0,1:T(8,128)(2,1)} fusion(bf16[128,4096]{1,0:T(8,128)(2,1)S(1)} %copy-done, f32[128,512]{1,0:T(8,128)S(1)} %get-tuple-element.20, f32[128,512]{1,0:T(8,128)S(1)} %gather_fusion, f32[128]{0:T(128)S(1)} %get-tuple-element.18, f32[128]{0:T(128)S(1)} %get-tuple-element.17, s32[512]{0:T(512)S(1)} %iota_add_fusion, s32[128]{0:T(128)S(1)} %copy-done.1, ...), kind=kOutput, calls=%fused_computation.2 | convolution fusion | flops 539623424 | bytes 5770880 | tf_op jit(solution)/shard_map/dot_general | solution.py:54
  163.2 6.5 %copy.9 = bf16[4096,512]{1,0:T(8,128)(2,1)} copy(bf16[4096,512]{0,1:T(8,128)(2,1)} %fusion) | data formatting | bytes 8388608
  169.6 0.6 dynamic_slice.3
  170.2 48.6 %reduce-scatter.2.cloned.1.call-done = f32[8,4096]{1,0:T(8,128)} async-done(((f32[128,4096]{1,0:T(8,128)}), f32[8,4096]{1,0:T(8,128)}) %reduce-scatter.2.cloned.1.call-update) | async-done | bytes 131088 | tf_op jit(solution)/shard_map/reduce_scatter | solution.py:57
  (3 shorter events, 0.0 us)
Async XLA Ops:
  7.2 43.7 %all-gather.3.cloned.1.call-start = ((), (), s32[]{:S(2)}) async-start(), calls=%async_computation.1 | async-start | bytes 1114112 | tf_op jit(solution)/shard_map/all_gather | solution.py:13
  7.9 82.0 %all-gather.5.cloned.1.call-start = ((), (), s32[]{:S(2)}) async-start(), calls=%async_computation.2 | async-start | bytes 1114112 | tf_op jit(solution)/shard_map/all_gather | solution.py:18
  8.6 210.1 %reduce-scatter.2.cloned.1.call-start = ((), (), s32[]{:S(2)}) async-start(), calls=%async_computation.3 | async-start | bytes 2228224 | tf_op jit(solution)/shard_map/reduce_scatter | solution.py:57
  54.1 70.8 %copy-start.1 = (s32[128]{0:T(128)S(1)}, s32[128]{0:T(128)}, u32[]{:S(2)}) copy-start(s32[128]{0:T(128)} %param.10) | copy-start | bytes 1540
  154.6 5.2 %copy-start = (bf16[128,4096]{1,0:T(8,128)(2,1)S(1)}, bf16[128,4096]{1,0:T(8,128)(2,1)}, u32[]{:S(2)}) copy-start(bf16[128,4096]{1,0:T(8,128)(2,1)} %all-gather.5.cloned.1.call-done) | copy-start | bytes 3145732
Sparse Core Ops, SparseCore 0:
  10.2 40.6 all-gather.2
  53.0 36.8 all-gather.4
  159.9 58.8 reduce-scatter.1
where the time goes:
time: 226 us; the launch traced here: 225 us
  waiting for transfers between devices  126 us (56%)
  blocking collectives  61.1 us (27%)
  matrix products  15 us (7%)
  between operations  13.8 us (6%)
  local copies, waits for them, and re-layouts  7.82 us (3%)
    reduce_scatter x1, waiting for transfers between devices, per_device(): lax.psum_scatter(lax.dot_general(logit_grad, student_head, (((1,), (1,)),...  48.6 us
    all_gather x1, waiting for transfers between devices, per_device(): lax.all_gather(teacher_hidden, 'dp', axis=0, tiled=True)  40.8 us
    all_gather x1, waiting for transfers between devices, per_device(): student_all = lax.all_gather(student_hidden, 'dp', axis=0, tiled=True)  34.9 us
    pmax x1, blocking collectives, per_device(): teacher_max, student_max = lax.pmax((teacher_local, student_local), 'dp')  31.6 us
    psum x1, blocking collectives, per_device(): lax.psum((jnp.sum(teacher_exp, axis=1), jnp.sum(student_exp, axis=1), jnp...  29.5 us
    unnamed x5, local copies, waits for them, and re-layouts  6.48 us
    dot_general x1, matrix products, per_device(): lax.dot_general(logit_grad, student_head, (((1,), (1,)), ((), ())), prefe...  5.12 us
  transfers between devices with their start and end apart: 3, of which 3 were waited for; matrix products, arithmetic and copies ran while one was open for 7% of the time, Pallas kernels for 0%

commit v1 on v0

v1 whole, which is shorter than its diff:
```python
import functools

import jax
import jax.numpy as jnp
from jax import lax
from jax.experimental import pallas as pl
from jax.experimental.pallas import tpu as pltpu
from jax.sharding import PartitionSpec as P

CE_WEIGHT = 0.5
STATS = 8


def xor_order(n):
    return (0, 4, 2, 6, 8, 12, 10, 14, 1, 5, 3, 7, 9, 13, 11, 15) if n == 16 else None


def held_rows(shape, dim, me, rows_local, tuned):
    held = lax.broadcasted_iota(jnp.int32, shape, dim)
    if not tuned:
        return held
    step = rows_local.bit_length() - 1
    block = lax.shift_right_logical(held, step)
    bit = lambda k: lax.shift_right_logical(block, k) & 1
    distance = bit(3) + bit(2) * 8 + bit(1) * 2 + bit(0) * 4
    return (me ^ distance) * rows_local + (held & (rows_local - 1))


def to_column(is_row, row):
    return jnp.sum(jnp.where(is_row, row, 0.0), axis=1, keepdims=True)


def logits_kernel(rows_local, tuned, parts, me_ref, order_ref, labels_ref, *refs):
    teacher_rows, student_rows = refs[:parts], refs[parts : 2 * parts]
    teacher_head, student_head, teacher_out, student_out, stats_out, teacher_acc, student_acc = refs[2 * parts :]
    step = pl.program_id(0)

    @pl.when(step == 0)
    def _():
        teacher_acc[...] = jnp.zeros_like(teacher_acc)
        student_acc[...] = jnp.zeros_like(student_acc)

    def rows(pieces):
        return jnp.concatenate([piece[...] for piece in pieces], axis=0)

    teacher_acc[...] += jnp.dot(rows(teacher_rows), teacher_head[...], preferred_element_type=jnp.float32)
    student_acc[...] += jnp.dot(rows(student_rows), student_head[...], preferred_element_type=jnp.float32)

    @pl.when(step == pl.num_programs(0) - 1)
    def _():
        me = me_ref[0]
        count, vocab = student_acc.shape
        lanes = lax.broadcasted_iota(jnp.int32, (count, count), 1)
        is_row = held_rows((count, count), 0, me, rows_local, tuned) == lanes
        wanted = to_column(is_row, order_ref[...].astype(jnp.float32))
        have = held_rows((count, count), 1, me, rows_local, tuned).astype(jnp.float32)
        pick = jnp.where(wanted == have, 1.0, 0.0).astype(jnp.bfloat16)
        raw = teacher_acc[...]
        high = raw.astype(jnp.bfloat16)
        rest = raw - high.astype(jnp.float32)
        middle = rest.astype(jnp.bfloat16)
        low = (rest - middle.astype(jnp.float32)).astype(jnp.bfloat16)
        teacher = sum(jnp.dot(pick, piece, preferred_element_type=jnp.float32) for piece in (high, middle, low))
        student = student_acc[...]
        teacher_out[...] = teacher
        student_out[...] = student
        label = to_column(is_row, labels_ref[...].astype(jnp.float32)).astype(jnp.int32)
        is_label = label == lax.broadcasted_iota(jnp.int32, (count, vocab), 1) + me * vocab
        teacher_max = jnp.max(teacher, axis=1, keepdims=True)
        student_max = jnp.max(student, axis=1, keepdims=True)
        teacher_exp = jnp.exp(teacher - teacher_max)
        values = (
            teacher_max,
            student_max,
            jnp.sum(teacher_exp, axis=1, keepdims=True),
            jnp.sum(jnp.exp(student - student_max), axis=1, keepdims=True),
            jnp.sum(teacher_exp * (teacher - student), axis=1, keepdims=True),
            jnp.sum(jnp.where(is_label, student, 0.0), axis=1, keepdims=True),
        )
        block = [jnp.sum(jnp.where(is_row, value, 0.0), axis=0, keepdims=True) for value in values]
        block.append(jnp.zeros((STATS - len(block), count), jnp.float32))
        stats_out[...] = jnp.broadcast_to(jnp.concatenate(block, axis=0)[None], stats_out.shape)


def logits(me, order, labels, hidden, heads, n, rows_local, tuned):
    count = sum(piece.shape[0] for piece in hidden)
    depth, vocab = heads[0].shape
    step = min(512, depth)
    steps = depth // step

    def columns(piece, first):
        return pl.BlockSpec((piece.shape[0], step), lambda k: (0, k + first))

    whole = lambda shape: pl.BlockSpec(shape, lambda k: (0,) * len(shape))
    return pl.pallas_call(
        functools.partial(logits_kernel, rows_local, tuned, len(hidden)),
        grid=(steps,),
        in_specs=[pl.BlockSpec(memory_space=pltpu.SMEM), whole((1, count)), whole((1, count))]
        + [columns(piece, 0) for piece in hidden]
        + [columns(piece, steps) for piece in hidden]
        + [pl.BlockSpec((step, vocab), lambda k: (k, 0))] * 2,
        out_specs=(whole((count, vocab)), whole((count, vocab)), whole((n, STATS, count))),
        out_shape=(
            jax.ShapeDtypeStruct((count, vocab), jnp.float32),
            jax.ShapeDtypeStruct((count, vocab), jnp.float32),
            jax.ShapeDtypeStruct((n, STATS, count), jnp.float32),
        ),
        scratch_shapes=[pltpu.VMEM((count, vocab), jnp.float32)] * 2,
        compiler_params=pltpu.CompilerParams(vmem_limit_bytes=40 * 2**20),
        cost_estimate=pl.CostEstimate(
            flops=4 * count * depth * vocab, bytes_accessed=4 * depth * (vocab + count), transcendentals=2 * count * vocab
        ),
    )(me, order[None], labels[None], *hidden, *hidden, *heads)


def grad_kernel(
    rows_local, tuned, me_ref, labels_ref, stats_ref, teacher_ref, student_ref, head_ref, keep_out, send_out, grad_out, loss_out
):
    @pl.when(pl.program_id(0) == 0)
    def _():
        me = me_ref[0]
        count, vocab = student_ref.shape
        devices = stats_ref.shape[0]
        top = stats_ref[0, 0:2]
        for d in range(1, devices):
            top = jnp.maximum(top, stats_ref[d, 0:2])
        totals = jnp.zeros((2, count), jnp.float32)
        cross = jnp.zeros((1, count), jnp.float32)
        label_logit = jnp.zeros((1, count), jnp.float32)
        for d in range(devices):
            weight = jnp.exp(stats_ref[d, 0:2] - top)
            totals += weight * stats_ref[d, 2:4]
            cross += weight[0:1] * stats_ref[d, 4:5]
            label_logit += stats_ref[d, 5:6]
        norms = top + jnp.log(totals)
        teacher_norm, student_norm = norms[0:1], norms[1:2]
        loss = cross / totals[0:1] - teacher_norm + student_norm + CE_WEIGHT * (student_norm - label_logit)
        lanes = lax.broadcasted_iota(jnp.int32, (count, count), 1)
        is_row = held_rows((count, count), 0, me, rows_local, tuned) == lanes
        mine = lax.broadcasted_iota(jnp.int32, (count, count), 0) + me * rows_local == lanes
        by_lane = lax.broadcasted_iota(jnp.int32, (count, count), 0) == lanes
        loss_out[...] = jnp.sum(jnp.where(by_lane, to_column(mine, loss), 0.0), axis=0, keepdims=True)
        label = to_column(is_row, labels_ref[...].astype(jnp.float32)).astype(jnp.int32)
        is_label = label == lax.broadcasted_iota(jnp.int32, (count, vocab), 1) + me * vocab
        grad_out[...] = (
            (1.0 + CE_WEIGHT) * jnp.exp(student_ref[...] - to_column(is_row, student_norm))
            - jnp.exp(teacher_ref[...] - to_column(is_row, teacher_norm))
            - jnp.where(is_label, CE_WEIGHT, 0.0)
        ).astype(jnp.bfloat16)

    part = lax.dot_general(
        grad_out[...], head_ref[...], (((1,), (1,)), ((), ())), preferred_element_type=jnp.float32
    )
    kept = keep_out.shape[0]
    keep_out[...] = part[:kept]
    if send_out is not None:
        send_out[...] = part[kept:].astype(jnp.bfloat16)


def gradient(me, labels, stats, teacher_logits, student_logits, head, rows_local, tuned):
    count, vocab = student_logits.shape
    depth = head.shape[0]
    step = min(512, depth)
    kept = count // 2 if tuned else count
    whole = lambda shape: pl.BlockSpec(shape, lambda k: (0,) * len(shape))
    column = lambda rows: pl.BlockSpec((rows, step), lambda k: (0, k))
    shapes = [jax.ShapeDtypeStruct((kept, depth), jnp.float32)]
    specs = [column(kept)]
    if tuned:
        shapes.append(jax.ShapeDtypeStruct((count - kept, depth), jnp.bfloat16))
        specs.append(column(count - kept))
    shapes += [jax.ShapeDtypeStruct((count, vocab), jnp.bfloat16), jax.ShapeDtypeStruct((1, count), jnp.float32)]
    specs += [whole((count, vocab)), whole((1, count))]

    def kernel(*refs):
        if tuned:
            grad_kernel(rows_local, tuned, *refs)
        else:
            grad_kernel(rows_local, tuned, *refs[:7], None, *refs[7:])

    return pl.pallas_call(
        kernel,
        grid=(depth // step,),
        in_specs=[
            pl.BlockSpec(memory_space=pltpu.SMEM),
            whole((1, count)),
            whole(stats.shape),
            whole((count, vocab)),
            whole((count, vocab)),
            pl.BlockSpec((step, vocab), lambda k: (k, 0)),
        ],
        out_specs=tuple(specs),
        out_shape=tuple(shapes),
        compiler_params=pltpu.CompilerParams(vmem_limit_bytes=40 * 2**20),
        cost_estimate=pl.CostEstimate(
            flops=2 * count * depth * vocab, bytes_accessed=2 * depth * (vocab + 2 * count), transcendentals=2 * count * vocab
        ),
    )(me, labels[None], stats, teacher_logits, student_logits, head)


def head_kernel(parts, *refs):
    rows = jnp.concatenate([piece[...] for piece in refs[:parts]], axis=0)
    grad_ref, out_ref = refs[parts:]
    out_ref[...] = lax.dot_general(
        rows, grad_ref[...], (((0,), (0,)), ((), ())), preferred_element_type=jnp.float32
    ).astype(jnp.bfloat16)


def head_gradient(hidden, logit_grad, depth):
    count, vocab = logit_grad.shape
    step = min(512, depth)
    first = depth // step
    return pl.pallas_call(
        functools.partial(head_kernel, len(hidden)),
        grid=(depth // step,),
        in_specs=[pl.BlockSpec((piece.shape[0], step), lambda k: (0, k + first)) for piece in hidden]
        + [pl.BlockSpec((count, vocab), lambda k: (0, 0))],
        out_specs=pl.BlockSpec((step, vocab), lambda k: (k, 0)),
        out_shape=jax.ShapeDtypeStruct((depth, vocab), jnp.bfloat16),
        compiler_params=pltpu.CompilerParams(vmem_limit_bytes=40 * 2**20),
        cost_estimate=pl.CostEstimate(
            flops=2 * count * depth * vocab, bytes_accessed=2 * depth * (vocab + count), transcendentals=0
        ),
    )(*hidden, logit_grad)


def swap(value, distance, n):
    return lax.ppermute(value, "dp", [(i, i ^ distance) for i in range(n)])


def gather_rows(rows, n):
    far = swap(rows, 8, n)
    side = swap(rows, 2, n)
    near = swap(rows, 4, n)
    far_near = swap(far, 4, n)
    near_side = swap(near, 2, n)
    far_side = swap(far, 2, n)
    far_near_side = swap(far_near, 2, n)
    first = jnp.concatenate([rows, near, side, near_side], axis=0)
    second = jnp.concatenate([far, far_near, far_side, far_near_side], axis=0)
    return [first, second, swap(first, 1, n), swap(second, 1, n)]


def scatter_rows(keep, send, rows_local, n):
    low = jnp.bfloat16
    full = jnp.float32
    held = keep + swap(send, 1, n).astype(full)
    quarter = 2 * rows_local
    near_keep, near_send, far_keep, far_send = (held[k * quarter : (k + 1) * quarter] for k in range(4))
    far = (far_keep + swap(far_send.astype(low), 2, n).astype(full)).astype(low)
    near = near_keep + swap(near_send.astype(low), 2, n).astype(full)
    from_far = swap(far[:rows_local], 8, n)
    from_far_near = swap(far[rows_local:], 12, n)
    from_near = swap(near[rows_local:].astype(low), 4, n)
    return near[:rows_local] + from_far.astype(full) + from_far_near.astype(full) + from_near.astype(full)


def per_device(n, teacher_hidden, student_hidden, teacher_head, student_head, labels, order):
    rows_local, depth = student_hidden.shape
    tuned = xor_order(n) is not None and rows_local == 8
    me = lax.axis_index("dp").astype(jnp.int32).reshape(1)
    rows = jnp.concatenate([teacher_hidden, student_hidden], axis=1)
    hidden = gather_rows(rows, n) if tuned else [lax.all_gather(rows, "dp", axis=0, tiled=True)]
    teacher_logits, student_logits, stats = logits(
        me, order, labels, hidden, (teacher_head, student_head), n, rows_local, tuned
    )
    stats = lax.all_to_all(stats, "dp", 0, 0)
    outs = gradient(me, labels, stats, teacher_logits, student_logits, student_head, rows_local, tuned)
    logit_grad, loss = outs[-2:]
    grad_head = head_gradient(hidden, logit_grad, depth)
    if tuned:
        grad_hidden = scatter_rows(outs[0], outs[1], rows_local, n)
    else:
        grad_hidden = lax.psum_scatter(outs[0], "dp", scatter_dimension=0, tiled=True)
    return (loss[0, :rows_local], grad_hidden, grad_head)


def solution(mesh):
    in_specs = (
        P(("groups", "dp"), None),
        P(("groups", "dp"), None),
        P(None, "dp"),
        P(None, "dp"),
        P("groups"),
        P("groups"),
    )
    out_specs = (P(("groups", "dp")), P(("groups", "dp"), None), P("groups", "dp"))
    return jax.shard_map(
        functools.partial(per_device, mesh.shape["dp"]),
        mesh=mesh,
        in_specs=in_specs,
        out_specs=out_specs,
        check_vma=False,
    )
```

time: 226 us -> 75.2 us (0.33)
  waiting for transfers between devices: 126 us -> 23.2 us
  blocking collectives: 61.1 us -> 12.9 us
  starting transfers between devices: 0.11 us -> 17.7 us
  matrix products: 15 us -> 0 us
  between operations: 13.8 us -> 0.79 us
  Pallas kernels: 0 us -> 11.3 us
    all_gather x2 -> x0, waiting for transfers between devices: 75.7 us -> none  [the longest x1 40.8 us: per_device(): lax.all_gather(teacher_hidden, 'dp', axis=0, tiled=True)]
    reduce_scatter x1 -> x0, waiting for transfers between devices: 48.6 us -> none  [per_device(): lax.psum_scatter(lax.dot_general(logit_grad, student_head, (((1,), (1,)),...]
    pmax x1 -> x0, blocking collectives: 31.6 us -> none  [per_device(): teacher_max, student_max = lax.pmax((teacher_local, student_local), 'dp')]
    psum x1 -> x0, blocking collectives: 29.5 us -> none  [per_device(): lax.psum((jnp.sum(teacher_exp, axis=1), jnp.sum(student_exp, axis=1), jnp...]
    ppermute x0 -> x15, waiting for transfers between devices: none -> 23.2 us  [swap(): return lax.ppermute(value, 'dp', [(i, i ^ distance) for i in range(n)])]
    ppermute x0 -> x15, starting transfers between devices: none -> 17.7 us  [swap(): return lax.ppermute(value, 'dp', [(i, i ^ distance) for i in range(n)])]
    dot_general x4 -> x0, matrix products: 15 us -> none  [the longest x1 5.12 us: per_device(): lax.dot_general(logit_grad, student_head, (((1,), (1,)), ((), ())), prefe...]
    all_to_all x0 -> x1, blocking collectives: none -> 12.9 us  [per_device(): stats = lax.all_to_all(stats, 'dp', 0, 0)]
  transfers between devices with their start and end apart: 3 -> 15, of which waited for: 3 -> 7; matrix products, arithmetic and copies ran while one was open for 7% -> 1% of each run, Pallas kernels for 0% -> 7%
where the time goes in v1:
time: 75.2 us; the launch traced here: 74.8 us
  waiting for transfers between devices  23.2 us (31%)
  starting transfers between devices  17.7 us (24%)
  blocking collectives  12.9 us (17%)
  Pallas kernels  11.3 us (15%)
  local copies, waits for them, and re-layouts  7.97 us (11%)
  other arithmetic  0.92 us (1%)
  between operations  0.79 us (1%)
    ppermute x15, waiting for transfers between devices, swap(): return lax.ppermute(value, 'dp', [(i, i ^ distance) for i in range(n)])  23.2 us
    ppermute x15, starting transfers between devices, swap(): return lax.ppermute(value, 'dp', [(i, i ^ distance) for i in range(n)])  17.7 us
    all_to_all x1, blocking collectives, per_device(): stats = lax.all_to_all(stats, 'dp', 0, 0)  12.9 us
    unnamed x16, local copies, waits for them, and re-layouts  6.57 us
    pallas_call x1, Pallas kernels, head_gradient(): pl.pallas_call(functools.partial(head_kernel, len(hidden)), grid=(depth /...  4.86 us
    pallas_call x1, Pallas kernels, logits(): pl.pallas_call(functools.partial(logits_kernel, rows_local, tuned, len(hi...  3.57 us
    pallas_call x1, Pallas kernels, gradient(): pl.pallas_call(kernel, grid=(depth // step,), in_specs=[pl.BlockSpec(memo...  2.86 us
  transfers between devices with their start and end apart: 15, of which 7 were waited for; matrix products, arithmetic and copies ran while one was open for 1% of the time, Pallas kernels for 7%

profile of v1, /device:TPU:0, one launch (start us, length us, event | category | flops | bytes accessed | tf_op | source)
XLA Modules:
  0.0 74.8 jit_solution(10736444650104554814)
XLA Ops:
  0.6 0.8 %constant_dynamic-update-slice_fusion.1 = bf16[8,8192]{1,0:T(8,128)(2,1)S(1)} fusion(bf16[8,4096]{1,0:T(8,128)(2,1)} %param.6), kind=kLoop, calls=%fused_computation.10 | loop fusion | bytes 131072
  1.5 0.8 %constant_dynamic-update-slice_fusion = bf16[8,8192]{1,0:T(8,128)(2,1)S(1)} fusion(bf16[8,8192]{1,0:T(8,128)(2,1)S(1)} %constant_dynamic-update-slice_fusion.1, bf16[8,4096]{1,0:T(8,128)(2,1)} %param.7), kind=kLoop, calls=%fused_computation.9 | loop fusion | bytes 131072 | tf_op jit(solution)/shard_map/concatenate | solution.py:262
  2.3 4.0 %collective-permute-start.3 = (bf16[8,8192]{1,0:T(8,128)(2,1)S(1)}, bf16[8,8192]{1,0:T(8,128)(2,1)S(1)}, u32[]{:S(2)}, u32[]{:S(2)}) collective-permute-start(bf16[8,8192]{1,0:T(8,128)(2,1)S(1)} %constant_dynamic-update-slice_fusion), channel_id=1, source_target_pairs={{0,8},{1,9},{2,10},{3,11},{4,12},{5,13},{6,14},{7,15},{8,0},{9,1},... | collective-permute-start | bytes 393224 | tf_op jit(solution)/shard_map/ppermute | solution.py:228
  6.4 1.6 %collective-permute-start = (bf16[8,8192]{1,0:T(8,128)(2,1)S(1)}, bf16[8,8192]{1,0:T(8,128)(2,1)S(1)}, u32[]{:S(2)}, u32[]{:S(2)}) collective-permute-start(bf16[8,8192]{1,0:T(8,128)(2,1)S(1)} %constant_dynamic-update-slice_fusion), channel_id=1, source_target_pairs={{0,4},{1,5},{2,6},{3,7},{4,0},{5,1},{6,2},{7,3},{8,12},{9,13},{10,... | collective-permute-start | bytes 393224 | tf_op jit(solution)/shard_map/ppermute | solution.py:228
  7.9 1.5 %collective-permute-start.1 = (bf16[8,8192]{1,0:T(8,128)(2,1)S(1)}, bf16[8,8192]{1,0:T(8,128)(2,1)S(1)}, u32[]{:S(2)}, u32[]{:S(2)}) collective-permute-start(bf16[8,8192]{1,0:T(8,128)(2,1)S(1)} %constant_dynamic-update-slice_fusion), channel_id=1, source_target_pairs={{0,2},{1,3},{2,0},{3,1},{4,6},{5,7},{6,4},{7,5},{8,10},{9,11},{10,... | collective-permute-start | bytes 393224 | tf_op jit(solution)/shard_map/ppermute | solution.py:228
  9.5 3.3 %collective-permute-done.3 = bf16[8,8192]{1,0:T(8,128)(2,1)S(1)} collective-permute-done((bf16[8,8192]{1,0:T(8,128)(2,1)S(1)}, bf16[8,8192]{1,0:T(8,128)(2,1)S(1)}, u32[]{:S(2)}, u32[]{:S(2)}) %collective-permute-start.3) | collective-permute-done | bytes 131104 | tf_op jit(solution)/shard_map/ppermute | solution.py:228
  12.8 1.6 %collective-permute-start.5 = (bf16[8,8192]{1,0:T(8,128)(2,1)S(1)}, bf16[8,8192]{1,0:T(8,128)(2,1)S(1)}, u32[]{:S(2)}, u32[]{:S(2)}) collective-permute-start(bf16[8,8192]{1,0:T(8,128)(2,1)S(1)} %collective-permute-done.3), channel_id=1, source_target_pairs={{0,2},{1,3},{2,0},{3,1},{4,6},{5,7},{6,4},{7,5},{8,10},{9,11},{10,... | collective-permute-start | bytes 393224 | tf_op jit(solution)/shard_map/ppermute | solution.py:228
  14.3 0.6 collective-permute-start.4
  14.9 0.5 collective-permute-start.2
  15.4 5.1 %collective-permute-done.2 = bf16[8,8192]{1,0:T(8,128)(2,1)S(1)} collective-permute-done((bf16[8,8192]{1,0:T(8,128)(2,1)S(1)}, bf16[8,8192]{1,0:T(8,128)(2,1)S(1)}, u32[]{:S(2)}, u32[]{:S(2)}) %collective-permute-start.2) | collective-permute-done | bytes 131104 | tf_op jit(solution)/shard_map/ppermute | solution.py:228
  20.7 1.2 %collective-permute-start.6 = (bf16[8,8192]{1,0:T(8,128)(2,1)S(1)}, bf16[8,8192]{1,0:T(8,128)(2,1)S(1)}, u32[]{:S(2)}, u32[]{:S(2)}) collective-permute-start(bf16[8,8192]{1,0:T(8,128)(2,1)S(1)} %collective-permute-done.4), channel_id=1, source_target_pairs={{0,2},{1,3},{2,0},{3,1},{4,6},{5,7},{6,4},{7,5},{8,10},{9,11},{10,... | collective-permute-start | bytes 393224 | tf_op jit(solution)/shard_map/ppermute | solution.py:228
  21.9 4.7 %collective-permute-done.6 = bf16[8,8192]{1,0:T(8,128)(2,1)S(1)} collective-permute-done((bf16[8,8192]{1,0:T(8,128)(2,1)S(1)}, bf16[8,8192]{1,0:T(8,128)(2,1)S(1)}, u32[]{:S(2)}, u32[]{:S(2)}) %collective-permute-start.6) | collective-permute-done | bytes 131104 | tf_op jit(solution)/shard_map/ppermute | solution.py:228
  26.7 1.9 %collective-permute-done.8.refs_3_.refs_7_ = bf16[32,8192]{1,0:T(8,128)(2,1)S(1)} collective-permute-done((bf16[32,8192]{1,0:T(8,128)(2,1)S(1)}, bf16[32,8192]{1,0:T(8,128)(2,1)S(1)}, u32[]{:S(2)}, u32[]{:S(2)}) %collective-permute-start.8) | collective-permute-done | bytes 524320 | tf_op jit(solution)/shard_map/ppermute | solution.py:228
  28.6 2.2 %copy-done = bf16[4096,512]{1,0:T(8,128)(2,1)S(1)} copy-done((bf16[4096,512]{1,0:T(8,128)(2,1)S(1)}, bf16[4096,512]{1,0:T(8,128)(2,1)}, u32[]{:S(2)}) %copy-start) | copy-done | bytes 4194328
  30.8 2.2 %copy-done.2 = bf16[4096,512]{1,0:T(8,128)(2,1)S(1)} copy-done((bf16[4096,512]{1,0:T(8,128)(2,1)S(1)}, bf16[4096,512]{1,0:T(8,128)(2,1)}, u32[]{:S(2)}) %copy-start.2) | copy-done | bytes 4194328
  32.9 0.7 copy-done.3
  33.6 0.7 copy-done.5
  34.3 3.6 %shard_map.85 = (f32[128,512]{1,0:T(8,128)S(1)}, f32[128,512]{1,0:T(8,128)S(1)}, f32[16,8,128]{2,1,0:T(8,128)S(1)}) custom-call(s32[1]{0:T(128)} %bitcast.me_ref.refs_0_, s32[1,128]{1,0:T(1,128)S(1)} %bitcast.7, s32[1,128]{1,0:T(1,128)S(1)} %bitcast.5, bf16[32,8192]{1,0:T(8,128)(2,1)S(1)} %pad_maximum_fusion.refs_0_.refs_4_, ...), custom_call_target="tpu_custom_call" | custom-call | flops 1073741824 | bytes 10485760 | tf_op jit(solution)/shard_map/pallas_call | solution.py:95
  37.8 12.9 %all_to_all.5.refs_2_ = f32[16,8,128]{2,1,0:T(8,128)S(1)} all-to-all(f32[16,8,128]{2,1,0:T(8,128)S(1)} %get-tuple-element.10), channel_id=1, replica_groups=mesh['groups'=2,'dp'=16] {'dp'}, dimensions={0} | all-to-all | bytes 131072 | tf_op jit(solution)/shard_map/all_to_all | solution.py:267
  50.8 2.9 %shard_map.86 = (f32[64,4096]{1,0:T(8,128)S(1)}, bf16[64,4096]{1,0:T(8,128)(2,1)S(1)}, bf16[128,512]{1,0:T(8,128)(2,1)S(1)}, f32[1,128]{1,0:T(1,128)S(1)}) custom-call(s32[1]{0:T(128)} %bitcast.me_ref.refs_0_, s32[1,128]{1,0:T(1,128)S(1)} %bitcast.6, f32[16,8,128]{2,1,0:T(8,128)S(1)} %all_to_all.5.refs_2_, f32[128,512]{1,0:T(8,128)S(1)} %get-tuple-element.11.refs_3_, ...), custom_call_target="tpu_custom_call" | custom-call | flops 536870912 | bytes 6291456 | tf_op jit(solution)/shard_map/pallas_call | solution.py:181
  53.7 1.9 %collective-permute-done.9 = bf16[64,4096]{1,0:T(8,128)(2,1)S(1)} collective-permute-done((bf16[64,4096]{1,0:T(8,128)(2,1)S(1)}, bf16[64,4096]{1,0:T(8,128)(2,1)S(1)}, u32[]{:S(2)}, u32[]{:S(2)}) %collective-permute-start.9) | collective-permute-done | bytes 524320 | tf_op jit(solution)/shard_map/ppermute | solution.py:228
  55.6 0.2 fusion.3
  55.8 0.2 collective-permute-start.11
  56.0 1.9 %collective-permute-start.10 = (bf16[16,4096]{1,0:T(8,128)(2,1)S(1)}, bf16[16,4096]{1,0:T(8,128)(2,1)S(1)}, u32[]{:S(2)}, u32[]{:S(2)}) collective-permute-start(bf16[16,4096]{1,0:T(8,128)(2,1)S(1)} %get-tuple-element.22), channel_id=1, source_target_pairs={{0,2},{1,3},{2,0},{3,1},{4,6},{5,7},{6,4},{7,5},{8,10},{9,11},{10,... | collective-permute-start | bytes 393224 | tf_op jit(solution)/shard_map/ppermute | solution.py:228
  57.9 4.3 %collective-permute-done.11 = bf16[16,4096]{1,0:T(8,128)(2,1)S(1)} collective-permute-done((bf16[16,4096]{1,0:T(8,128)(2,1)S(1)}, bf16[16,4096]{1,0:T(8,128)(2,1)S(1)}, u32[]{:S(2)}, u32[]{:S(2)}) %collective-permute-start.11) | collective-permute-done | bytes 131104 | tf_op jit(solution)/shard_map/ppermute | solution.py:228
  62.2 2.0 %collective-permute-done.10 = bf16[16,4096]{1,0:T(8,128)(2,1)S(1)} collective-permute-done((bf16[16,4096]{1,0:T(8,128)(2,1)S(1)}, bf16[16,4096]{1,0:T(8,128)(2,1)S(1)}, u32[]{:S(2)}, u32[]{:S(2)}) %collective-permute-start.10) | collective-permute-done | bytes 131104 | tf_op jit(solution)/shard_map/ppermute | solution.py:228
  64.3 0.2 collective-permute-start.14
  64.5 1.0 %collective-permute-start.12 = (bf16[8,4096]{1,0:T(8,128)(2,1)S(1)}, bf16[8,4096]{1,0:T(8,128)(2,1)S(1)}, u32[]{:S(2)}, u32[]{:S(2)}) collective-permute-start(bf16[8,4096]{1,0:T(8,128)(2,1)S(1)} %get-tuple-element.23), channel_id=1, source_target_pairs={{0,8},{1,9},{2,10},{3,11},{4,12},{5,13},{6,14},{7,15},{8,0},{9,1},... | collective-permute-start | bytes 196616 | tf_op jit(solution)/shard_map/ppermute | solution.py:228
  65.5 3.3 %collective-permute-start.13 = (bf16[8,4096]{1,0:T(8,128)(2,1)S(1)}, bf16[8,4096]{1,0:T(8,128)(2,1)S(1)}, u32[]{:S(2)}, u32[]{:S(2)}) collective-permute-start(bf16[8,4096]{1,0:T(8,128)(2,1)S(1)} %get-tuple-element.24), channel_id=1, source_target_pairs={{0,12},{1,13},{2,14},{3,15},{4,8},{5,9},{6,10},{7,11},{8,4},{9,5},... | collective-permute-start | bytes 196616 | tf_op jit(solution)/shard_map/ppermute | solution.py:228
  68.7 0.5 slice_bitcast_fusion
  69.3 4.9 %shard_map.87 = bf16[4096,512]{1,0:T(8,128)(2,1)} custom-call(bf16[32,8192]{1,0:T(8,128)(2,1)S(1)} %pad_maximum_fusion.refs_0_.refs_4_, bf16[32,8192]{1,0:T(8,128)(2,1)S(1)} %constant_dynamic-update-slice_fusion.2.refs_1_.refs_5_, bf16[32,8192]{1,0:T(8,128)(2,1)S(1)} %collective-permute-done.7.refs_2_.refs_6_, ...), custom_call_target="tpu_custom_call" | custom-call | flops 536870912 | bytes 5242880 | tf_op jit(solution)/shard_map/pallas_call | solution.py:213
  74.1 0.7 fusion.2
  (28 shorter events, 0.4 us)
Async XLA Ops:
  2.3 10.4 %collective-permute-start.3 = (bf16[8,8192]{1,0:T(8,128)(2,1)S(1)}, bf16[8,8192]{1,0:T(8,128)(2,1)S(1)}, u32[]{:S(2)}, u32[]{:S(2)}) collective-permute-start(bf16[8,8192]{1,0:T(8,128)(2,1)S(1)} %constant_dynamic-update-slice_fusion), channel_id=1, source_target_pairs={{0,8},{1,9},{2,10},{3,11},{4,12},{5,13},{6,14},{7,15},{8,0},{9,1},... | collective-permute-start | bytes 393224 | tf_op jit(solution)/shard_map/ppermute | solution.py:228
  6.4 8.6 %collective-permute-start = (bf16[8,8192]{1,0:T(8,128)(2,1)S(1)}, bf16[8,8192]{1,0:T(8,128)(2,1)S(1)}, u32[]{:S(2)}, u32[]{:S(2)}) collective-permute-start(bf16[8,8192]{1,0:T(8,128)(2,1)S(1)} %constant_dynamic-update-slice_fusion), channel_id=1, source_target_pairs={{0,4},{1,5},{2,6},{3,7},{4,0},{5,1},{6,2},{7,3},{8,12},{9,13},{10,... | collective-permute-start | bytes 393224 | tf_op jit(solution)/shard_map/ppermute | solution.py:228
  7.9 7.5 %collective-permute-start.1 = (bf16[8,8192]{1,0:T(8,128)(2,1)S(1)}, bf16[8,8192]{1,0:T(8,128)(2,1)S(1)}, u32[]{:S(2)}, u32[]{:S(2)}) collective-permute-start(bf16[8,8192]{1,0:T(8,128)(2,1)S(1)} %constant_dynamic-update-slice_fusion), channel_id=1, source_target_pairs={{0,2},{1,3},{2,0},{3,1},{4,6},{5,7},{6,4},{7,5},{8,10},{9,11},{10,... | collective-permute-start | bytes 393224 | tf_op jit(solution)/shard_map/ppermute | solution.py:228
  12.8 9.1 %collective-permute-start.5 = (bf16[8,8192]{1,0:T(8,128)(2,1)S(1)}, bf16[8,8192]{1,0:T(8,128)(2,1)S(1)}, u32[]{:S(2)}, u32[]{:S(2)}) collective-permute-start(bf16[8,8192]{1,0:T(8,128)(2,1)S(1)} %collective-permute-done.3), channel_id=1, source_target_pairs={{0,2},{1,3},{2,0},{3,1},{4,6},{5,7},{6,4},{7,5},{8,10},{9,11},{10,... | collective-permute-start | bytes 393224 | tf_op jit(solution)/shard_map/ppermute | solution.py:228
  14.3 6.3 %collective-permute-start.4 = (bf16[8,8192]{1,0:T(8,128)(2,1)S(1)}, bf16[8,8192]{1,0:T(8,128)(2,1)S(1)}, u32[]{:S(2)}, u32[]{:S(2)}) collective-permute-start(bf16[8,8192]{1,0:T(8,128)(2,1)S(1)} %collective-permute-done.3), channel_id=1, source_target_pairs={{0,4},{1,5},{2,6},{3,7},{4,0},{5,1},{6,2},{7,3},{8,12},{9,13},{10,... | collective-permute-start | bytes 393224 | tf_op jit(solution)/shard_map/ppermute | solution.py:228
  14.9 5.6 %collective-permute-start.2 = (bf16[8,8192]{1,0:T(8,128)(2,1)S(1)}, bf16[8,8192]{1,0:T(8,128)(2,1)S(1)}, u32[]{:S(2)}, u32[]{:S(2)}) collective-permute-start(bf16[8,8192]{1,0:T(8,128)(2,1)S(1)} %collective-permute-done), channel_id=1, source_target_pairs={{0,2},{1,3},{2,0},{3,1},{4,6},{5,7},{6,4},{7,5},{8,10},{9,11},{10,... | collective-permute-start | bytes 393224 | tf_op jit(solution)/shard_map/ppermute | solution.py:228
  20.6 6.1 %collective-permute-start.7 = (bf16[32,8192]{1,0:T(8,128)(2,1)S(1)}, bf16[32,8192]{1,0:T(8,128)(2,1)S(1)}, u32[]{:S(2)}, u32[]{:S(2)}) collective-permute-start(bf16[32,8192]{1,0:T(8,128)(2,1)S(1)} %pad_maximum_fusion.refs_0_.refs_4_), channel_id=1, source_target_pairs={{0,1},{1,0},{2,3},{3,2},{4,5},{5,4},{6,7},{7,6},{8,9},{9,8},{10,11... | collective-permute-start | bytes 1572872 | tf_op jit(solution)/shard_map/ppermute | solution.py:228
  20.7 5.9 %collective-permute-start.6 = (bf16[8,8192]{1,0:T(8,128)(2,1)S(1)}, bf16[8,8192]{1,0:T(8,128)(2,1)S(1)}, u32[]{:S(2)}, u32[]{:S(2)}) collective-permute-start(bf16[8,8192]{1,0:T(8,128)(2,1)S(1)} %collective-permute-done.4), channel_id=1, source_target_pairs={{0,2},{1,3},{2,0},{3,1},{4,6},{5,7},{6,4},{7,5},{8,10},{9,11},{10,... | collective-permute-start | bytes 393224 | tf_op jit(solution)/shard_map/ppermute | solution.py:228
  26.6 2.0 %collective-permute-start.8 = (bf16[32,8192]{1,0:T(8,128)(2,1)S(1)}, bf16[32,8192]{1,0:T(8,128)(2,1)S(1)}, u32[]{:S(2)}, u32[]{:S(2)}) collective-permute-start(bf16[32,8192]{1,0:T(8,128)(2,1)S(1)} %constant_dynamic-update-slice_fusion.2.refs_1_.refs_5_), channel_id=1, source_target_pairs={{0,1},{1,0},{2,3},{3,2},{4,5},{5,4},{6,7},{7,6},{8,9},{9,8},{10,11... | collective-permute-start | bytes 1572872 | tf_op jit(solution)/shard_map/ppermute | solution.py:228
  28.6 2.2 %copy-start = (bf16[4096,512]{1,0:T(8,128)(2,1)S(1)}, bf16[4096,512]{1,0:T(8,128)(2,1)}, u32[]{:S(2)}) copy-start(bf16[4096,512]{1,0:T(8,128)(2,1)} %refs_5_.1) | copy-start | bytes 12582916
  30.8 2.2 %copy-start.2 = (bf16[4096,512]{1,0:T(8,128)(2,1)S(1)}, bf16[4096,512]{1,0:T(8,128)(2,1)}, u32[]{:S(2)}) copy-start(bf16[4096,512]{1,0:T(8,128)(2,1)} %refs_8_.1) | copy-start | bytes 12582916
  32.9 0.7 copy-start.3
  33.6 0.7 copy-start.5
  34.3 16.5 %copy-start.1 = (bf16[4096,512]{1,0:T(8,128)(2,1)S(1)}, bf16[4096,512]{1,0:T(8,128)(2,1)}, u32[]{:S(2)}) copy-start(bf16[4096,512]{1,0:T(8,128)(2,1)} %refs_5_.1) | copy-start | bytes 12582916
  34.3 16.5 %copy-start.4 = (s32[128]{0:T(128)S(1)}, s32[128]{0:T(128)}, u32[]{:S(2)}) copy-start(s32[128]{0:T(128)} %param.10) | copy-start | bytes 1540
  53.6 2.0 %collective-permute-start.9 = (bf16[64,4096]{1,0:T(8,128)(2,1)S(1)}, bf16[64,4096]{1,0:T(8,128)(2,1)S(1)}, u32[]{:S(2)}, u32[]{:S(2)}) collective-permute-start(bf16[64,4096]{1,0:T(8,128)(2,1)S(1)} %get-tuple-element.15), channel_id=1, source_target_pairs={{0,1},{1,0},{2,3},{3,2},{4,5},{5,4},{6,7},{7,6},{8,9},{9,8},{10,11... | collective-permute-start | bytes 1572872 | tf_op jit(solution)/shard_map/ppermute | solution.py:228
  55.8 6.4 %collective-permute-start.11 = (bf16[16,4096]{1,0:T(8,128)(2,1)S(1)}, bf16[16,4096]{1,0:T(8,128)(2,1)S(1)}, u32[]{:S(2)}, u32[]{:S(2)}) collective-permute-start(bf16[16,4096]{1,0:T(8,128)(2,1)S(1)} %get-tuple-element.21), channel_id=1, source_target_pairs={{0,2},{1,3},{2,0},{3,1},{4,6},{5,7},{6,4},{7,5},{8,10},{9,11},{10,... | collective-permute-start | bytes 393224 | tf_op jit(solution)/shard_map/ppermute | solution.py:228
  56.0 8.2 %collective-permute-start.10 = (bf16[16,4096]{1,0:T(8,128)(2,1)S(1)}, bf16[16,4096]{1,0:T(8,128)(2,1)S(1)}, u32[]{:S(2)}, u32[]{:S(2)}) collective-permute-start(bf16[16,4096]{1,0:T(8,128)(2,1)S(1)} %get-tuple-element.22), channel_id=1, source_target_pairs={{0,2},{1,3},{2,0},{3,1},{4,6},{5,7},{6,4},{7,5},{8,10},{9,11},{10,... | collective-permute-start | bytes 393224 | tf_op jit(solution)/shard_map/ppermute | solution.py:228
  64.3 9.8 %collective-permute-start.14 = (bf16[8,4096]{1,0:T(8,128)(2,1)S(1)}, bf16[8,4096]{1,0:T(8,128)(2,1)S(1)}, u32[]{:S(2)}, u32[]{:S(2)}) collective-permute-start(bf16[8,4096]{1,0:T(8,128)(2,1)S(1)} %slice.58), channel_id=1, source_target_pairs={{0,4},{1,5},{2,6},{3,7},{4,0},{5,1},{6,2},{7,3},{8,12},{9,13},{10,... | collective-permute-start | bytes 196616 | tf_op jit(solution)/shard_map/ppermute | solution.py:228
  64.5 9.6 %collective-permute-start.12 = (bf16[8,4096]{1,0:T(8,128)(2,1)S(1)}, bf16[8,4096]{1,0:T(8,128)(2,1)S(1)}, u32[]{:S(2)}, u32[]{:S(2)}) collective-permute-start(bf16[8,4096]{1,0:T(8,128)(2,1)S(1)} %get-tuple-element.23), channel_id=1, source_target_pairs={{0,8},{1,9},{2,10},{3,11},{4,12},{5,13},{6,14},{7,15},{8,0},{9,1},... | collective-permute-start | bytes 196616 | tf_op jit(solution)/shard_map/ppermute | solution.py:228
  65.5 8.7 %collective-permute-start.13 = (bf16[8,4096]{1,0:T(8,128)(2,1)S(1)}, bf16[8,4096]{1,0:T(8,128)(2,1)S(1)}, u32[]{:S(2)}, u32[]{:S(2)}) collective-permute-start(bf16[8,4096]{1,0:T(8,128)(2,1)S(1)} %get-tuple-element.24), channel_id=1, source_target_pairs={{0,12},{1,13},{2,14},{3,15},{4,8},{5,9},{6,10},{7,11},{8,4},{9,5},... | collective-permute-start | bytes 196616 | tf_op jit(solution)/shard_map/ppermute | solution.py:228

commit v2 on v1

v2 whole, which is shorter than its diff:
```python
import functools

import jax
import jax.numpy as jnp
from jax import lax
from jax.experimental import pallas as pl
from jax.experimental.pallas import tpu as pltpu
from jax.sharding import PartitionSpec as P

CE_WEIGHT = 0.5
STATS = 8


def xor_order(n):
    return (0, 4, 2, 6, 8, 12, 10, 14, 1, 5, 3, 7, 9, 13, 11, 15) if n == 16 else None


def held_rows(shape, dim, me, rows_local, tuned):
    held = lax.broadcasted_iota(jnp.int32, shape, dim)
    if not tuned:
        return held
    step = rows_local.bit_length() - 1
    block = lax.shift_right_logical(held, step)
    bit = lambda k: lax.shift_right_logical(block, k) & 1
    distance = bit(3) + bit(2) * 8 + bit(1) * 2 + bit(0) * 4
    return (me ^ distance) * rows_local + (held & (rows_local - 1))


def to_column(is_row, row):
    return jnp.sum(jnp.where(is_row, row, 0.0), axis=1, keepdims=True)


def prepare_kernel(
    rows_local, tuned, me_ref, order_ref, labels_ref, teacher_ref, student_ref, teacher_out, student_out, pick_out, label_out, sems
):
    copies = []
    pieces = sems.shape[1]
    rows = teacher_ref.shape[0] // pieces
    for k in range(pieces):
        for j, (source, target) in enumerate(((teacher_ref, teacher_out), (student_ref, student_out))):
            part = pl.ds(k * rows, rows)
            copies.append(pltpu.make_async_copy(source.at[part], target.at[part], sems.at[j, k]))
    for copy in copies:
        copy.start()
    me = me_ref[0]
    count = order_ref.shape[1]
    vocab = teacher_ref.shape[1]
    lanes = lax.broadcasted_iota(jnp.int32, (count, count), 1)
    is_row = held_rows((count, count), 0, me, rows_local, tuned) == lanes
    wanted = to_column(is_row, order_ref[...].astype(jnp.float32))
    have = held_rows((count, count), 1, me, rows_local, tuned).astype(jnp.float32)
    pick_out[...] = jnp.where(wanted == have, 1.0, 0.0).astype(jnp.bfloat16)
    label = to_column(is_row, labels_ref[...].astype(jnp.float32)) - (me * vocab).astype(jnp.float32)
    label_out[...] = jnp.broadcast_to(label, label_out.shape)
    for copy in copies:
        copy.wait()


def prepare(me, order, labels, heads, rows_local, tuned):
    count = order.shape[0]
    vmem = pl.BlockSpec(memory_space=pltpu.VMEM)
    hbm = pl.BlockSpec(memory_space=pltpu.HBM)
    return pl.pallas_call(
        functools.partial(prepare_kernel, rows_local, tuned),
        in_specs=[pl.BlockSpec(memory_space=pltpu.SMEM), vmem, vmem, hbm, hbm],
        out_specs=(vmem,) * 4,
        out_shape=(
            jax.ShapeDtypeStruct(heads[0].shape, heads[0].dtype),
            jax.ShapeDtypeStruct(heads[1].shape, heads[1].dtype),
            jax.ShapeDtypeStruct((count, count), jnp.bfloat16),
            jax.ShapeDtypeStruct((count, 128), jnp.float32),
        ),
        scratch_shapes=[pltpu.SemaphoreType.DMA((2, 4))],
        compiler_params=pltpu.CompilerParams(vmem_limit_bytes=24 * 2**20),
        cost_estimate=pl.CostEstimate(flops=0, bytes_accessed=2 * heads[0].size * 4, transcendentals=0),
    )(me, order[None], labels[None], *(pltpu.with_memory_space_constraint(head, pltpu.HBM) for head in heads))


def logits_kernel(rows_local, tuned, parts, me_ref, pick_ref, label_ref, *refs):
    pieces = refs[:parts]
    teacher_head, student_head, teacher_out, student_out, stats_out = refs[parts:]
    depth, vocab = student_head.shape

    def product(first, head):
        rows = jnp.concatenate([piece[:, first : first + depth] for piece in pieces], axis=0)
        return jnp.dot(rows, head[...], preferred_element_type=jnp.float32)

    me = me_ref[0]
    raw = product(0, teacher_head)
    student = product(depth, student_head)
    count = student.shape[0]
    high = raw.astype(jnp.bfloat16)
    rest = raw - high.astype(jnp.float32)
    middle = rest.astype(jnp.bfloat16)
    low = (rest - middle.astype(jnp.float32)).astype(jnp.bfloat16)
    pick = pick_ref[...]
    teacher = sum(jnp.dot(pick, piece, preferred_element_type=jnp.float32) for piece in (high, middle, low))
    teacher_out[...] = teacher
    student_out[...] = student
    is_label = label_ref[:, 0:1].astype(jnp.int32) == lax.broadcasted_iota(jnp.int32, (count, vocab), 1)
    teacher_max = jnp.max(teacher, axis=1, keepdims=True)
    student_max = jnp.max(student, axis=1, keepdims=True)
    teacher_exp = jnp.exp(teacher - teacher_max)
    values = (
        teacher_max,
        student_max,
        jnp.sum(teacher_exp, axis=1, keepdims=True),
        jnp.sum(jnp.exp(student - student_max), axis=1, keepdims=True),
        jnp.sum(teacher_exp * (teacher - student), axis=1, keepdims=True),
        jnp.sum(jnp.where(is_label, student, 0.0), axis=1, keepdims=True),
    )
    lanes = lax.broadcasted_iota(jnp.int32, (count, count), 1)
    is_row = held_rows((count, count), 0, me, rows_local, tuned) == lanes
    block = [jnp.sum(jnp.where(is_row, value, 0.0), axis=0, keepdims=True) for value in values]
    block.append(jnp.zeros((STATS - len(block), count), jnp.float32))
    stats_out[...] = jnp.broadcast_to(jnp.concatenate(block, axis=0)[None], stats_out.shape)


def logits(me, pick, label, hidden, heads, n, rows_local, tuned):
    count = pick.shape[0]
    depth, vocab = heads[0].shape
    vmem = pl.BlockSpec(memory_space=pltpu.VMEM)
    return pl.pallas_call(
        functools.partial(logits_kernel, rows_local, tuned, len(hidden)),
        in_specs=[pl.BlockSpec(memory_space=pltpu.SMEM)] + [vmem] * (4 + len(hidden)),
        out_specs=(vmem,) * 3,
        out_shape=(
            jax.ShapeDtypeStruct((count, vocab), jnp.float32),
            jax.ShapeDtypeStruct((count, vocab), jnp.float32),
            jax.ShapeDtypeStruct((n, STATS, count), jnp.float32),
        ),
        compiler_params=pltpu.CompilerParams(vmem_limit_bytes=40 * 2**20),
        cost_estimate=pl.CostEstimate(
            flops=4 * count * depth * vocab, bytes_accessed=4 * depth * (vocab + count), transcendentals=2 * count * vocab
        ),
    )(me, pick, label, *hidden, *heads)


def grad_kernel(
    rows_local, tuned, me_ref, label_ref, stats_ref, teacher_ref, student_ref, head_ref, keep_out, send_out, grad_out, loss_out
):
    me = me_ref[0]
    count, vocab = student_ref.shape
    devices = stats_ref.shape[0]
    top = stats_ref[0, 0:2]
    for d in range(1, devices):
        top = jnp.maximum(top, stats_ref[d, 0:2])
    totals = jnp.zeros((2, count), jnp.float32)
    cross = jnp.zeros((1, count), jnp.float32)
    label_logit = jnp.zeros((1, count), jnp.float32)
    for d in range(devices):
        weight = jnp.exp(stats_ref[d, 0:2] - top)
        totals += weight * stats_ref[d, 2:4]
        cross += weight[0:1] * stats_ref[d, 4:5]
        label_logit += stats_ref[d, 5:6]
    norms = top + jnp.log(totals)
    teacher_norm, student_norm = norms[0:1], norms[1:2]
    loss = cross / totals[0:1] - teacher_norm + student_norm + CE_WEIGHT * (student_norm - label_logit)
    lanes = lax.broadcasted_iota(jnp.int32, (count, count), 1)
    is_row = held_rows((count, count), 0, me, rows_local, tuned) == lanes
    mine = lax.broadcasted_iota(jnp.int32, (count, count), 0) + me * rows_local == lanes
    by_lane = lax.broadcasted_iota(jnp.int32, (count, count), 0) == lanes
    loss_out[...] = jnp.sum(jnp.where(by_lane, to_column(mine, loss), 0.0), axis=0, keepdims=True)
    is_label = label_ref[:, 0:1].astype(jnp.int32) == lax.broadcasted_iota(jnp.int32, (count, vocab), 1)
    grad = (
        (1.0 + CE_WEIGHT) * jnp.exp(student_ref[...] - to_column(is_row, student_norm))
        - jnp.exp(teacher_ref[...] - to_column(is_row, teacher_norm))
        - jnp.where(is_label, CE_WEIGHT, 0.0)
    ).astype(jnp.bfloat16)
    grad_out[...] = grad
    kept = keep_out.shape[0]
    depth = head_ref.shape[0]
    step = min(512, depth)
    for k in range(0, depth, step):
        part = lax.dot_general(
            grad, head_ref[k : k + step], (((1,), (1,)), ((), ())), preferred_element_type=jnp.float32
        )
        keep_out[:, k : k + step] = part[:kept]
        if send_out is not None:
            send_out[:, k : k + step] = part[kept:].astype(jnp.bfloat16)


def gradient(me, label, stats, teacher_logits, student_logits, head, rows_local, tuned):
    count, vocab = student_logits.shape
    depth = head.shape[0]
    kept = count // 2 if tuned else count
    vmem = pl.BlockSpec(memory_space=pltpu.VMEM)
    shapes = [jax.ShapeDtypeStruct((kept, depth), jnp.float32)]
    if tuned:
        shapes.append(jax.ShapeDtypeStruct((count - kept, depth), jnp.bfloat16))
    shapes += [jax.ShapeDtypeStruct((count, vocab), jnp.bfloat16), jax.ShapeDtypeStruct((1, count), jnp.float32)]

    def kernel(*refs):
        if tuned:
            grad_kernel(rows_local, tuned, *refs)
        else:
            grad_kernel(rows_local, tuned, *refs[:7], None, *refs[7:])

    return pl.pallas_call(
        kernel,
        in_specs=[pl.BlockSpec(memory_space=pltpu.SMEM)] + [vmem] * 5,
        out_specs=(vmem,) * len(shapes),
        out_shape=tuple(shapes),
        compiler_params=pltpu.CompilerParams(vmem_limit_bytes=40 * 2**20),
        cost_estimate=pl.CostEstimate(
            flops=2 * count * depth * vocab, bytes_accessed=2 * depth * (vocab + 2 * count), transcendentals=2 * count * vocab
        ),
    )(me, label, stats, teacher_logits, student_logits, head)


def head_kernel(parts, *refs):
    rows = jnp.concatenate([piece[...] for piece in refs[:parts]], axis=0)
    grad_ref, out_ref = refs[parts:]
    out_ref[...] = lax.dot_general(
        rows, grad_ref[...], (((0,), (0,)), ((), ())), preferred_element_type=jnp.float32
    ).astype(jnp.bfloat16)


def head_gradient(hidden, logit_grad, depth):
    count, vocab = logit_grad.shape
    step = min(512, depth)
    first = depth // step
    return pl.pallas_call(
        functools.partial(head_kernel, len(hidden)),
        grid=(depth // step,),
        in_specs=[pl.BlockSpec((piece.shape[0], step), lambda k: (0, k + first)) for piece in hidden]
        + [pl.BlockSpec((count, vocab), lambda k: (0, 0))],
        out_specs=pl.BlockSpec((step, vocab), lambda k: (k, 0)),
        out_shape=jax.ShapeDtypeStruct((depth, vocab), jnp.bfloat16),
        compiler_params=pltpu.CompilerParams(vmem_limit_bytes=40 * 2**20),
        cost_estimate=pl.CostEstimate(
            flops=2 * count * depth * vocab, bytes_accessed=2 * depth * (vocab + count), transcendentals=0
        ),
    )(*hidden, logit_grad)


def swap(value, distance, n):
    return lax.ppermute(value, "dp", [(i, i ^ distance) for i in range(n)])


def after(value, *done):
    return lax.optimization_barrier((value, *done))[0]


def gather_rows(teacher_rows, student_rows, n, prepared):
    far = jnp.concatenate([after(swap(teacher_rows, 8, n), *prepared), swap(student_rows, 8, n)], axis=1)
    rows = jnp.concatenate([teacher_rows, student_rows], axis=1)
    side = swap(rows, 2, n)
    near = swap(rows, 4, n)
    far_near = swap(far, 4, n)
    near_side = swap(near, 2, n)
    far_side = swap(far, 2, n)
    far_near_side = swap(far_near, 2, n)
    first = jnp.concatenate([rows, near, side, near_side], axis=0)
    second = jnp.concatenate([far, far_near, far_side, far_near_side], axis=0)
    return [first, second, swap(first, 1, n), swap(second, 1, n)]


def scatter_rows(keep, send, rows_local, n, grad_head):
    low = jnp.bfloat16
    full = jnp.float32
    held = keep + swap(send, 1, n).astype(full)
    quarter = 2 * rows_local
    near_keep, near_send, far_keep, far_send = (held[k * quarter : (k + 1) * quarter] for k in range(4))
    far_part = after(swap(far_send.astype(low), 2, n), grad_head)
    far = (far_keep + far_part.astype(full)).astype(low)
    near = near_keep + swap(near_send.astype(low), 2, n).astype(full)
    from_far = swap(far[:rows_local], 8, n)
    from_far_near = swap(far[rows_local:], 12, n)
    from_near = swap(near[rows_local:].astype(low), 4, n)
    return near[:rows_local] + from_far.astype(full) + from_far_near.astype(full) + from_near.astype(full)


def per_device(n, teacher_hidden, student_hidden, teacher_head, student_head, labels, order):
    rows_local, depth = student_hidden.shape
    tuned = xor_order(n) is not None and rows_local == 8
    me = lax.axis_index("dp").astype(jnp.int32).reshape(1)
    *heads, pick, label = prepare(me, order, labels, (teacher_head, student_head), rows_local, tuned)
    if tuned:
        hidden = gather_rows(teacher_hidden, student_hidden, n, (*heads, pick, label))
    else:
        rows = jnp.concatenate([teacher_hidden, student_hidden], axis=1)
        hidden = [lax.all_gather(rows, "dp", axis=0, tiled=True)]
    teacher_logits, student_logits, stats = logits(me, pick, label, hidden, heads, n, rows_local, tuned)
    stats = lax.all_to_all(stats, "dp", 0, 0)
    outs = gradient(me, label, stats, teacher_logits, student_logits, heads[1], rows_local, tuned)
    logit_grad, loss = outs[-2:]
    grad_head = head_gradient(hidden, logit_grad, depth)
    if tuned:
        grad_hidden = scatter_rows(outs[0], outs[1], rows_local, n, grad_head)
    else:
        grad_hidden = lax.psum_scatter(outs[0], "dp", scatter_dimension=0, tiled=True)
    return (loss[0, :rows_local], grad_hidden, grad_head)


def solution(mesh):
    in_specs = (
        P(("groups", "dp"), None),
        P(("groups", "dp"), None),
        P(None, "dp"),
        P(None, "dp"),
        P("groups"),
        P("groups"),
    )
    out_specs = (P(("groups", "dp")), P(("groups", "dp"), None), P("groups", "dp"))
    return jax.shard_map(
        functools.partial(per_device, mesh.shape["dp"]),
        mesh=mesh,
        in_specs=in_specs,
        out_specs=out_specs,
        check_vma=False,
    )
```

time: 75.2 us -> 63.8 us (0.85)
  waiting for transfers between devices: 23.2 us -> 15.5 us
  local copies, waits for them, and re-layouts: 7.97 us -> 3.56 us
    ppermute x15 -> x16, waiting for transfers between devices: 23.2 us -> 15.5 us  [swap(): return lax.ppermute(value, 'dp', [(i, i ^ distance) for i in range(n)])]
    unnamed x16 -> x6, local copies, waits for them, and re-layouts: 6.57 us -> 2.16 us
    pallas_call x1 -> x2, Pallas kernels: 2.86 us -> 5.05 us  [the longest x1 3.47 us: prepare(): pl.pallas_call(functools.partial(prepare_kernel, rows_local, tuned), in_s...]
    pallas_call x1, Pallas kernels: 3.57 us -> 1.6 us  [logits(): pl.pallas_call(functools.partial(logits_kernel, rows_local, tuned, len(hi...]
    ppermute x15 -> x16, starting transfers between devices: 17.7 us -> 18.3 us  [swap(): return lax.ppermute(value, 'dp', [(i, i ^ distance) for i in range(n)])]
  transfers between devices with their start and end apart: 15 -> 16, of which waited for: 7 -> 9; matrix products, arithmetic and copies ran while one was open for 1% -> 4% of each run, Pallas kernels for 7% -> 13%
where the time goes in v2:
time: 63.8 us; the launch traced here: 63.5 us
  starting transfers between devices  18.3 us (29%)
  waiting for transfers between devices  15.5 us (24%)
  blocking collectives  12.8 us (20%)
  Pallas kernels  11.5 us (18%)
  local copies, waits for them, and re-layouts  3.56 us (6%)
  other arithmetic  0.96 us (2%)
  between operations  0.77 us (1%)
    ppermute x16, starting transfers between devices, swap(): return lax.ppermute(value, 'dp', [(i, i ^ distance) for i in range(n)])  18.3 us
    ppermute x16, waiting for transfers between devices, swap(): return lax.ppermute(value, 'dp', [(i, i ^ distance) for i in range(n)])  15.5 us
    all_to_all x1, blocking collectives, per_device(): stats = lax.all_to_all(stats, 'dp', 0, 0)  12.8 us
    pallas_call x1, Pallas kernels, head_gradient(): pl.pallas_call(functools.partial(head_kernel, len(hidden)), grid=(depth /...  4.87 us
    pallas_call x1, Pallas kernels, prepare(): pl.pallas_call(functools.partial(prepare_kernel, rows_local, tuned), in_s...  3.47 us
    unnamed x6, local copies, waits for them, and re-layouts  2.16 us
    pallas_call x1, Pallas kernels, logits(): pl.pallas_call(functools.partial(logits_kernel, rows_local, tuned, len(hi...  1.6 us
    pallas_call x1, Pallas kernels, gradient(): pl.pallas_call(kernel, in_specs=[pl.BlockSpec(memory_space=pltpu.SMEM)] +...  1.58 us
  transfers between devices with their start and end apart: 16, of which 9 were waited for; matrix products, arithmetic and copies ran while one was open for 4% of the time, Pallas kernels for 13%

profile of v2, /device:TPU:0, one launch (start us, length us, event | category | flops | bytes accessed | tf_op | source)
XLA Modules:
  0.0 63.5 jit_solution(13815805508981085598)
XLA Ops:
  0.6 4.1 %collective-permute-start.3 = (bf16[8,4096]{1,0:T(8,128)(2,1)}, bf16[8,4096]{1,0:T(8,128)(2,1)S(1)}, u32[]{:S(2)}, u32[]{:S(2)}) collective-permute-start(bf16[8,4096]{1,0:T(8,128)(2,1)} %param.6), channel_id=1, source_target_pairs={{0,8},{1,9},{2,10},{3,11},{4,12},{5,13},{6,14},{7,15},{8,0},{9,1},... | collective-permute-start | bytes 196616 | tf_op jit(solution)/shard_map/ppermute | solution.py:238
  4.8 0.8 %constant_dynamic-update-slice_fusion.1 = bf16[8,8192]{1,0:T(8,128)(2,1)S(1)} fusion(bf16[8,4096]{1,0:T(8,128)(2,1)} %param.6), kind=kLoop, calls=%fused_computation.11 | loop fusion | bytes 131072
  5.7 0.8 %constant_dynamic-update-slice_fusion = bf16[8,8192]{1,0:T(8,128)(2,1)S(1)} fusion(bf16[8,8192]{1,0:T(8,128)(2,1)S(1)} %constant_dynamic-update-slice_fusion.1, bf16[8,4096]{1,0:T(8,128)(2,1)} %param.7), kind=kLoop, calls=%fused_computation.10 | loop fusion | bytes 131072 | tf_op jit(solution)/shard_map/concatenate | solution.py:247
  6.5 1.8 %collective-permute-start = (bf16[8,8192]{1,0:T(8,128)(2,1)S(1)}, bf16[8,8192]{1,0:T(8,128)(2,1)S(1)}, u32[]{:S(2)}, u32[]{:S(2)}) collective-permute-start(bf16[8,8192]{1,0:T(8,128)(2,1)S(1)} %constant_dynamic-update-slice_fusion), channel_id=1, source_target_pairs={{0,4},{1,5},{2,6},{3,7},{4,0},{5,1},{6,2},{7,3},{8,12},{9,13},{10,... | collective-permute-start | bytes 393224 | tf_op jit(solution)/shard_map/ppermute | solution.py:238
  8.3 0.7 %copy-done = s32[128]{0:T(128)S(1)} copy-done((s32[128]{0:T(128)S(1)}, s32[128]{0:T(128)}, u32[]{:S(2)}) %copy-start) | copy-done | bytes 536
  9.0 0.7 %copy-done.1 = s32[128]{0:T(128)S(1)} copy-done((s32[128]{0:T(128)S(1)}, s32[128]{0:T(128)}, u32[]{:S(2)}) %copy-start.1) | copy-done | bytes 536
  9.6 3.5 %shard_map.85 = (bf16[4096,512]{1,0:T(8,128)(2,1)S(1)}, bf16[4096,512]{1,0:T(8,128)(2,1)S(1)}, bf16[128,128]{1,0:T(8,128)(2,1)S(1)}, f32[128,128]{1,0:T(8,128)S(1)}) custom-call(s32[1]{0:T(128)} %bitcast.me_ref.refs_0_, s32[1,128]{1,0:T(1,128)S(1)} %bitcast.5, s32[1,128]{1,0:T(1,128)S(1)} %bitcast.6, bf16[4096,512]{1,0:T(8,128)(2,1)} %teacher_ref.1, ...), custom_call_target="tpu_custom_call" | custom-call | bytes 16777216 | tf_op jit(solution)/shard_map/pallas_call | solution.py:63
  13.2 0.3 collective-permute-start.5
  13.4 1.8 %collective-permute-start.1 = (bf16[8,8192]{1,0:T(8,128)(2,1)S(1)}, bf16[8,8192]{1,0:T(8,128)(2,1)S(1)}, u32[]{:S(2)}, u32[]{:S(2)}) collective-permute-start(bf16[8,8192]{1,0:T(8,128)(2,1)S(1)} %constant_dynamic-update-slice_fusion), channel_id=1, source_target_pairs={{0,2},{1,3},{2,0},{3,1},{4,6},{5,7},{6,4},{7,5},{8,10},{9,11},{10,... | collective-permute-start | bytes 393224 | tf_op jit(solution)/shard_map/ppermute | solution.py:238
  15.2 0.2 collective-permute-start.2
  15.5 1.8 %collective-permute-start.6 = (bf16[8,8192]{1,0:T(8,128)(2,1)S(1)}, bf16[8,8192]{1,0:T(8,128)(2,1)S(1)}, u32[]{:S(2)}, u32[]{:S(2)}) collective-permute-start(bf16[8,8192]{1,0:T(8,128)(2,1)S(1)} %constant_dynamic-update-slice_fusion.2), channel_id=1, source_target_pairs={{0,2},{1,3},{2,0},{3,1},{4,6},{5,7},{6,4},{7,5},{8,10},{9,11},{10,... | collective-permute-start | bytes 393224 | tf_op jit(solution)/shard_map/ppermute | solution.py:238
  17.2 1.0 %collective-permute-done.5 = bf16[8,8192]{1,0:T(8,128)(2,1)S(1)} collective-permute-done((bf16[8,8192]{1,0:T(8,128)(2,1)S(1)}, bf16[8,8192]{1,0:T(8,128)(2,1)S(1)}, u32[]{:S(2)}, u32[]{:S(2)}) %collective-permute-start.5) | collective-permute-done | bytes 131104 | tf_op jit(solution)/shard_map/ppermute | solution.py:238
  18.2 1.5 %collective-permute-start.7 = (bf16[8,8192]{1,0:T(8,128)(2,1)S(1)}, bf16[8,8192]{1,0:T(8,128)(2,1)S(1)}, u32[]{:S(2)}, u32[]{:S(2)}) collective-permute-start(bf16[8,8192]{1,0:T(8,128)(2,1)S(1)} %collective-permute-done.5), channel_id=1, source_target_pairs={{0,2},{1,3},{2,0},{3,1},{4,6},{5,7},{6,4},{7,5},{8,10},{9,11},{10,... | collective-permute-start | bytes 393224 | tf_op jit(solution)/shard_map/ppermute | solution.py:238
  19.7 0.1 collective-permute-done.1
  19.9 2.8 %collective-permute-done.2 = bf16[8,8192]{1,0:T(8,128)(2,1)S(1)} collective-permute-done((bf16[8,8192]{1,0:T(8,128)(2,1)S(1)}, bf16[8,8192]{1,0:T(8,128)(2,1)S(1)}, u32[]{:S(2)}, u32[]{:S(2)}) %collective-permute-start.2) | collective-permute-done | bytes 131104 | tf_op jit(solution)/shard_map/ppermute | solution.py:238
  22.8 2.0 %collective-permute-done.6 = bf16[8,8192]{1,0:T(8,128)(2,1)S(1)} collective-permute-done((bf16[8,8192]{1,0:T(8,128)(2,1)S(1)}, bf16[8,8192]{1,0:T(8,128)(2,1)S(1)}, u32[]{:S(2)}, u32[]{:S(2)}) %collective-permute-start.6) | collective-permute-done | bytes 131104 | tf_op jit(solution)/shard_map/ppermute | solution.py:238
  24.9 1.4 %collective-permute-done.7 = bf16[8,8192]{1,0:T(8,128)(2,1)S(1)} collective-permute-done((bf16[8,8192]{1,0:T(8,128)(2,1)S(1)}, bf16[8,8192]{1,0:T(8,128)(2,1)S(1)}, u32[]{:S(2)}, u32[]{:S(2)}) %collective-permute-start.7) | collective-permute-done | bytes 131104 | tf_op jit(solution)/shard_map/ppermute | solution.py:238
  26.4 1.9 %collective-permute-done.9.refs_3_ = bf16[32,8192]{1,0:T(8,128)(2,1)S(1)} collective-permute-done((bf16[32,8192]{1,0:T(8,128)(2,1)S(1)}, bf16[32,8192]{1,0:T(8,128)(2,1)S(1)}, u32[]{:S(2)}, u32[]{:S(2)}) %collective-permute-start.9) | collective-permute-done | bytes 524320 | tf_op jit(solution)/shard_map/ppermute | solution.py:238
  28.3 1.6 %shard_map.86 = (f32[128,512]{1,0:T(8,128)S(1)}, f32[128,512]{1,0:T(8,128)S(1)}, f32[16,8,128]{2,1,0:T(8,128)S(1)}) custom-call(s32[1]{0:T(128)} %bitcast.me_ref.refs_0_, bf16[128,128]{1,0:T(8,128)(2,1)S(1)} %get-tuple-element.17.pick_ref, f32[128,128]{1,0:T(8,128)S(1)} %get-tuple-element.16.label_ref.refs_1_, bf16[32,8192]{1,0:T(8,128)(2,1)S(1)} %pad_maximum_fusion.refs_0_, ...), custom_call_target="tpu_custom_call" | custom-call | flops 1073741824 | bytes 10485760 | tf_op jit(solution)/shard_map/pallas_call | solution.py:123
  29.9 12.8 %all_to_all.5.refs_2_ = f32[16,8,128]{2,1,0:T(8,128)S(1)} all-to-all(f32[16,8,128]{2,1,0:T(8,128)S(1)} %get-tuple-element.21), channel_id=1, replica_groups=mesh['groups'=2,'dp'=16] {'dp'}, dimensions={0} | all-to-all | bytes 131072 | tf_op jit(solution)/shard_map/all_to_all | solution.py:285
  42.7 1.6 %shard_map.87 = (f32[64,4096]{1,0:T(8,128)S(1)}, bf16[64,4096]{1,0:T(8,128)(2,1)S(1)}, bf16[128,512]{1,0:T(8,128)(2,1)S(1)}, f32[1,128]{1,0:T(1,128)S(1)}) custom-call(s32[1]{0:T(128)} %bitcast.me_ref.refs_0_, f32[128,128]{1,0:T(8,128)S(1)} %get-tuple-element.16.label_ref.refs_1_, f32[16,8,128]{2,1,0:T(8,128)S(1)} %all_to_all.5.refs_2_, ...), custom_call_target="tpu_custom_call" | custom-call | flops 536870912 | bytes 6291456 | tf_op jit(solution)/shard_map/pallas_call | solution.py:199
  44.4 1.9 %collective-permute-done.10 = bf16[64,4096]{1,0:T(8,128)(2,1)S(1)} collective-permute-done((bf16[64,4096]{1,0:T(8,128)(2,1)S(1)}, bf16[64,4096]{1,0:T(8,128)(2,1)S(1)}, u32[]{:S(2)}, u32[]{:S(2)}) %collective-permute-start.10) | collective-permute-done | bytes 524320 | tf_op jit(solution)/shard_map/ppermute | solution.py:238
  46.4 0.2 collective-permute-start.12
  46.6 1.9 %collective-permute-start.11 = (bf16[16,4096]{1,0:T(8,128)(2,1)S(1)}, bf16[16,4096]{1,0:T(8,128)(2,1)S(1)}, u32[]{:S(2)}, u32[]{:S(2)}) collective-permute-start(bf16[16,4096]{1,0:T(8,128)(2,1)S(1)} %get-tuple-element.34), channel_id=1, source_target_pairs={{0,2},{1,3},{2,0},{3,1},{4,6},{5,7},{6,4},{7,5},{8,10},{9,11},{10,... | collective-permute-start | bytes 393224 | tf_op jit(solution)/shard_map/ppermute | solution.py:238
  48.5 4.9 %shard_map.88 = bf16[4096,512]{1,0:T(8,128)(2,1)} custom-call(bf16[32,8192]{1,0:T(8,128)(2,1)S(1)} %pad_maximum_fusion.refs_0_, bf16[32,8192]{1,0:T(8,128)(2,1)S(1)} %pad_maximum_fusion.1.refs_1_, bf16[32,8192]{1,0:T(8,128)(2,1)S(1)} %collective-permute-done.8.refs_2_, bf16[32,8192]{1,0:T(8,128)(2,1)S(1)} %collective-permute-done.9.refs_3_, ...), custom_call_target="tpu_custom_call" | custom-call | flops 536870912 | bytes 5242880 | tf_op jit(solution)/shard_map/pallas_call | solution.py:223
  53.4 1.4 %collective-permute-done.11 = bf16[16,4096]{1,0:T(8,128)(2,1)S(1)} collective-permute-done((bf16[16,4096]{1,0:T(8,128)(2,1)S(1)}, bf16[16,4096]{1,0:T(8,128)(2,1)S(1)}, u32[]{:S(2)}, u32[]{:S(2)}) %collective-permute-start.11) | collective-permute-done | bytes 131104 | tf_op jit(solution)/shard_map/ppermute | solution.py:238
  54.9 0.2 collective-permute-start.15
  55.1 1.0 %collective-permute-start.13 = (bf16[8,4096]{1,0:T(8,128)(2,1)S(1)}, bf16[8,4096]{1,0:T(8,128)(2,1)S(1)}, u32[]{:S(2)}, u32[]{:S(2)}) collective-permute-start(bf16[8,4096]{1,0:T(8,128)(2,1)S(1)} %get-tuple-element.35), channel_id=1, source_target_pairs={{0,8},{1,9},{2,10},{3,11},{4,12},{5,13},{6,14},{7,15},{8,0},{9,1},... | collective-permute-start | bytes 196616 | tf_op jit(solution)/shard_map/ppermute | solution.py:238
  56.1 3.3 %collective-permute-start.14 = (bf16[8,4096]{1,0:T(8,128)(2,1)S(1)}, bf16[8,4096]{1,0:T(8,128)(2,1)S(1)}, u32[]{:S(2)}, u32[]{:S(2)}) collective-permute-start(bf16[8,4096]{1,0:T(8,128)(2,1)S(1)} %get-tuple-element.36), channel_id=1, source_target_pairs={{0,12},{1,13},{2,14},{3,15},{4,8},{5,9},{6,10},{7,11},{8,4},{9,5},... | collective-permute-start | bytes 196616 | tf_op jit(solution)/shard_map/ppermute | solution.py:238
  59.4 0.5 slice_bitcast_fusion
  59.9 2.9 %collective-permute-done.13 = bf16[8,4096]{1,0:T(8,128)(2,1)S(1)} collective-permute-done((bf16[8,4096]{1,0:T(8,128)(2,1)S(1)}, bf16[8,4096]{1,0:T(8,128)(2,1)S(1)}, u32[]{:S(2)}, u32[]{:S(2)}) %collective-permute-start.13) | collective-permute-done | bytes 65568 | tf_op jit(solution)/shard_map/ppermute | solution.py:238
  62.8 0.7 %fusion.2 = f32[8,4096]{1,0:T(8,128)} fusion(f32[16,4096]{1,0:T(8,128)S(1)} %get-tuple-element.32, bf16[8,4096]{1,0:T(8,128)(2,1)S(1)} %collective-permute-done.15, bf16[8,4096]{1,0:T(8,128)(2,1)S(1)} %collective-permute-done.14, bf16[8,4096]{1,0:T(8,128)(2,1)S(1)} %collective-permute-done.13), kind=kLoop, calls=%fused_computation.9 | loop fusion | flops 196608 | bytes 458752 | tf_op jit(solution)/shard_map/add | solution.py:271
  (22 shorter events, 0.6 us)
Async XLA Ops:
  0.6 12.5 %collective-permute-start.3 = (bf16[8,4096]{1,0:T(8,128)(2,1)}, bf16[8,4096]{1,0:T(8,128)(2,1)S(1)}, u32[]{:S(2)}, u32[]{:S(2)}) collective-permute-start(bf16[8,4096]{1,0:T(8,128)(2,1)} %param.6), channel_id=1, source_target_pairs={{0,8},{1,9},{2,10},{3,11},{4,12},{5,13},{6,14},{7,15},{8,0},{9,1},... | collective-permute-start | bytes 196616 | tf_op jit(solution)/shard_map/ppermute | solution.py:238
  4.7 8.4 %collective-permute-start.4 = (bf16[8,4096]{1,0:T(8,128)(2,1)}, bf16[8,4096]{1,0:T(8,128)(2,1)S(1)}, u32[]{:S(2)}, u32[]{:S(2)}) collective-permute-start(bf16[8,4096]{1,0:T(8,128)(2,1)} %param.7), channel_id=1, source_target_pairs={{0,8},{1,9},{2,10},{3,11},{4,12},{5,13},{6,14},{7,15},{8,0},{9,1},... | collective-permute-start | bytes 196616 | tf_op jit(solution)/shard_map/ppermute | solution.py:238
  6.5 8.7 %collective-permute-start = (bf16[8,8192]{1,0:T(8,128)(2,1)S(1)}, bf16[8,8192]{1,0:T(8,128)(2,1)S(1)}, u32[]{:S(2)}, u32[]{:S(2)}) collective-permute-start(bf16[8,8192]{1,0:T(8,128)(2,1)S(1)} %constant_dynamic-update-slice_fusion), channel_id=1, source_target_pairs={{0,4},{1,5},{2,6},{3,7},{4,0},{5,1},{6,2},{7,3},{8,12},{9,13},{10,... | collective-permute-start | bytes 393224 | tf_op jit(solution)/shard_map/ppermute | solution.py:238
  8.3 0.7 %copy-start = (s32[128]{0:T(128)S(1)}, s32[128]{0:T(128)}, u32[]{:S(2)}) copy-start(s32[128]{0:T(128)} %param.11) | copy-start | bytes 1540
  9.0 0.7 %copy-start.1 = (s32[128]{0:T(128)S(1)}, s32[128]{0:T(128)}, u32[]{:S(2)}) copy-start(s32[128]{0:T(128)} %param.10) | copy-start | bytes 1540
  13.2 5.0 %collective-permute-start.5 = (bf16[8,8192]{1,0:T(8,128)(2,1)S(1)}, bf16[8,8192]{1,0:T(8,128)(2,1)S(1)}, u32[]{:S(2)}, u32[]{:S(2)}) collective-permute-start(bf16[8,8192]{1,0:T(8,128)(2,1)S(1)} %constant_dynamic-update-slice_fusion.2), channel_id=1, source_target_pairs={{0,4},{1,5},{2,6},{3,7},{4,0},{5,1},{6,2},{7,3},{8,12},{9,13},{10,... | collective-permute-start | bytes 393224 | tf_op jit(solution)/shard_map/ppermute | solution.py:238
  13.4 6.4 %collective-permute-start.1 = (bf16[8,8192]{1,0:T(8,128)(2,1)S(1)}, bf16[8,8192]{1,0:T(8,128)(2,1)S(1)}, u32[]{:S(2)}, u32[]{:S(2)}) collective-permute-start(bf16[8,8192]{1,0:T(8,128)(2,1)S(1)} %constant_dynamic-update-slice_fusion), channel_id=1, source_target_pairs={{0,2},{1,3},{2,0},{3,1},{4,6},{5,7},{6,4},{7,5},{8,10},{9,11},{10,... | collective-permute-start | bytes 393224 | tf_op jit(solution)/shard_map/ppermute | solution.py:238
  15.2 7.5 %collective-permute-start.2 = (bf16[8,8192]{1,0:T(8,128)(2,1)S(1)}, bf16[8,8192]{1,0:T(8,128)(2,1)S(1)}, u32[]{:S(2)}, u32[]{:S(2)}) collective-permute-start(bf16[8,8192]{1,0:T(8,128)(2,1)S(1)} %collective-permute-done), channel_id=1, source_target_pairs={{0,2},{1,3},{2,0},{3,1},{4,6},{5,7},{6,4},{7,5},{8,10},{9,11},{10,... | collective-permute-start | bytes 393224 | tf_op jit(solution)/shard_map/ppermute | solution.py:238
  15.5 9.4 %collective-permute-start.6 = (bf16[8,8192]{1,0:T(8,128)(2,1)S(1)}, bf16[8,8192]{1,0:T(8,128)(2,1)S(1)}, u32[]{:S(2)}, u32[]{:S(2)}) collective-permute-start(bf16[8,8192]{1,0:T(8,128)(2,1)S(1)} %constant_dynamic-update-slice_fusion.2), channel_id=1, source_target_pairs={{0,2},{1,3},{2,0},{3,1},{4,6},{5,7},{6,4},{7,5},{8,10},{9,11},{10,... | collective-permute-start | bytes 393224 | tf_op jit(solution)/shard_map/ppermute | solution.py:238
  18.2 8.0 %collective-permute-start.7 = (bf16[8,8192]{1,0:T(8,128)(2,1)S(1)}, bf16[8,8192]{1,0:T(8,128)(2,1)S(1)}, u32[]{:S(2)}, u32[]{:S(2)}) collective-permute-start(bf16[8,8192]{1,0:T(8,128)(2,1)S(1)} %collective-permute-done.5), channel_id=1, source_target_pairs={{0,2},{1,3},{2,0},{3,1},{4,6},{5,7},{6,4},{7,5},{8,10},{9,11},{10,... | collective-permute-start | bytes 393224 | tf_op jit(solution)/shard_map/ppermute | solution.py:238
  22.7 3.6 %collective-permute-start.8 = (bf16[32,8192]{1,0:T(8,128)(2,1)S(1)}, bf16[32,8192]{1,0:T(8,128)(2,1)S(1)}, u32[]{:S(2)}, u32[]{:S(2)}) collective-permute-start(bf16[32,8192]{1,0:T(8,128)(2,1)S(1)} %pad_maximum_fusion.refs_0_), channel_id=1, source_target_pairs={{0,1},{1,0},{2,3},{3,2},{4,5},{5,4},{6,7},{7,6},{8,9},{9,8},{10,11... | collective-permute-start | bytes 1572872 | tf_op jit(solution)/shard_map/ppermute | solution.py:238
  26.3 2.0 %collective-permute-start.9 = (bf16[32,8192]{1,0:T(8,128)(2,1)S(1)}, bf16[32,8192]{1,0:T(8,128)(2,1)S(1)}, u32[]{:S(2)}, u32[]{:S(2)}) collective-permute-start(bf16[32,8192]{1,0:T(8,128)(2,1)S(1)} %pad_maximum_fusion.1.refs_1_), channel_id=1, source_target_pairs={{0,1},{1,0},{2,3},{3,2},{4,5},{5,4},{6,7},{7,6},{8,9},{9,8},{10,11... | collective-permute-start | bytes 1572872 | tf_op jit(solution)/shard_map/ppermute | solution.py:238
  44.3 2.0 %collective-permute-start.10 = (bf16[64,4096]{1,0:T(8,128)(2,1)S(1)}, bf16[64,4096]{1,0:T(8,128)(2,1)S(1)}, u32[]{:S(2)}, u32[]{:S(2)}) collective-permute-start(bf16[64,4096]{1,0:T(8,128)(2,1)S(1)} %get-tuple-element.26), channel_id=1, source_target_pairs={{0,1},{1,0},{2,3},{3,2},{4,5},{5,4},{6,7},{7,6},{8,9},{9,8},{10,11... | collective-permute-start | bytes 1572872 | tf_op jit(solution)/shard_map/ppermute | solution.py:238
  46.4 7.0 %collective-permute-start.12 = (bf16[16,4096]{1,0:T(8,128)(2,1)S(1)}, bf16[16,4096]{1,0:T(8,128)(2,1)S(1)}, u32[]{:S(2)}, u32[]{:S(2)}) collective-permute-start(bf16[16,4096]{1,0:T(8,128)(2,1)S(1)} %get-tuple-element.33), channel_id=1, source_target_pairs={{0,2},{1,3},{2,0},{3,1},{4,6},{5,7},{6,4},{7,5},{8,10},{9,11},{10,... | collective-permute-start | bytes 393224 | tf_op jit(solution)/shard_map/ppermute | solution.py:238
  46.6 8.2 %collective-permute-start.11 = (bf16[16,4096]{1,0:T(8,128)(2,1)S(1)}, bf16[16,4096]{1,0:T(8,128)(2,1)S(1)}, u32[]{:S(2)}, u32[]{:S(2)}) collective-permute-start(bf16[16,4096]{1,0:T(8,128)(2,1)S(1)} %get-tuple-element.34), channel_id=1, source_target_pairs={{0,2},{1,3},{2,0},{3,1},{4,6},{5,7},{6,4},{7,5},{8,10},{9,11},{10,... | collective-permute-start | bytes 393224 | tf_op jit(solution)/shard_map/ppermute | solution.py:238
  54.9 5.0 %collective-permute-start.15 = (bf16[8,4096]{1,0:T(8,128)(2,1)S(1)}, bf16[8,4096]{1,0:T(8,128)(2,1)S(1)}, u32[]{:S(2)}, u32[]{:S(2)}) collective-permute-start(bf16[8,4096]{1,0:T(8,128)(2,1)S(1)} %slice.58), channel_id=1, source_target_pairs={{0,4},{1,5},{2,6},{3,7},{4,0},{5,1},{6,2},{7,3},{8,12},{9,13},{10,... | collective-permute-start | bytes 196616 | tf_op jit(solution)/shard_map/ppermute | solution.py:238
  55.1 7.7 %collective-permute-start.13 = (bf16[8,4096]{1,0:T(8,128)(2,1)S(1)}, bf16[8,4096]{1,0:T(8,128)(2,1)S(1)}, u32[]{:S(2)}, u32[]{:S(2)}) collective-permute-start(bf16[8,4096]{1,0:T(8,128)(2,1)S(1)} %get-tuple-element.35), channel_id=1, source_target_pairs={{0,8},{1,9},{2,10},{3,11},{4,12},{5,13},{6,14},{7,15},{8,0},{9,1},... | collective-permute-start | bytes 196616 | tf_op jit(solution)/shard_map/ppermute | solution.py:238
  56.1 6.7 %collective-permute-start.14 = (bf16[8,4096]{1,0:T(8,128)(2,1)S(1)}, bf16[8,4096]{1,0:T(8,128)(2,1)S(1)}, u32[]{:S(2)}, u32[]{:S(2)}) collective-permute-start(bf16[8,4096]{1,0:T(8,128)(2,1)S(1)} %get-tuple-element.36), channel_id=1, source_target_pairs={{0,12},{1,13},{2,14},{3,15},{4,8},{5,9},{6,10},{7,11},{8,4},{9,5},... | collective-permute-start | bytes 196616 | tf_op jit(solution)/shard_map/ppermute | solution.py:238

commit v3 on v2

--- a/solution.py
+++ b/solution.py
@@ -8,6 +8,7 @@
 from jax.sharding import PartitionSpec as P
 
 CE_WEIGHT = 0.5
+FETCH_PARTS = 4
 STATS = 8
 
 
@@ -30,50 +31,82 @@
     return jnp.sum(jnp.where(is_row, row, 0.0), axis=1, keepdims=True)
 
 
+def fetch_copies(source, target, sems):
+    rows = source.shape[0] // sems.shape[0]
+    parts = [pl.ds(k * rows, rows) for k in range(sems.shape[0])]
+    return [pltpu.make_async_copy(source.at[part], target.at[part], sems.at[k]) for k, part in enumerate(parts)]
+
+
+def fetch_kernel(after_ref, source, target, sems):
+    copies = fetch_copies(source, target, sems)
+    for copy in copies:
+        copy.start()
+    for copy in copies:
+        copy.wait()
+
+
 def prepare_kernel(
-    rows_local, tuned, me_ref, order_ref, labels_ref, teacher_ref, student_ref, teacher_out, student_out, pick_out, label_out, sems
+    rows_local, tuned, me_ref, order_ref, labels_ref, head_ref, head_out, pick_out, label_out, ids, id_sems, sems
 ):
-    copies = []
-    pieces = sems.shape[1]
-    rows = teacher_ref.shape[0] // pieces
-    for k in range(pieces):
-        for j, (source, target) in enumerate(((teacher_ref, teacher_out), (student_ref, student_out))):
-            part = pl.ds(k * rows, rows)
-            copies.append(pltpu.make_async_copy(source.at[part], target.at[part], sems.at[j, k]))
-    for copy in copies:
+    id_copies = [
+        pltpu.make_async_copy(source, ids.at[j], id_sems.at[j]) for j, source in enumerate((order_ref, labels_ref))
+    ]
+    copies = fetch_copies(head_ref, head_out, sems)
+    for copy in id_copies + copies:
         copy.start()
     me = me_ref[0]
     count = order_ref.shape[1]
-    vocab = teacher_ref.shape[1]
+    vocab = head_ref.shape[1]
     lanes = lax.broadcasted_iota(jnp.int32, (count, count), 1)
     is_row = held_rows((count, count), 0, me, rows_local, tuned) == lanes
-    wanted = to_column(is_row, order_ref[...].astype(jnp.float32))
     have = held_rows((count, count), 1, me, rows_local, tuned).astype(jnp.float32)
+    for copy in id_copies:
+        copy.wait()
+    wanted = to_column(is_row, ids[0].astype(jnp.float32))
     pick_out[...] = jnp.where(wanted == have, 1.0, 0.0).astype(jnp.bfloat16)
-    label = to_column(is_row, labels_ref[...].astype(jnp.float32)) - (me * vocab).astype(jnp.float32)
+    label = to_column(is_row, ids[1].astype(jnp.float32)) - (me * vocab).astype(jnp.float32)
     label_out[...] = jnp.broadcast_to(label, label_out.shape)
     for copy in copies:
         copy.wait()
 
 
-def prepare(me, order, labels, heads, rows_local, tuned):
+def stay(value):
+    return pltpu.with_memory_space_constraint(value, pltpu.HBM)
+
+
+def fetch(me, head):
+    return pl.pallas_call(
+        fetch_kernel,
+        in_specs=[pl.BlockSpec(memory_space=pltpu.SMEM), pl.BlockSpec(memory_space=pltpu.HBM)],
+        out_specs=pl.BlockSpec(memory_space=pltpu.VMEM),
+        out_shape=jax.ShapeDtypeStruct(head.shape, head.dtype),
+        scratch_shapes=[pltpu.SemaphoreType.DMA((FETCH_PARTS,))],
+        compiler_params=pltpu.CompilerParams(vmem_limit_bytes=24 * 2**20),
+        cost_estimate=pl.CostEstimate(flops=0, bytes_accessed=head.size * 4, transcendentals=0),
+    )(me, stay(head))
+
+
+def prepare(me, order, labels, head, rows_local, tuned):
     count = order.shape[0]
     vmem = pl.BlockSpec(memory_space=pltpu.VMEM)
     hbm = pl.BlockSpec(memory_space=pltpu.HBM)
     return pl.pallas_call(
         functools.partial(prepare_kernel, rows_local, tuned),
-        in_specs=[pl.BlockSpec(memory_space=pltpu.SMEM), vmem, vmem, hbm, hbm],
-        out_specs=(vmem,) * 4,
+        in_specs=[pl.BlockSpec(memory_space=pltpu.SMEM)] + [hbm] * 3,
+        out_specs=(vmem,) * 3,
         out_shape=(
-            jax.ShapeDtypeStruct(heads[0].shape, heads[0].dtype),
-            jax.ShapeDtypeStruct(heads[1].shape, heads[1].dtype),
+            jax.ShapeDtypeStruct(head.shape, head.dtype),
             jax.ShapeDtypeStruct((count, count), jnp.bfloat16),
             jax.ShapeDtypeStruct((count, 128), jnp.float32),
         ),
-        scratch_shapes=[pltpu.SemaphoreType.DMA((2, 4))],
+        scratch_shapes=[
+            pltpu.VMEM((2, 1, count), jnp.int32),
+            pltpu.SemaphoreType.DMA((2,)),
+            pltpu.SemaphoreType.DMA((FETCH_PARTS,)),
+        ],
         compiler_params=pltpu.CompilerParams(vmem_limit_bytes=24 * 2**20),
-        cost_estimate=pl.CostEstimate(flops=0, bytes_accessed=2 * heads[0].size * 4, transcendentals=0),
-    )(me, order[None], labels[None], *(pltpu.with_memory_space_constraint(head, pltpu.HBM) for head in heads))
+        cost_estimate=pl.CostEstimate(flops=0, bytes_accessed=head.size * 4, transcendentals=0),
+    )(me, stay(order[None]), stay(labels[None]), stay(head))
 
 
 def logits_kernel(rows_local, tuned, parts, me_ref, pick_ref, label_ref, *refs):
@@ -210,28 +243,34 @@
 
 def head_kernel(parts, *refs):
     rows = jnp.concatenate([piece[...] for piece in refs[:parts]], axis=0)
-    grad_ref, out_ref = refs[parts:]
+    grad_ref, out_ref = refs[parts], refs[-1]
     out_ref[...] = lax.dot_general(
         rows, grad_ref[...], (((0,), (0,)), ((), ())), preferred_element_type=jnp.float32
     ).astype(jnp.bfloat16)
 
 
-def head_gradient(hidden, logit_grad, depth):
+def head_gradient(hidden, logit_grad, depth, part, parts, written):
     count, vocab = logit_grad.shape
     step = min(512, depth)
-    first = depth // step
+    steps = depth // step // parts
+    first = depth // step + part * steps
+    more = () if written is None else (written,)
     return pl.pallas_call(
         functools.partial(head_kernel, len(hidden)),
-        grid=(depth // step,),
+        grid=(steps,),
         in_specs=[pl.BlockSpec((piece.shape[0], step), lambda k: (0, k + first)) for piece in hidden]
-        + [pl.BlockSpec((count, vocab), lambda k: (0, 0))],
-        out_specs=pl.BlockSpec((step, vocab), lambda k: (k, 0)),
+        + [pl.BlockSpec((count, vocab), lambda k: (0, 0))]
+        + [pl.BlockSpec(memory_space=pl.ANY)] * len(more),
+        out_specs=pl.BlockSpec((step, vocab), lambda k: (k + part * steps, 0)),
         out_shape=jax.ShapeDtypeStruct((depth, vocab), jnp.bfloat16),
+        input_output_aliases={len(hidden) + 1: 0} if more else {},
         compiler_params=pltpu.CompilerParams(vmem_limit_bytes=40 * 2**20),
         cost_estimate=pl.CostEstimate(
-            flops=2 * count * depth * vocab, bytes_accessed=2 * depth * (vocab + count), transcendentals=0
-        ),
-    )(*hidden, logit_grad)
+            flops=2 * count * depth * vocab // parts,
+            bytes_accessed=2 * depth * (vocab + count) // parts,
+            transcendentals=0,
+        ),
+    )(*hidden, logit_grad, *more)
 
 
 def swap(value, distance, n):
@@ -242,53 +281,70 @@
     return lax.optimization_barrier((value, *done))[0]
 
 
-def gather_rows(teacher_rows, student_rows, n, prepared):
-    far = jnp.concatenate([after(swap(teacher_rows, 8, n), *prepared), swap(student_rows, 8, n)], axis=1)
-    rows = jnp.concatenate([teacher_rows, student_rows], axis=1)
-    side = swap(rows, 2, n)
-    near = swap(rows, 4, n)
-    far_near = swap(far, 4, n)
-    near_side = swap(near, 2, n)
-    far_side = swap(far, 2, n)
-    far_near_side = swap(far_near, 2, n)
-    first = jnp.concatenate([rows, near, side, near_side], axis=0)
-    second = jnp.concatenate([far, far_near, far_side, far_near_side], axis=0)
-    return [first, second, swap(first, 1, n), swap(second, 1, n)]
-
-
-def scatter_rows(keep, send, rows_local, n, grad_head):
+def gather_rows(teacher_rows, student_rows, n, teacher_fetch, student_fetch):
+    join = lambda pair: jnp.concatenate(pair, axis=1)
+    both = (teacher_rows, student_rows)
+    far = [swap(rows, 8, n) for rows in both]
+    near = [swap(rows, 4, n) for rows in both]
+    side = [swap(rows, 2, n) for rows in both]
+    teacher_fetched = teacher_fetch(None)
+    far[0] = after(far[0], *side, *teacher_fetched)
+    far_near = [swap(rows, 4, n) for rows in far]
+    far_side = [swap(rows, 2, n) for rows in far]
+    near_side = swap(join(near), 2, n)
+    far_near_side = [swap(rows, 2, n) for rows in far_near]
+    first = jnp.concatenate([join(both), join(near), join(side), near_side], axis=0)
+    second = jnp.concatenate([join(far), join(far_near), join(far_side), join(far_near_side)], axis=0)
+    student_fetched = student_fetch(far_near_side[1])
+    return [first, second, swap(first, 1, n), swap(second, 1, n)], teacher_fetched, student_fetched
+
+
+def scatter_rows(keep, send, logit_grad, rows_local, n, head_parts):
     low = jnp.bfloat16
     full = jnp.float32
-    held = keep + swap(send, 1, n).astype(full)
-    quarter = 2 * rows_local
-    near_keep, near_send, far_keep, far_send = (held[k * quarter : (k + 1) * quarter] for k in range(4))
-    far_part = after(swap(far_send.astype(low), 2, n), grad_head)
-    far = (far_keep + far_part.astype(full)).astype(low)
-    near = near_keep + swap(near_send.astype(low), 2, n).astype(full)
+    half = 2 * rows_local
+    other = swap(send, 1, n)
+    held = keep + other.astype(full)
+    near_keep, near_send, far_keep, far_send = (held[k * half : (k + 1) * half] for k in range(4))
+    near_keep, near_send, far_keep, far_send = lax.optimization_barrier(
+        (near_keep, near_send.astype(low), far_keep, far_send.astype(low))
+    )
+    far_other = swap(far_send, 2, n)
+    part = head_parts(0, after(logit_grad, other), None)
+    near_other = swap(after(near_send, part), 2, n)
+    far = (far_keep + far_other.astype(full)).astype(low)
     from_far = swap(far[:rows_local], 8, n)
     from_far_near = swap(far[rows_local:], 12, n)
+    grad_head = head_parts(1, after(logit_grad, far_other), part)
+    near = near_keep + after(near_other, grad_head).astype(full)
     from_near = swap(near[rows_local:].astype(low), 4, n)
-    return near[:rows_local] + from_far.astype(full) + from_far_near.astype(full) + from_near.astype(full)
+    total = near[:rows_local] + from_far.astype(full) + from_far_near.astype(full) + from_near.astype(full)
+    return total, grad_head
 
 
 def per_device(n, teacher_hidden, student_hidden, teacher_head, student_head, labels, order):
     rows_local, depth = student_hidden.shape
     tuned = xor_order(n) is not None and rows_local == 8
     me = lax.axis_index("dp").astype(jnp.int32).reshape(1)
-    *heads, pick, label = prepare(me, order, labels, (teacher_head, student_head), rows_local, tuned)
+    teacher_fetch = lambda done: prepare(me if done is None else after(me, done), order, labels, teacher_head, rows_local, tuned)
+    student_fetch = lambda done: fetch(after(me, done), student_head)
     if tuned:
-        hidden = gather_rows(teacher_hidden, student_hidden, n, (*heads, pick, label))
+        hidden, *fetched = gather_rows(teacher_hidden, student_hidden, n, teacher_fetch, student_fetch)
     else:
+        fetched = teacher_fetch(me), student_fetch(me)
         rows = jnp.concatenate([teacher_hidden, student_hidden], axis=1)
         hidden = [lax.all_gather(rows, "dp", axis=0, tiled=True)]
+    (teacher_head, pick, label), student_head = fetched
+    heads = (teacher_head, student_head)
     teacher_logits, student_logits, stats = logits(me, pick, label, hidden, heads, n, rows_local, tuned)
     stats = lax.all_to_all(stats, "dp", 0, 0)
     outs = gradient(me, label, stats, teacher_logits, student_logits, heads[1], rows_local, tuned)
     logit_grad, loss = outs[-2:]
-    grad_head = head_gradient(hidden, logit_grad, depth)
     if tuned:
-        grad_hidden = scatter_rows(outs[0], outs[1], rows_local, n, grad_head)
+        head_parts = lambda part, logit_grad, written: head_gradient(hidden, logit_grad, depth, part, 2, written)
+        grad_hidden, grad_head = scatter_rows(outs[0], outs[1], logit_grad, rows_local, n, head_parts)
     else:
+        grad_head = head_gradient(hidden, logit_grad, depth, 0, 1, None)
         grad_hidden = lax.psum_scatter(outs[0], "dp", scatter_dimension=0, tiled=True)
     return (loss[0, :rows_local], grad_hidden, grad_head)
 

time: 63.8 us -> 59.4 us (0.931)
  local copies, waits for them, and re-layouts: 3.56 us -> 0.61 us
  waiting for transfers between devices: 15.5 us -> 12.6 us
  starting transfers between devices: 18.3 us -> 21.1 us
  blocking collectives: 12.8 us -> 10.3 us
  Pallas kernels: 11.5 us -> 13 us
    ppermute x16 -> x21, waiting for transfers between devices: 15.5 us -> 12.6 us  [swap(): return lax.ppermute(value, 'dp', [(i, i ^ distance) for i in range(n)])]
    ppermute x16 -> x21, starting transfers between devices: 18.3 us -> 21.1 us  [swap(): return lax.ppermute(value, 'dp', [(i, i ^ distance) for i in range(n)])]
    pallas_call x1 -> x3, Pallas kernels: 4.87 us -> 7.46 us  [the longest x2 5.25 us: head_gradient(): pl.pallas_call(functools.partial(head_kernel, len(hidden)), grid=(steps,)...]
    all_to_all x1, blocking collectives: 12.8 us -> 10.3 us  [per_device(): stats = lax.all_to_all(stats, 'dp', 0, 0)]
    unnamed x6 -> x5, local copies, waits for them, and re-layouts: 2.16 us -> 0.01 us
    pallas_call x1, Pallas kernels: 3.47 us -> 2.26 us  [prepare(): pl.pallas_call(functools.partial(prepare_kernel, rows_local, tuned), in_s...]
    concatenate x2 -> x1, local copies, waits for them, and re-layouts: 0.85 us -> 0.01 us  [gather_rows(): join = lambda pair: jnp.concatenate(pair, axis=1)]
  transfers between devices with their start and end apart: 16 -> 21, of which waited for: 9 -> 9; matrix products, arithmetic and copies ran while one was open for 4% -> 1% of each run, Pallas kernels for 13% -> 16%
where the time goes in v3:
time: 59.4 us; the launch traced here: 59.3 us
  starting transfers between devices  21.1 us (36%)
  Pallas kernels  13 us (22%)
  waiting for transfers between devices  12.6 us (21%)
  blocking collectives  10.3 us (17%)
  other arithmetic  0.96 us (2%)
  between operations  0.83 us (1%)
  local copies, waits for them, and re-layouts  0.61 us (1%)
    ppermute x21, starting transfers between devices, swap(): return lax.ppermute(value, 'dp', [(i, i ^ distance) for i in range(n)])  21.1 us
    ppermute x21, waiting for transfers between devices, swap(): return lax.ppermute(value, 'dp', [(i, i ^ distance) for i in range(n)])  12.6 us
    all_to_all x1, blocking collectives, per_device(): stats = lax.all_to_all(stats, 'dp', 0, 0)  10.3 us
    pallas_call x2, Pallas kernels, head_gradient(): pl.pallas_call(functools.partial(head_kernel, len(hidden)), grid=(steps,)...  5.25 us
    pallas_call x1, Pallas kernels, prepare(): pl.pallas_call(functools.partial(prepare_kernel, rows_local, tuned), in_s...  2.26 us
    pallas_call x1, Pallas kernels, fetch(): pl.pallas_call(fetch_kernel, in_specs=[pl.BlockSpec(memory_space=pltpu.SM...  2.21 us
    pallas_call x1, Pallas kernels, logits(): pl.pallas_call(functools.partial(logits_kernel, rows_local, tuned, len(hi...  1.68 us
    pallas_call x1, Pallas kernels, gradient(): pl.pallas_call(kernel, in_specs=[pl.BlockSpec(memory_space=pltpu.SMEM)] +...  1.58 us
  transfers between devices with their start and end apart: 21, of which 9 were waited for; matrix products, arithmetic and copies ran while one was open for 1% of the time, Pallas kernels for 16%

profile of v3, /device:TPU:0, one launch (start us, length us, event | category | flops | bytes accessed | tf_op | source)
XLA Modules:
  0.0 59.3 jit_solution(9597625463659510216)
XLA Ops:
  0.6 3.1 %collective-permute-start = (bf16[8,4096]{1,0:T(8,128)(2,1)}, bf16[8,4096]{1,0:T(8,128)(2,1)S(1)}, u32[]{:S(2)}, u32[]{:S(2)}) collective-permute-start(bf16[8,4096]{1,0:T(8,128)(2,1)} %param.6), channel_id=1, source_target_pairs={{0,4},{1,5},{2,6},{3,7},{4,0},{5,1},{6,2},{7,3},{8,12},{9,13},{10,... | collective-permute-start | bytes 196616 | tf_op jit(solution)/shard_map/ppermute | solution.py:277
  3.7 2.6 %collective-permute-start.5 = (bf16[8,4096]{1,0:T(8,128)(2,1)}, bf16[8,4096]{1,0:T(8,128)(2,1)S(1)}, u32[]{:S(2)}, u32[]{:S(2)}) collective-permute-start(bf16[8,4096]{1,0:T(8,128)(2,1)} %param.6), channel_id=1, source_target_pairs={{0,8},{1,9},{2,10},{3,11},{4,12},{5,13},{6,14},{7,15},{8,0},{9,1},... | collective-permute-start | bytes 196616 | tf_op jit(solution)/shard_map/ppermute | solution.py:277
  6.3 1.5 %collective-permute-start.2 = (bf16[8,4096]{1,0:T(8,128)(2,1)}, bf16[8,4096]{1,0:T(8,128)(2,1)S(1)}, u32[]{:S(2)}, u32[]{:S(2)}) collective-permute-start(bf16[8,4096]{1,0:T(8,128)(2,1)} %param.6), channel_id=1, source_target_pairs={{0,2},{1,3},{2,0},{3,1},{4,6},{5,7},{6,4},{7,5},{8,10},{9,11},{10,... | collective-permute-start | bytes 196616 | tf_op jit(solution)/shard_map/ppermute | solution.py:277
  7.8 0.4 collective-permute-start.1
  8.3 0.3 collective-permute-start.6
  8.8 3.5 %collective-permute-done.1 = bf16[8,4096]{1,0:T(8,128)(2,1)S(1)} collective-permute-done((bf16[8,4096]{1,0:T(8,128)(2,1)}, bf16[8,4096]{1,0:T(8,128)(2,1)S(1)}, u32[]{:S(2)}, u32[]{:S(2)}) %collective-permute-start.1) | collective-permute-done | bytes 65568 | tf_op jit(solution)/shard_map/ppermute | solution.py:277
  12.3 0.8 %collective-permute-start.4 = (bf16[8,8192]{1,0:T(8,128)(2,1)S(1)}, bf16[8,8192]{1,0:T(8,128)(2,1)S(1)}, u32[]{:S(2)}, u32[]{:S(2)}) collective-permute-start(bf16[8,8192]{1,0:T(8,128)(2,1)S(1)} %constant_dynamic-update-slice_fusion), channel_id=1, source_target_pairs={{0,2},{1,3},{2,0},{3,1},{4,6},{5,7},{6,4},{7,5},{8,10},{9,11},{10,... | collective-permute-start | bytes 393224 | tf_op jit(solution)/shard_map/ppermute | solution.py:277
  13.2 2.3 %shard_map.85 = (bf16[4096,512]{1,0:T(8,128)(2,1)S(1)}, bf16[128,128]{1,0:T(8,128)(2,1)S(1)}, f32[128,128]{1,0:T(8,128)S(1)}) custom-call(s32[1]{0:T(128)} %bitcast.me_ref.after_ref.refs_0_, s32[1,128]{1,0:T(1,128)} %bitcast.5, s32[1,128]{1,0:T(1,128)} %bitcast.6, bf16[4096,512]{1,0:T(8,128)(2,1)} %head_ref.1), custom_call_target="tpu_custom_call" | custom-call | bytes 8388608 | tf_op jit(solution)/shard_map/pallas_call | solution.py:93
  15.5 0.7 %collective-permute-start.8 = (bf16[8,4096]{1,0:T(8,128)(2,1)S(1)}, bf16[8,4096]{1,0:T(8,128)(2,1)S(1)}, u32[]{:S(2)}, u32[]{:S(2)}) collective-permute-start(bf16[8,4096]{1,0:T(8,128)(2,1)S(1)} %collective-permute-done.6), channel_id=1, source_target_pairs={{0,4},{1,5},{2,6},{3,7},{4,0},{5,1},{6,2},{7,3},{8,12},{9,13},{10,... | collective-permute-start | bytes 196616 | tf_op jit(solution)/shard_map/ppermute | solution.py:277
  16.1 1.4 %collective-permute-start.7 = (bf16[8,4096]{1,0:T(8,128)(2,1)S(1)}, bf16[8,4096]{1,0:T(8,128)(2,1)S(1)}, u32[]{:S(2)}, u32[]{:S(2)}) collective-permute-start(bf16[8,4096]{1,0:T(8,128)(2,1)S(1)} %collective-permute-done.5), channel_id=1, source_target_pairs={{0,4},{1,5},{2,6},{3,7},{4,0},{5,1},{6,2},{7,3},{8,12},{9,13},{10,... | collective-permute-start | bytes 196616 | tf_op jit(solution)/shard_map/ppermute | solution.py:277
  17.6 1.2 %collective-permute-start.9 = (bf16[8,4096]{1,0:T(8,128)(2,1)S(1)}, bf16[8,4096]{1,0:T(8,128)(2,1)S(1)}, u32[]{:S(2)}, u32[]{:S(2)}) collective-permute-start(bf16[8,4096]{1,0:T(8,128)(2,1)S(1)} %collective-permute-done.5), channel_id=1, source_target_pairs={{0,2},{1,3},{2,0},{3,1},{4,6},{5,7},{6,4},{7,5},{8,10},{9,11},{10,... | collective-permute-start | bytes 196616 | tf_op jit(solution)/shard_map/ppermute | solution.py:277
  18.8 0.8 %collective-permute-start.10 = (bf16[8,4096]{1,0:T(8,128)(2,1)S(1)}, bf16[8,4096]{1,0:T(8,128)(2,1)S(1)}, u32[]{:S(2)}, u32[]{:S(2)}) collective-permute-start(bf16[8,4096]{1,0:T(8,128)(2,1)S(1)} %collective-permute-done.6), channel_id=1, source_target_pairs={{0,2},{1,3},{2,0},{3,1},{4,6},{5,7},{6,4},{7,5},{8,10},{9,11},{10,... | collective-permute-start | bytes 196616 | tf_op jit(solution)/shard_map/ppermute | solution.py:277
  19.8 1.2 %collective-permute-start.12 = (bf16[8,4096]{1,0:T(8,128)(2,1)S(1)}, bf16[8,4096]{1,0:T(8,128)(2,1)S(1)}, u32[]{:S(2)}, u32[]{:S(2)}) collective-permute-start(bf16[8,4096]{1,0:T(8,128)(2,1)S(1)} %collective-permute-done.8), channel_id=1, source_target_pairs={{0,2},{1,3},{2,0},{3,1},{4,6},{5,7},{6,4},{7,5},{8,10},{9,11},{10,... | collective-permute-start | bytes 196616 | tf_op jit(solution)/shard_map/ppermute | solution.py:277
  21.0 0.8 %collective-permute-start.11 = (bf16[8,4096]{1,0:T(8,128)(2,1)S(1)}, bf16[8,4096]{1,0:T(8,128)(2,1)S(1)}, u32[]{:S(2)}, u32[]{:S(2)}) collective-permute-start(bf16[8,4096]{1,0:T(8,128)(2,1)S(1)} %collective-permute-done.7), channel_id=1, source_target_pairs={{0,2},{1,3},{2,0},{3,1},{4,6},{5,7},{6,4},{7,5},{8,10},{9,11},{10,... | collective-permute-start | bytes 196616 | tf_op jit(solution)/shard_map/ppermute | solution.py:277
  22.0 1.0 %collective-permute-done.10 = bf16[8,4096]{1,0:T(8,128)(2,1)S(1)} collective-permute-done((bf16[8,4096]{1,0:T(8,128)(2,1)S(1)}, bf16[8,4096]{1,0:T(8,128)(2,1)S(1)}, u32[]{:S(2)}, u32[]{:S(2)}) %collective-permute-start.10) | collective-permute-done | bytes 65568 | tf_op jit(solution)/shard_map/ppermute | solution.py:277
  23.0 1.1 %collective-permute-done.12 = bf16[8,4096]{1,0:T(8,128)(2,1)S(1)} collective-permute-done((bf16[8,4096]{1,0:T(8,128)(2,1)S(1)}, bf16[8,4096]{1,0:T(8,128)(2,1)S(1)}, u32[]{:S(2)}, u32[]{:S(2)}) %collective-permute-start.12) | collective-permute-done | bytes 65568 | tf_op jit(solution)/shard_map/ppermute | solution.py:277
  24.1 1.2 %collective-permute-done.11 = bf16[8,4096]{1,0:T(8,128)(2,1)S(1)} collective-permute-done((bf16[8,4096]{1,0:T(8,128)(2,1)S(1)}, bf16[8,4096]{1,0:T(8,128)(2,1)S(1)}, u32[]{:S(2)}, u32[]{:S(2)}) %collective-permute-start.11) | collective-permute-done | bytes 65568 | tf_op jit(solution)/shard_map/ppermute | solution.py:277
  25.4 2.2 %shard_map.86.refs_5_ = bf16[4096,512]{1,0:T(8,128)(2,1)S(1)} custom-call(s32[1]{0:T(128)} %bitcast.me_ref.after_ref.refs_0_, bf16[4096,512]{1,0:T(8,128)(2,1)} %source.1), custom_call_target="tpu_custom_call" | custom-call | bytes 8388608 | tf_op jit(solution)/shard_map/pallas_call | solution.py:78
  27.6 1.7 %shard_map.87 = (f32[128,512]{1,0:T(8,128)S(1)}, f32[128,512]{1,0:T(8,128)S(1)}, f32[16,8,128]{2,1,0:T(8,128)S(1)}) custom-call(s32[1]{0:T(128)} %bitcast.me_ref.after_ref.refs_0_, bf16[128,128]{1,0:T(8,128)(2,1)S(1)} %get-tuple-element.24.pick_ref, f32[128,128]{1,0:T(8,128)S(1)} %get-tuple-element.23.label_ref.refs_1_, ...), custom_call_target="tpu_custom_call" | custom-call | flops 1073741824 | bytes 10485760 | tf_op jit(solution)/shard_map/pallas_call | solution.py:156
  29.3 10.3 %all_to_all.5.refs_2_ = f32[16,8,128]{2,1,0:T(8,128)S(1)} all-to-all(f32[16,8,128]{2,1,0:T(8,128)S(1)} %get-tuple-element.28), channel_id=1, replica_groups=mesh['groups'=2,'dp'=16] {'dp'}, dimensions={0} | all-to-all | bytes 131072 | tf_op jit(solution)/shard_map/all_to_all | solution.py:340
  39.6 1.6 %shard_map.88 = (f32[64,4096]{1,0:T(8,128)S(1)}, bf16[64,4096]{1,0:T(8,128)(2,1)S(1)}, bf16[128,512]{1,0:T(8,128)(2,1)S(1)}, f32[1,128]{1,0:T(1,128)S(1)}) custom-call(s32[1]{0:T(128)} %bitcast.me_ref.after_ref.refs_0_, f32[128,128]{1,0:T(8,128)S(1)} %get-tuple-element.23.label_ref.refs_1_, f32[16,8,128]{2,1,0:T(8,128)S(1)} %all_to_all.5.refs_2_, ...), custom_call_target="tpu_custom_call" | custom-call | flops 536870912 | bytes 6291456 | tf_op jit(solution)/shard_map/pallas_call | solution.py:232
  41.2 1.9 %collective-permute-done.15 = bf16[64,4096]{1,0:T(8,128)(2,1)S(1)} collective-permute-done((bf16[64,4096]{1,0:T(8,128)(2,1)S(1)}, bf16[64,4096]{1,0:T(8,128)(2,1)S(1)}, u32[]{:S(2)}, u32[]{:S(2)}) %collective-permute-start.15) | collective-permute-done | bytes 524320 | tf_op jit(solution)/shard_map/ppermute | solution.py:277
  43.5 2.6 %shard_map.89.refs_5_ = bf16[4096,512]{1,0:T(8,128)(2,1)} custom-call(bf16[32,8192]{1,0:T(8,128)(2,1)S(1)} %pad_maximum_fusion.refs_0_, bf16[32,8192]{1,0:T(8,128)(2,1)S(1)} %maximum_maximum_fusion.refs_1_, bf16[32,8192]{1,0:T(8,128)(2,1)S(1)} %collective-permute-done.13.refs_2_, bf16[32,8192]{1,0:T(8,128)(2,1)S(1)} %collective-permute-done.14.refs_3_, ...), custom_call_target="tpu_custom_call" | custom-call | flops 268435456 | bytes 2621440 | tf_op jit(solution)/shard_map/pallas_call | solution.py:258
  46.2 1.9 %collective-permute-start.16 = (bf16[16,4096]{1,0:T(8,128)(2,1)S(1)}, bf16[16,4096]{1,0:T(8,128)(2,1)S(1)}, u32[]{:S(2)}, u32[]{:S(2)}) collective-permute-start(bf16[16,4096]{1,0:T(8,128)(2,1)S(1)} %get-tuple-element.38), channel_id=1, source_target_pairs={{0,2},{1,3},{2,0},{3,1},{4,6},{5,7},{6,4},{7,5},{8,10},{9,11},{10,... | collective-permute-start | bytes 393224 | tf_op jit(solution)/shard_map/ppermute | solution.py:277
  48.1 1.0 %collective-permute-done.17 = bf16[16,4096]{1,0:T(8,128)(2,1)S(1)} collective-permute-done((bf16[16,4096]{1,0:T(8,128)(2,1)S(1)}, bf16[16,4096]{1,0:T(8,128)(2,1)S(1)}, u32[]{:S(2)}, u32[]{:S(2)}) %collective-permute-start.17) | collective-permute-done | bytes 131104 | tf_op jit(solution)/shard_map/ppermute | solution.py:277
  49.3 2.3 %collective-permute-start.19 = (bf16[8,4096]{1,0:T(8,128)(2,1)S(1)}, bf16[8,4096]{1,0:T(8,128)(2,1)S(1)}, u32[]{:S(2)}, u32[]{:S(2)}) collective-permute-start(bf16[8,4096]{1,0:T(8,128)(2,1)S(1)} %get-tuple-element.50), channel_id=1, source_target_pairs={{0,12},{1,13},{2,14},{3,15},{4,8},{5,9},{6,10},{7,11},{8,4},{9,5},... | collective-permute-start | bytes 196616 | tf_op jit(solution)/shard_map/ppermute | solution.py:277
  51.6 2.6 %shard_map.90 = bf16[4096,512]{1,0:T(8,128)(2,1)} custom-call(bf16[32,8192]{1,0:T(8,128)(2,1)S(1)} %pad_maximum_fusion.refs_0_, bf16[32,8192]{1,0:T(8,128)(2,1)S(1)} %maximum_maximum_fusion.refs_1_, bf16[32,8192]{1,0:T(8,128)(2,1)S(1)} %collective-permute-done.13.refs_2_, ...), custom_call_target="tpu_custom_call", output_to_operand_aliasing={{}: (5, {})} | custom-call | flops 268435456 | bytes 2621440 | tf_op jit(solution)/shard_map/pallas_call | solution.py:258
  54.2 1.2 %collective-permute-start.20 = (bf16[8,4096]{1,0:T(8,128)(2,1)S(1)}, bf16[8,4096]{1,0:T(8,128)(2,1)S(1)}, u32[]{:S(2)}, u32[]{:S(2)}) collective-permute-start(bf16[8,4096]{1,0:T(8,128)(2,1)S(1)} %slice.54), channel_id=1, source_target_pairs={{0,4},{1,5},{2,6},{3,7},{4,0},{5,1},{6,2},{7,3},{8,12},{9,13},{10,... | collective-permute-start | bytes 196616 | tf_op jit(solution)/shard_map/ppermute | solution.py:277
  55.4 0.5 slice_bitcast_fusion
  55.9 0.5 collective-permute-done.18
  56.5 2.1 %collective-permute-done.20 = bf16[8,4096]{1,0:T(8,128)(2,1)S(1)} collective-permute-done((bf16[8,4096]{1,0:T(8,128)(2,1)S(1)}, bf16[8,4096]{1,0:T(8,128)(2,1)S(1)}, u32[]{:S(2)}, u32[]{:S(2)}) %collective-permute-start.20) | collective-permute-done | bytes 65568 | tf_op jit(solution)/shard_map/ppermute | solution.py:277
  58.6 0.7 %fusion.1 = f32[8,4096]{1,0:T(8,128)} fusion(f32[16,4096]{1,0:T(8,128)S(1)} %convert_add_fusion.1, bf16[8,4096]{1,0:T(8,128)(2,1)S(1)} %collective-permute-done.20, bf16[8,4096]{1,0:T(8,128)(2,1)S(1)} %collective-permute-done.19, bf16[8,4096]{1,0:T(8,128)(2,1)S(1)} %collective-permute-done.18), kind=kLoop, calls=%fused_computation.8 | loop fusion | flops 196608 | bytes 458752 | tf_op jit(solution)/shard_map/add | solution.py:321
  (34 shorter events, 1.4 us)
Async XLA Ops:
  0.6 21.2 %copy-start = (bf16[8,4096]{1,0:T(8,128)(2,1)S(1)}, bf16[8,4096]{1,0:T(8,128)(2,1)}, u32[]{:S(2)}) copy-start(bf16[8,4096]{1,0:T(8,128)(2,1)} %param.6) | copy-start | bytes 196612
  0.6 21.2 %copy-start.1 = (bf16[8,4096]{1,0:T(8,128)(2,1)S(1)}, bf16[8,4096]{1,0:T(8,128)(2,1)}, u32[]{:S(2)}) copy-start(bf16[8,4096]{1,0:T(8,128)(2,1)} %param.7) | copy-start | bytes 196612
  0.6 8.0 %collective-permute-start = (bf16[8,4096]{1,0:T(8,128)(2,1)}, bf16[8,4096]{1,0:T(8,128)(2,1)S(1)}, u32[]{:S(2)}, u32[]{:S(2)}) collective-permute-start(bf16[8,4096]{1,0:T(8,128)(2,1)} %param.6), channel_id=1, source_target_pairs={{0,4},{1,5},{2,6},{3,7},{4,0},{5,1},{6,2},{7,3},{8,12},{9,13},{10,... | collective-permute-start | bytes 196616 | tf_op jit(solution)/shard_map/ppermute | solution.py:277
  3.7 11.7 %collective-permute-start.5 = (bf16[8,4096]{1,0:T(8,128)(2,1)}, bf16[8,4096]{1,0:T(8,128)(2,1)S(1)}, u32[]{:S(2)}, u32[]{:S(2)}) collective-permute-start(bf16[8,4096]{1,0:T(8,128)(2,1)} %param.6), channel_id=1, source_target_pairs={{0,8},{1,9},{2,10},{3,11},{4,12},{5,13},{6,14},{7,15},{8,0},{9,1},... | collective-permute-start | bytes 196616 | tf_op jit(solution)/shard_map/ppermute | solution.py:277
  6.3 9.1 %collective-permute-start.2 = (bf16[8,4096]{1,0:T(8,128)(2,1)}, bf16[8,4096]{1,0:T(8,128)(2,1)S(1)}, u32[]{:S(2)}, u32[]{:S(2)}) collective-permute-start(bf16[8,4096]{1,0:T(8,128)(2,1)} %param.6), channel_id=1, source_target_pairs={{0,2},{1,3},{2,0},{3,1},{4,6},{5,7},{6,4},{7,5},{8,10},{9,11},{10,... | collective-permute-start | bytes 196616 | tf_op jit(solution)/shard_map/ppermute | solution.py:277
  7.8 4.5 %collective-permute-start.1 = (bf16[8,4096]{1,0:T(8,128)(2,1)}, bf16[8,4096]{1,0:T(8,128)(2,1)S(1)}, u32[]{:S(2)}, u32[]{:S(2)}) collective-permute-start(bf16[8,4096]{1,0:T(8,128)(2,1)} %param.7), channel_id=1, source_target_pairs={{0,4},{1,5},{2,6},{3,7},{4,0},{5,1},{6,2},{7,3},{8,12},{9,13},{10,... | collective-permute-start | bytes 196616 | tf_op jit(solution)/shard_map/ppermute | solution.py:277
  8.3 7.2 %collective-permute-start.6 = (bf16[8,4096]{1,0:T(8,128)(2,1)}, bf16[8,4096]{1,0:T(8,128)(2,1)S(1)}, u32[]{:S(2)}, u32[]{:S(2)}) collective-permute-start(bf16[8,4096]{1,0:T(8,128)(2,1)} %param.7), channel_id=1, source_target_pairs={{0,8},{1,9},{2,10},{3,11},{4,12},{5,13},{6,14},{7,15},{8,0},{9,1},... | collective-permute-start | bytes 196616 | tf_op jit(solution)/shard_map/ppermute | solution.py:277
  8.6 6.8 %collective-permute-start.3 = (bf16[8,4096]{1,0:T(8,128)(2,1)}, bf16[8,4096]{1,0:T(8,128)(2,1)S(1)}, u32[]{:S(2)}, u32[]{:S(2)}) collective-permute-start(bf16[8,4096]{1,0:T(8,128)(2,1)} %param.7), channel_id=1, source_target_pairs={{0,2},{1,3},{2,0},{3,1},{4,6},{5,7},{6,4},{7,5},{8,10},{9,11},{10,... | collective-permute-start | bytes 196616 | tf_op jit(solution)/shard_map/ppermute | solution.py:277
  12.3 9.5 %collective-permute-start.4 = (bf16[8,8192]{1,0:T(8,128)(2,1)S(1)}, bf16[8,8192]{1,0:T(8,128)(2,1)S(1)}, u32[]{:S(2)}, u32[]{:S(2)}) collective-permute-start(bf16[8,8192]{1,0:T(8,128)(2,1)S(1)} %constant_dynamic-update-slice_fusion), channel_id=1, source_target_pairs={{0,2},{1,3},{2,0},{3,1},{4,6},{5,7},{6,4},{7,5},{8,10},{9,11},{10,... | collective-permute-start | bytes 393224 | tf_op jit(solution)/shard_map/ppermute | solution.py:277
  15.5 4.3 %collective-permute-start.8 = (bf16[8,4096]{1,0:T(8,128)(2,1)S(1)}, bf16[8,4096]{1,0:T(8,128)(2,1)S(1)}, u32[]{:S(2)}, u32[]{:S(2)}) collective-permute-start(bf16[8,4096]{1,0:T(8,128)(2,1)S(1)} %collective-permute-done.6), channel_id=1, source_target_pairs={{0,4},{1,5},{2,6},{3,7},{4,0},{5,1},{6,2},{7,3},{8,12},{9,13},{10,... | collective-permute-start | bytes 196616 | tf_op jit(solution)/shard_map/ppermute | solution.py:277
  16.1 4.9 %collective-permute-start.7 = (bf16[8,4096]{1,0:T(8,128)(2,1)S(1)}, bf16[8,4096]{1,0:T(8,128)(2,1)S(1)}, u32[]{:S(2)}, u32[]{:S(2)}) collective-permute-start(bf16[8,4096]{1,0:T(8,128)(2,1)S(1)} %collective-permute-done.5), channel_id=1, source_target_pairs={{0,4},{1,5},{2,6},{3,7},{4,0},{5,1},{6,2},{7,3},{8,12},{9,13},{10,... | collective-permute-start | bytes 196616 | tf_op jit(solution)/shard_map/ppermute | solution.py:277
  17.6 5.5 %collective-permute-start.9 = (bf16[8,4096]{1,0:T(8,128)(2,1)S(1)}, bf16[8,4096]{1,0:T(8,128)(2,1)S(1)}, u32[]{:S(2)}, u32[]{:S(2)}) collective-permute-start(bf16[8,4096]{1,0:T(8,128)(2,1)S(1)} %collective-permute-done.5), channel_id=1, source_target_pairs={{0,2},{1,3},{2,0},{3,1},{4,6},{5,7},{6,4},{7,5},{8,10},{9,11},{10,... | collective-permute-start | bytes 196616 | tf_op jit(solution)/shard_map/ppermute | solution.py:277
  18.8 4.3 %collective-permute-start.10 = (bf16[8,4096]{1,0:T(8,128)(2,1)S(1)}, bf16[8,4096]{1,0:T(8,128)(2,1)S(1)}, u32[]{:S(2)}, u32[]{:S(2)}) collective-permute-start(bf16[8,4096]{1,0:T(8,128)(2,1)S(1)} %collective-permute-done.6), channel_id=1, source_target_pairs={{0,2},{1,3},{2,0},{3,1},{4,6},{5,7},{6,4},{7,5},{8,10},{9,11},{10,... | collective-permute-start | bytes 196616 | tf_op jit(solution)/shard_map/ppermute | solution.py:277
  19.8 4.3 %collective-permute-start.12 = (bf16[8,4096]{1,0:T(8,128)(2,1)S(1)}, bf16[8,4096]{1,0:T(8,128)(2,1)S(1)}, u32[]{:S(2)}, u32[]{:S(2)}) collective-permute-start(bf16[8,4096]{1,0:T(8,128)(2,1)S(1)} %collective-permute-done.8), channel_id=1, source_target_pairs={{0,2},{1,3},{2,0},{3,1},{4,6},{5,7},{6,4},{7,5},{8,10},{9,11},{10,... | collective-permute-start | bytes 196616 | tf_op jit(solution)/shard_map/ppermute | solution.py:277
  21.0 4.3 %collective-permute-start.11 = (bf16[8,4096]{1,0:T(8,128)(2,1)S(1)}, bf16[8,4096]{1,0:T(8,128)(2,1)S(1)}, u32[]{:S(2)}, u32[]{:S(2)}) collective-permute-start(bf16[8,4096]{1,0:T(8,128)(2,1)S(1)} %collective-permute-done.7), channel_id=1, source_target_pairs={{0,2},{1,3},{2,0},{3,1},{4,6},{5,7},{6,4},{7,5},{8,10},{9,11},{10,... | collective-permute-start | bytes 196616 | tf_op jit(solution)/shard_map/ppermute | solution.py:277
  21.9 5.7 %collective-permute-start.13 = (bf16[32,8192]{1,0:T(8,128)(2,1)S(1)}, bf16[32,8192]{1,0:T(8,128)(2,1)S(1)}, u32[]{:S(2)}, u32[]{:S(2)}) collective-permute-start(bf16[32,8192]{1,0:T(8,128)(2,1)S(1)} %pad_maximum_fusion.refs_0_), channel_id=1, source_target_pairs={{0,1},{1,0},{2,3},{3,2},{4,5},{5,4},{6,7},{7,6},{8,9},{9,8},{10,11... | collective-permute-start | bytes 1572872 | tf_op jit(solution)/shard_map/ppermute | solution.py:277
  25.3 2.3 %collective-permute-start.14 = (bf16[32,8192]{1,0:T(8,128)(2,1)S(1)}, bf16[32,8192]{1,0:T(8,128)(2,1)S(1)}, u32[]{:S(2)}, u32[]{:S(2)}) collective-permute-start(bf16[32,8192]{1,0:T(8,128)(2,1)S(1)} %maximum_maximum_fusion.refs_1_), channel_id=1, source_target_pairs={{0,1},{1,0},{2,3},{3,2},{4,5},{5,4},{6,7},{7,6},{8,9},{9,8},{10,11... | collective-permute-start | bytes 1572872 | tf_op jit(solution)/shard_map/ppermute | solution.py:277
  41.1 2.0 %collective-permute-start.15 = (bf16[64,4096]{1,0:T(8,128)(2,1)S(1)}, bf16[64,4096]{1,0:T(8,128)(2,1)S(1)}, u32[]{:S(2)}, u32[]{:S(2)}) collective-permute-start(bf16[64,4096]{1,0:T(8,128)(2,1)S(1)} %get-tuple-element.33), channel_id=1, source_target_pairs={{0,1},{1,0},{2,3},{3,2},{4,5},{5,4},{6,7},{7,6},{8,9},{9,8},{10,11... | collective-permute-start | bytes 1572872 | tf_op jit(solution)/shard_map/ppermute | solution.py:277
  43.4 5.7 %collective-permute-start.17 = (bf16[16,4096]{1,0:T(8,128)(2,1)S(1)}, bf16[16,4096]{1,0:T(8,128)(2,1)S(1)}, u32[]{:S(2)}, u32[]{:S(2)}) collective-permute-start(bf16[16,4096]{1,0:T(8,128)(2,1)S(1)} %get-tuple-element.39), channel_id=1, source_target_pairs={{0,2},{1,3},{2,0},{3,1},{4,6},{5,7},{6,4},{7,5},{8,10},{9,11},{10,... | collective-permute-start | bytes 393224 | tf_op jit(solution)/shard_map/ppermute | solution.py:277
  46.2 8.0 %collective-permute-start.16 = (bf16[16,4096]{1,0:T(8,128)(2,1)S(1)}, bf16[16,4096]{1,0:T(8,128)(2,1)S(1)}, u32[]{:S(2)}, u32[]{:S(2)}) collective-permute-start(bf16[16,4096]{1,0:T(8,128)(2,1)S(1)} %get-tuple-element.38), channel_id=1, source_target_pairs={{0,2},{1,3},{2,0},{3,1},{4,6},{5,7},{6,4},{7,5},{8,10},{9,11},{10,... | collective-permute-start | bytes 393224 | tf_op jit(solution)/shard_map/ppermute | solution.py:277
  49.1 7.4 %collective-permute-start.18 = (bf16[8,4096]{1,0:T(8,128)(2,1)S(1)}, bf16[8,4096]{1,0:T(8,128)(2,1)S(1)}, u32[]{:S(2)}, u32[]{:S(2)}) collective-permute-start(bf16[8,4096]{1,0:T(8,128)(2,1)S(1)} %get-tuple-element.49), channel_id=1, source_target_pairs={{0,8},{1,9},{2,10},{3,11},{4,12},{5,13},{6,14},{7,15},{8,0},{9,1},... | collective-permute-start | bytes 196616 | tf_op jit(solution)/shard_map/ppermute | solution.py:277
  49.3 7.2 %collective-permute-start.19 = (bf16[8,4096]{1,0:T(8,128)(2,1)S(1)}, bf16[8,4096]{1,0:T(8,128)(2,1)S(1)}, u32[]{:S(2)}, u32[]{:S(2)}) collective-permute-start(bf16[8,4096]{1,0:T(8,128)(2,1)S(1)} %get-tuple-element.50), channel_id=1, source_target_pairs={{0,12},{1,13},{2,14},{3,15},{4,8},{5,9},{6,10},{7,11},{8,4},{9,5},... | collective-permute-start | bytes 196616 | tf_op jit(solution)/shard_map/ppermute | solution.py:277
  54.2 4.3 %collective-permute-start.20 = (bf16[8,4096]{1,0:T(8,128)(2,1)S(1)}, bf16[8,4096]{1,0:T(8,128)(2,1)S(1)}, u32[]{:S(2)}, u32[]{:S(2)}) collective-permute-start(bf16[8,4096]{1,0:T(8,128)(2,1)S(1)} %slice.54), channel_id=1, source_target_pairs={{0,4},{1,5},{2,6},{3,7},{4,0},{5,1},{6,2},{7,3},{8,12},{9,13},{10,... | collective-permute-start | bytes 196616 | tf_op jit(solution)/shard_map/ppermute | solution.py:277

commit v4 on v2

--- a/solution.py
+++ b/solution.py
@@ -11,18 +11,13 @@
 STATS = 8
 
 
-def xor_order(n):
-    return (0, 4, 2, 6, 8, 12, 10, 14, 1, 5, 3, 7, 9, 13, 11, 15) if n == 16 else None
-
-
 def held_rows(shape, dim, me, rows_local, tuned):
     held = lax.broadcasted_iota(jnp.int32, shape, dim)
     if not tuned:
         return held
     step = rows_local.bit_length() - 1
     block = lax.shift_right_logical(held, step)
-    bit = lambda k: lax.shift_right_logical(block, k) & 1
-    distance = bit(3) + bit(2) * 8 + bit(1) * 2 + bit(0) * 4
+    distance = (block & 7) * 2 + lax.shift_right_logical(block, 3)
     return (me ^ distance) * rows_local + (held & (rows_local - 1))
 
 
@@ -31,29 +26,34 @@
 
 
 def prepare_kernel(
-    rows_local, tuned, me_ref, order_ref, labels_ref, teacher_ref, student_ref, teacher_out, student_out, pick_out, label_out, sems
+    rows_local, tuned, me_ref, order_ref, labels_ref, *refs
 ):
-    copies = []
-    pieces = sems.shape[1]
-    rows = teacher_ref.shape[0] // pieces
-    for k in range(pieces):
-        for j, (source, target) in enumerate(((teacher_ref, teacher_out), (student_ref, student_out))):
-            part = pl.ds(k * rows, rows)
-            copies.append(pltpu.make_async_copy(source.at[part], target.at[part], sems.at[j, k]))
-    for copy in copies:
+    sources, targets = refs[:2], refs[2:4]
+    pick_out, label_out, ids, id_sems, sems = refs[4:]
+    id_copies = [
+        pltpu.make_async_copy(source, ids.at[j], id_sems.at[j]) for j, source in enumerate((order_ref, labels_ref))
+    ]
+    copies = [pltpu.make_async_copy(source, target, sems.at[j]) for j, (source, target) in enumerate(zip(sources, targets))]
+    for copy in id_copies + copies:
         copy.start()
     me = me_ref[0]
     count = order_ref.shape[1]
-    vocab = teacher_ref.shape[1]
+    vocab = sources[0].shape[1]
     lanes = lax.broadcasted_iota(jnp.int32, (count, count), 1)
     is_row = held_rows((count, count), 0, me, rows_local, tuned) == lanes
-    wanted = to_column(is_row, order_ref[...].astype(jnp.float32))
     have = held_rows((count, count), 1, me, rows_local, tuned).astype(jnp.float32)
+    for copy in id_copies:
+        copy.wait()
+    wanted = to_column(is_row, ids[0].astype(jnp.float32))
     pick_out[...] = jnp.where(wanted == have, 1.0, 0.0).astype(jnp.bfloat16)
-    label = to_column(is_row, labels_ref[...].astype(jnp.float32)) - (me * vocab).astype(jnp.float32)
+    label = to_column(is_row, ids[1].astype(jnp.float32)) - (me * vocab).astype(jnp.float32)
     label_out[...] = jnp.broadcast_to(label, label_out.shape)
     for copy in copies:
         copy.wait()
+
+
+def stay(value):
+    return pltpu.with_memory_space_constraint(value, pltpu.HBM)
 
 
 def prepare(me, order, labels, heads, rows_local, tuned):
@@ -62,7 +62,7 @@
     hbm = pl.BlockSpec(memory_space=pltpu.HBM)
     return pl.pallas_call(
         functools.partial(prepare_kernel, rows_local, tuned),
-        in_specs=[pl.BlockSpec(memory_space=pltpu.SMEM), vmem, vmem, hbm, hbm],
+        in_specs=[pl.BlockSpec(memory_space=pltpu.SMEM)] + [hbm] * 4,
         out_specs=(vmem,) * 4,
         out_shape=(
             jax.ShapeDtypeStruct(heads[0].shape, heads[0].dtype),
@@ -70,10 +70,14 @@
             jax.ShapeDtypeStruct((count, count), jnp.bfloat16),
             jax.ShapeDtypeStruct((count, 128), jnp.float32),
         ),
-        scratch_shapes=[pltpu.SemaphoreType.DMA((2, 4))],
+        scratch_shapes=[
+            pltpu.VMEM((2, 1, count), jnp.int32),
+            pltpu.SemaphoreType.DMA((2,)),
+            pltpu.SemaphoreType.DMA((2,)),
+        ],
         compiler_params=pltpu.CompilerParams(vmem_limit_bytes=24 * 2**20),
-        cost_estimate=pl.CostEstimate(flops=0, bytes_accessed=2 * heads[0].size * 4, transcendentals=0),
-    )(me, order[None], labels[None], *(pltpu.with_memory_space_constraint(head, pltpu.HBM) for head in heads))
+        cost_estimate=pl.CostEstimate(flops=0, bytes_accessed=heads[0].size * 8, transcendentals=0),
+    )(me, stay(order[None]), stay(labels[None]), *map(stay, heads))
 
 
 def logits_kernel(rows_local, tuned, parts, me_ref, pick_ref, label_ref, *refs):
@@ -137,7 +141,7 @@
 
 
 def grad_kernel(
-    rows_local, tuned, me_ref, label_ref, stats_ref, teacher_ref, student_ref, head_ref, keep_out, send_out, grad_out, loss_out
+    rows_local, tuned, me_ref, label_ref, stats_ref, teacher_ref, student_ref, head_ref, keep_out, near_out, far_out, grad_out, loss_out
 ):
     me = me_ref[0]
     count, vocab = student_ref.shape
@@ -176,8 +180,10 @@
             grad, head_ref[k : k + step], (((1,), (1,)), ((), ())), preferred_element_type=jnp.float32
         )
         keep_out[:, k : k + step] = part[:kept]
-        if send_out is not None:
-            send_out[:, k : k + step] = part[kept:].astype(jnp.bfloat16)
+        if kept < count:
+            half = kept // 2
+            near_out[:, k : k + step] = part[kept : kept + half].astype(jnp.bfloat16)
+            far_out[:, k : k + step] = part[kept + half :].astype(jnp.bfloat16)
 
 
 def gradient(me, label, stats, teacher_logits, student_logits, head, rows_local, tuned):
@@ -187,14 +193,14 @@
     vmem = pl.BlockSpec(memory_space=pltpu.VMEM)
     shapes = [jax.ShapeDtypeStruct((kept, depth), jnp.float32)]
     if tuned:
-        shapes.append(jax.ShapeDtypeStruct((count - kept, depth), jnp.bfloat16))
+        shapes += [jax.ShapeDtypeStruct(((count - kept) // 2, depth), jnp.bfloat16)] * 2
     shapes += [jax.ShapeDtypeStruct((count, vocab), jnp.bfloat16), jax.ShapeDtypeStruct((1, count), jnp.float32)]
 
     def kernel(*refs):
         if tuned:
             grad_kernel(rows_local, tuned, *refs)
         else:
-            grad_kernel(rows_local, tuned, *refs[:7], None, *refs[7:])
+            grad_kernel(rows_local, tuned, *refs[:7], None, None, *refs[7:])
 
     return pl.pallas_call(
         kernel,
@@ -209,25 +215,34 @@
 
 
 def head_kernel(parts, *refs):
-    rows = jnp.concatenate([piece[...] for piece in refs[:parts]], axis=0)
-    grad_ref, out_ref = refs[parts:]
-    out_ref[...] = lax.dot_general(
-        rows, grad_ref[...], (((0,), (0,)), ((), ())), preferred_element_type=jnp.float32
-    ).astype(jnp.bfloat16)
+    grad_ref, out_ref, held, sems = refs[parts:]
+    steps, step, _ = held.shape
+    copies = []
+    for k in range(steps):
+        first = (steps + k) * step
+        rows = jnp.concatenate([piece[:, first : first + step] for piece in refs[:parts]], axis=0)
+        held[k] = lax.dot_general(
+            rows, grad_ref[...], (((0,), (0,)), ((), ())), preferred_element_type=jnp.float32
+        ).astype(jnp.bfloat16)
+        copies.append(pltpu.make_async_copy(held.at[k], out_ref.at[pl.ds(k * step, step)], sems.at[k]))
+        copies[-1].start()
+    for copy in copies:
+        copy.wait()
 
 
 def head_gradient(hidden, logit_grad, depth):
     count, vocab = logit_grad.shape
-    step = min(512, depth)
-    first = depth // step
+    step = min(256, depth)
     return pl.pallas_call(
         functools.partial(head_kernel, len(hidden)),
-        grid=(depth // step,),
-        in_specs=[pl.BlockSpec((piece.shape[0], step), lambda k: (0, k + first)) for piece in hidden]
-        + [pl.BlockSpec((count, vocab), lambda k: (0, 0))],
-        out_specs=pl.BlockSpec((step, vocab), lambda k: (k, 0)),
+        in_specs=[pl.BlockSpec(memory_space=pltpu.VMEM)] * (len(hidden) + 1),
+        out_specs=pl.BlockSpec(memory_space=pltpu.HBM),
         out_shape=jax.ShapeDtypeStruct((depth, vocab), jnp.bfloat16),
-        compiler_params=pltpu.CompilerParams(vmem_limit_bytes=40 * 2**20),
+        scratch_shapes=[
+            pltpu.VMEM((depth // step, step, vocab), jnp.bfloat16),
+            pltpu.SemaphoreType.DMA((depth // step,)),
+        ],
+        compiler_params=pltpu.CompilerParams(vmem_limit_bytes=24 * 2**20),
         cost_estimate=pl.CostEstimate(
             flops=2 * count * depth * vocab, bytes_accessed=2 * depth * (vocab + count), transcendentals=0
         ),
@@ -242,53 +257,96 @@
     return lax.optimization_barrier((value, *done))[0]
 
 
-def gather_rows(teacher_rows, student_rows, n, prepared):
-    far = jnp.concatenate([after(swap(teacher_rows, 8, n), *prepared), swap(student_rows, 8, n)], axis=1)
-    rows = jnp.concatenate([teacher_rows, student_rows], axis=1)
-    side = swap(rows, 2, n)
-    near = swap(rows, 4, n)
+def join_kernel(teacher_ref, student_ref, out_ref, sems):
+    depth = teacher_ref.shape[1]
+    copies = [
+        pltpu.make_async_copy(ref, out_ref.at[:, pl.ds(j * depth, depth)], sems.at[j])
+        for j, ref in enumerate((teacher_ref, student_ref))
+    ]
+    for copy in copies:
+        copy.start()
+    for copy in copies:
+        copy.wait()
+
+
+def join_rows(teacher_rows, student_rows):
+    count, depth = teacher_rows.shape
+    return pl.pallas_call(
+        join_kernel,
+        in_specs=[pl.BlockSpec(memory_space=pltpu.HBM)] * 2,
+        out_specs=pl.BlockSpec(memory_space=pltpu.VMEM),
+        out_shape=jax.ShapeDtypeStruct((count, 2 * depth), teacher_rows.dtype),
+        scratch_shapes=[pltpu.SemaphoreType.DMA((2,))],
+        compiler_params=pltpu.CompilerParams(vmem_limit_bytes=2**20),
+        cost_estimate=pl.CostEstimate(flops=0, bytes_accessed=8 * count * depth, transcendentals=0),
+    )(stay(teacher_rows), stay(student_rows))
+
+
+def gather_rows(teacher_rows, student_rows, n, fetch):
+    join = lambda pair: jnp.concatenate(pair, axis=1)
+    stack = lambda *parts: jnp.concatenate(parts, axis=0)
+    far = join((swap(teacher_rows, 8, n), swap(student_rows, 8, n)))
+    rows = join_rows(teacher_rows, student_rows)
+    near, side = swap(rows, 4, n), swap(rows, 2, n)
+    fetched = fetch(rows)
+    far = after(far, *fetched)
     far_near = swap(far, 4, n)
     near_side = swap(near, 2, n)
     far_side = swap(far, 2, n)
     far_near_side = swap(far_near, 2, n)
-    first = jnp.concatenate([rows, near, side, near_side], axis=0)
-    second = jnp.concatenate([far, far_near, far_side, far_near_side], axis=0)
-    return [first, second, swap(first, 1, n), swap(second, 1, n)]
-
-
-def scatter_rows(keep, send, rows_local, n, grad_head):
+    held = [stack(rows, side, near, near_side), stack(far, far_side, far_near, far_near_side)]
+    return held + [swap(piece, 1, n) for piece in held], fetched
+
+
+def scatter_rows(keep, sends, logit_grad, rows_local, n, head_gradient_of):
     low = jnp.bfloat16
     full = jnp.float32
-    held = keep + swap(send, 1, n).astype(full)
-    quarter = 2 * rows_local
-    near_keep, near_send, far_keep, far_send = (held[k * quarter : (k + 1) * quarter] for k in range(4))
-    far_part = after(swap(far_send.astype(low), 2, n), grad_head)
-    far = (far_keep + far_part.astype(full)).astype(low)
-    near = near_keep + swap(near_send.astype(low), 2, n).astype(full)
+    others = [swap(send, 1, n) for send in sends[::-1]][::-1]
+
+    def split(half):
+        count = keep.shape[0] // 2
+        held = keep[half * count : (half + 1) * count] + others[half].astype(full)
+        held = held.reshape(2, 2, rows_local, -1)
+        take = lambda side: held[:, side].reshape(2 * rows_local, -1)
+        return lax.optimization_barrier((take(0), take(1).astype(low)))
+
+    far_keep, far_send = split(1)
+    far_other = swap(far_send, 2, n)
+    grad_head = head_gradient_of(after(logit_grad, others[1]))
+    others[0] = after(others[0], far_send)
+    near_keep, near_send = split(0)
+    near_other = swap(after(near_send, grad_head), 2, n)
+    far = (far_keep + far_other.astype(full)).astype(low)
     from_far = swap(far[:rows_local], 8, n)
     from_far_near = swap(far[rows_local:], 12, n)
+    near = near_keep + near_other.astype(full)
     from_near = swap(near[rows_local:].astype(low), 4, n)
-    return near[:rows_local] + from_far.astype(full) + from_far_near.astype(full) + from_near.astype(full)
+    total = near[:rows_local] + from_far.astype(full) + from_far_near.astype(full) + from_near.astype(full)
+    return total, grad_head
 
 
 def per_device(n, teacher_hidden, student_hidden, teacher_head, student_head, labels, order):
     rows_local, depth = student_hidden.shape
-    tuned = xor_order(n) is not None and rows_local == 8
+    tuned = n == 16 and rows_local == 8
     me = lax.axis_index("dp").astype(jnp.int32).reshape(1)
-    *heads, pick, label = prepare(me, order, labels, (teacher_head, student_head), rows_local, tuned)
+    heads = (teacher_head, student_head)
+    fetch = lambda *done: prepare(after(me, *done), order, labels, heads, rows_local, tuned)
     if tuned:
-        hidden = gather_rows(teacher_hidden, student_hidden, n, (*heads, pick, label))
+        hidden, fetched = gather_rows(teacher_hidden, student_hidden, n, fetch)
     else:
+        fetched = fetch(me)
         rows = jnp.concatenate([teacher_hidden, student_hidden], axis=1)
         hidden = [lax.all_gather(rows, "dp", axis=0, tiled=True)]
+    *heads, pick, label = fetched
     teacher_logits, student_logits, stats = logits(me, pick, label, hidden, heads, n, rows_local, tuned)
     stats = lax.all_to_all(stats, "dp", 0, 0)
     outs = gradient(me, label, stats, teacher_logits, student_logits, heads[1], rows_local, tuned)
     logit_grad, loss = outs[-2:]
-    grad_head = head_gradient(hidden, logit_grad, depth)
+    head_gradient_of = lambda logit_grad: head_gradient(hidden, logit_grad, depth)
     if tuned:
-        grad_hidden = scatter_rows(outs[0], outs[1], rows_local, n, grad_head)
+        grad_hidden, grad_head = scatter_rows(outs[0], outs[1:3], logit_grad, rows_local, n, head_gradient_of)
     else:
+        grad_head = head_gradient_of(logit_grad)
         grad_hidden = lax.psum_scatter(outs[0], "dp", scatter_dimension=0, tiled=True)
     return (loss[0, :rows_local], grad_hidden, grad_head)
 

time: 63.8 us -> 56.5 us (0.89)
  local copies, waits for them, and re-layouts: 3.56 us -> 0.64 us
  Pallas kernels: 11.5 us -> 10 us
  starting transfers between devices: 18.3 us -> 16.9 us
  waiting for transfers between devices: 15.5 us -> 14.7 us
    unnamed x6 -> x3, local copies, waits for them, and re-layouts: 2.16 us -> 0.03 us
    pallas_call x1 -> x2, Pallas kernels: 4.87 us -> 3.28 us  [the longest x1 2.39 us: head_gradient(): pl.pallas_call(functools.partial(head_kernel, len(hidden)), in_specs=[pl....]
    ppermute x16 -> x17, starting transfers between devices: 18.3 us -> 16.9 us  [swap(): return lax.ppermute(value, 'dp', [(i, i ^ distance) for i in range(n)])]
    concatenate x2 -> x1, local copies, waits for them, and re-layouts: 0.85 us -> 0.01 us  [gather_rows(): stack = lambda *parts: jnp.concatenate(parts, axis=0)]
    ppermute x16 -> x17, waiting for transfers between devices: 15.5 us -> 14.7 us  [swap(): return lax.ppermute(value, 'dp', [(i, i ^ distance) for i in range(n)])]
  transfers between devices with their start and end apart: 16 -> 17, of which waited for: 9 -> 12; matrix products, arithmetic and copies ran while one was open for 4% -> 2% of each run, Pallas kernels for 13% -> 12%
where the time goes in v4:
time: 56.5 us; the launch traced here: 56.3 us
  starting transfers between devices  16.9 us (30%)
  waiting for transfers between devices  14.7 us (26%)
  blocking collectives  12.3 us (22%)
  Pallas kernels  10 us (18%)
  other arithmetic  0.91 us (2%)
  between operations  0.82 us (1%)
  local copies, waits for them, and re-layouts  0.64 us (1%)
    ppermute x17, starting transfers between devices, swap(): return lax.ppermute(value, 'dp', [(i, i ^ distance) for i in range(n)])  16.9 us
    ppermute x17, waiting for transfers between devices, swap(): return lax.ppermute(value, 'dp', [(i, i ^ distance) for i in range(n)])  14.7 us
    all_to_all x1, blocking collectives, per_device(): stats = lax.all_to_all(stats, 'dp', 0, 0)  12.3 us
    pallas_call x1, Pallas kernels, prepare(): pl.pallas_call(functools.partial(prepare_kernel, rows_local, tuned), in_s...  3.53 us
    pallas_call x1, Pallas kernels, head_gradient(): pl.pallas_call(functools.partial(head_kernel, len(hidden)), in_specs=[pl....  2.39 us
    pallas_call x1, Pallas kernels, logits(): pl.pallas_call(functools.partial(logits_kernel, rows_local, tuned, len(hi...  1.61 us
    pallas_call x1, Pallas kernels, gradient(): pl.pallas_call(kernel, in_specs=[pl.BlockSpec(memory_space=pltpu.SMEM)] +...  1.58 us
  transfers between devices with their start and end apart: 17, of which 12 were waited for; matrix products, arithmetic and copies ran while one was open for 2% of the time, Pallas kernels for 12%

profile of v4, /device:TPU:0, one launch (start us, length us, event | category | flops | bytes accessed | tf_op | source)
XLA Modules:
  0.0 56.3 jit_solution(177948037304260254)
XLA Ops:
  0.6 4.1 %collective-permute-start.3 = (bf16[8,4096]{1,0:T(8,128)(2,1)}, bf16[8,4096]{1,0:T(8,128)(2,1)S(1)}, u32[]{:S(2)}, u32[]{:S(2)}) collective-permute-start(bf16[8,4096]{1,0:T(8,128)(2,1)} %teacher_ref.1), channel_id=1, source_target_pairs={{0,8},{1,9},{2,10},{3,11},{4,12},{5,13},{6,14},{7,15},{8,0},{9,1},... | collective-permute-start | bytes 196616 | tf_op jit(solution)/shard_map/ppermute | solution.py:253
  4.8 0.9 %shard_map.85 = bf16[8,8192]{1,0:T(8,128)(2,1)S(1)} custom-call(bf16[8,4096]{1,0:T(8,128)(2,1)} %teacher_ref.1, bf16[8,4096]{1,0:T(8,128)(2,1)} %student_ref.1), custom_call_target="tpu_custom_call" | custom-call | bytes 262144 | tf_op jit(solution)/shard_map/pallas_call | solution.py:274
  5.7 1.9 %collective-permute-start.1 = (bf16[8,8192]{1,0:T(8,128)(2,1)S(1)}, bf16[8,8192]{1,0:T(8,128)(2,1)S(1)}, u32[]{:S(2)}, u32[]{:S(2)}) collective-permute-start(bf16[8,8192]{1,0:T(8,128)(2,1)S(1)} %shard_map.85), channel_id=1, source_target_pairs={{0,4},{1,5},{2,6},{3,7},{4,0},{5,1},{6,2},{7,3},{8,12},{9,13},{10,... | collective-permute-start | bytes 393224 | tf_op jit(solution)/shard_map/ppermute | solution.py:253
  7.6 1.5 %collective-permute-start = (bf16[8,8192]{1,0:T(8,128)(2,1)S(1)}, bf16[8,8192]{1,0:T(8,128)(2,1)S(1)}, u32[]{:S(2)}, u32[]{:S(2)}) collective-permute-start(bf16[8,8192]{1,0:T(8,128)(2,1)S(1)} %shard_map.85), channel_id=1, source_target_pairs={{0,2},{1,3},{2,0},{3,1},{4,6},{5,7},{6,4},{7,5},{8,10},{9,11},{10,... | collective-permute-start | bytes 393224 | tf_op jit(solution)/shard_map/ppermute | solution.py:253
  9.1 3.5 %shard_map.86 = (bf16[4096,512]{1,0:T(8,128)(2,1)S(1)}, bf16[4096,512]{1,0:T(8,128)(2,1)S(1)}, bf16[128,128]{1,0:T(8,128)(2,1)S(1)}, f32[128,128]{1,0:T(8,128)S(1)}) custom-call(s32[1]{0:T(128)} %bitcast.me_ref.refs_0_, s32[1,128]{1,0:T(1,128)} %bitcast.19, s32[1,128]{1,0:T(1,128)} %bitcast.20, bf16[4096,512]{1,0:T(8,128)(2,1)} %refs_0_.1, ...), custom_call_target="tpu_custom_call" | custom-call | bytes 16777216 | tf_op jit(solution)/shard_map/pallas_call | solution.py:63
  12.7 0.5 collective-permute-start.6
  13.2 0.7 %collective-permute-start.5 = (bf16[8,8192]{1,0:T(8,128)(2,1)S(1)}, bf16[8,8192]{1,0:T(8,128)(2,1)S(1)}, u32[]{:S(2)}, u32[]{:S(2)}) collective-permute-start(bf16[8,8192]{1,0:T(8,128)(2,1)S(1)} %pad_maximum_fusion.1), channel_id=1, source_target_pairs={{0,2},{1,3},{2,0},{3,1},{4,6},{5,7},{6,4},{7,5},{8,10},{9,11},{10,... | collective-permute-start | bytes 393224 | tf_op jit(solution)/shard_map/ppermute | solution.py:253
  13.9 1.4 %collective-permute-start.2 = (bf16[8,8192]{1,0:T(8,128)(2,1)S(1)}, bf16[8,8192]{1,0:T(8,128)(2,1)S(1)}, u32[]{:S(2)}, u32[]{:S(2)}) collective-permute-start(bf16[8,8192]{1,0:T(8,128)(2,1)S(1)} %collective-permute-done.1), channel_id=1, source_target_pairs={{0,2},{1,3},{2,0},{3,1},{4,6},{5,7},{6,4},{7,5},{8,10},{9,11},{10,... | collective-permute-start | bytes 393224 | tf_op jit(solution)/shard_map/ppermute | solution.py:253
  15.3 2.4 %collective-permute-done.6 = bf16[8,8192]{1,0:T(8,128)(2,1)S(1)} collective-permute-done((bf16[8,8192]{1,0:T(8,128)(2,1)S(1)}, bf16[8,8192]{1,0:T(8,128)(2,1)S(1)}, u32[]{:S(2)}, u32[]{:S(2)}) %collective-permute-start.6) | collective-permute-done | bytes 131104 | tf_op jit(solution)/shard_map/ppermute | solution.py:253
  17.7 0.5 collective-permute-start.7
  18.2 1.3 %collective-permute-done.5 = bf16[8,8192]{1,0:T(8,128)(2,1)S(1)} collective-permute-done((bf16[8,8192]{1,0:T(8,128)(2,1)S(1)}, bf16[8,8192]{1,0:T(8,128)(2,1)S(1)}, u32[]{:S(2)}, u32[]{:S(2)}) %collective-permute-start.5) | collective-permute-done | bytes 131104 | tf_op jit(solution)/shard_map/ppermute | solution.py:253
  19.6 2.0 %collective-permute-done.2 = bf16[8,8192]{1,0:T(8,128)(2,1)S(1)} collective-permute-done((bf16[8,8192]{1,0:T(8,128)(2,1)S(1)}, bf16[8,8192]{1,0:T(8,128)(2,1)S(1)}, u32[]{:S(2)}, u32[]{:S(2)}) %collective-permute-start.2) | collective-permute-done | bytes 131104 | tf_op jit(solution)/shard_map/ppermute | solution.py:253
  21.7 1.3 %collective-permute-done.7 = bf16[8,8192]{1,0:T(8,128)(2,1)S(1)} collective-permute-done((bf16[8,8192]{1,0:T(8,128)(2,1)S(1)}, bf16[8,8192]{1,0:T(8,128)(2,1)S(1)}, u32[]{:S(2)}, u32[]{:S(2)}) %collective-permute-start.7) | collective-permute-done | bytes 131104 | tf_op jit(solution)/shard_map/ppermute | solution.py:253
  23.0 0.5 collective-permute-done.8.refs_2_
  23.6 1.4 %collective-permute-done.9.refs_3_ = bf16[32,8192]{1,0:T(8,128)(2,1)S(1)} collective-permute-done((bf16[32,8192]{1,0:T(8,128)(2,1)S(1)}, bf16[32,8192]{1,0:T(8,128)(2,1)S(1)}, u32[]{:S(2)}, u32[]{:S(2)}) %collective-permute-start.9) | collective-permute-done | bytes 524320 | tf_op jit(solution)/shard_map/ppermute | solution.py:253
  24.9 1.6 %shard_map.87 = (f32[128,512]{1,0:T(8,128)S(1)}, f32[128,512]{1,0:T(8,128)S(1)}, f32[16,8,128]{2,1,0:T(8,128)S(1)}) custom-call(s32[1]{0:T(128)} %bitcast.me_ref.refs_0_, bf16[128,128]{1,0:T(8,128)(2,1)S(1)} %get-tuple-element.26.pick_ref, f32[128,128]{1,0:T(8,128)S(1)} %get-tuple-element.25.label_ref.refs_1_, bf16[32,8192]{1,0:T(8,128)(2,1)S(1)} %pad_maximum_fusion.refs_0_, ...), custom_call_target="tpu_custom_call" | custom-call | flops 1073741824 | bytes 10485760 | tf_op jit(solution)/shard_map/pallas_call | solution.py:127
  26.6 12.3 %all_to_all.5.refs_2_ = f32[16,8,128]{2,1,0:T(8,128)S(1)} all-to-all(f32[16,8,128]{2,1,0:T(8,128)S(1)} %get-tuple-element.30), channel_id=1, replica_groups=mesh['groups'=2,'dp'=16] {'dp'}, dimensions={0} | all-to-all | bytes 131072 | tf_op jit(solution)/shard_map/all_to_all | solution.py:342
  38.9 1.6 %shard_map.88 = (f32[64,4096]{1,0:T(8,128)S(1)}, bf16[32,4096]{1,0:T(8,128)(2,1)S(1)}, bf16[32,4096]{1,0:T(8,128)(2,1)S(1)}, bf16[128,512]{1,0:T(8,128)(2,1)S(1)}, f32[1,128]{1,0:T(1,128)S(1)}) custom-call(s32[1]{0:T(128)} %bitcast.me_ref.refs_0_, f32[128,128]{1,0:T(8,128)S(1)} %get-tuple-element.25.label_ref.refs_1_, f32[16,8,128]{2,1,0:T(8,128)S(1)} %all_to_all.5.refs_2_, ...), custom_call_target="tpu_custom_call" | custom-call | flops 536870912 | bytes 6291456 | tf_op jit(solution)/shard_map/pallas_call | solution.py:205
  40.5 0.5 collective-permute-start.10
  41.0 1.0 %collective-permute-done.11 = bf16[32,4096]{1,0:T(8,128)(2,1)S(1)} collective-permute-done((bf16[32,4096]{1,0:T(8,128)(2,1)S(1)}, bf16[32,4096]{1,0:T(8,128)(2,1)S(1)}, u32[]{:S(2)}, u32[]{:S(2)}) %collective-permute-start.11) | collective-permute-done | bytes 262176 | tf_op jit(solution)/shard_map/ppermute | solution.py:253
  42.2 0.2 collective-permute-start.13
  42.5 2.4 %shard_map.89 = bf16[4096,512]{1,0:T(8,128)(2,1)} custom-call(bf16[32,8192]{1,0:T(8,128)(2,1)S(1)} %pad_maximum_fusion.refs_0_, bf16[32,8192]{1,0:T(8,128)(2,1)S(1)} %constant_dynamic-update-slice_fusion.refs_1_, bf16[32,8192]{1,0:T(8,128)(2,1)S(1)} %collective-permute-done.8.refs_2_, bf16[32,8192]{1,0:T(8,128)(2,1)S(1)} %collective-permute-done.9.refs_3_, ...), custom_call_target="tpu_custom_call" | custom-call | flops 536870912 | bytes 5242880 | tf_op jit(solution)/shard_map/pallas_call | solution.py:236
  44.9 1.9 %collective-permute-start.12 = (bf16[16,4096]{1,0:T(8,128)(2,1)S(1)}, bf16[16,4096]{1,0:T(8,128)(2,1)S(1)}, u32[]{:S(2)}, u32[]{:S(2)}) collective-permute-start(bf16[16,4096]{1,0:T(8,128)(2,1)S(1)} %fusion.1), channel_id=1, source_target_pairs={{0,2},{1,3},{2,0},{3,1},{4,6},{5,7},{6,4},{7,5},{8,10},{9,11},{10,... | collective-permute-start | bytes 393224 | tf_op jit(solution)/shard_map/ppermute | solution.py:253
  46.8 0.9 %collective-permute-done.13 = bf16[16,4096]{1,0:T(8,128)(2,1)S(1)} collective-permute-done((bf16[16,4096]{1,0:T(8,128)(2,1)S(1)}, bf16[16,4096]{1,0:T(8,128)(2,1)S(1)}, u32[]{:S(2)}, u32[]{:S(2)}) %collective-permute-start.13) | collective-permute-done | bytes 131104 | tf_op jit(solution)/shard_map/ppermute | solution.py:253
  47.8 0.3 collective-permute-start.14
  48.1 2.3 %collective-permute-start.15 = (bf16[8,4096]{1,0:T(8,128)(2,1)S(1)}, bf16[8,4096]{1,0:T(8,128)(2,1)S(1)}, u32[]{:S(2)}, u32[]{:S(2)}) collective-permute-start(bf16[8,4096]{1,0:T(8,128)(2,1)S(1)} %get-tuple-element.46), channel_id=1, source_target_pairs={{0,12},{1,13},{2,14},{3,15},{4,8},{5,9},{6,10},{7,11},{8,4},{9,5},... | collective-permute-start | bytes 196616 | tf_op jit(solution)/shard_map/ppermute | solution.py:253
  50.4 0.2 collective-permute-done.12
  50.6 0.9 %collective-permute-start.16 = (bf16[8,4096]{1,0:T(8,128)(2,1)S(1)}, bf16[8,4096]{1,0:T(8,128)(2,1)S(1)}, u32[]{:S(2)}, u32[]{:S(2)}) collective-permute-start(bf16[8,4096]{1,0:T(8,128)(2,1)S(1)} %slice.72), channel_id=1, source_target_pairs={{0,4},{1,5},{2,6},{3,7},{4,0},{5,1},{6,2},{7,3},{8,12},{9,13},{10,... | collective-permute-start | bytes 196616 | tf_op jit(solution)/shard_map/ppermute | solution.py:253
  51.5 0.5 slice_bitcast_fusion.2
  52.0 3.2 %collective-permute-done.14 = bf16[8,4096]{1,0:T(8,128)(2,1)S(1)} collective-permute-done((bf16[8,4096]{1,0:T(8,128)(2,1)S(1)}, bf16[8,4096]{1,0:T(8,128)(2,1)S(1)}, u32[]{:S(2)}, u32[]{:S(2)}) %collective-permute-start.14) | collective-permute-done | bytes 65568 | tf_op jit(solution)/shard_map/ppermute | solution.py:253
  55.2 0.5 collective-permute-done.16
  55.6 0.7 %fusion.3 = f32[8,4096]{1,0:T(8,128)} fusion(f32[16,4096]{1,0:T(8,128)S(1)} %convert_add_fusion.2, bf16[8,4096]{1,0:T(8,128)(2,1)S(1)} %collective-permute-done.16, bf16[8,4096]{1,0:T(8,128)(2,1)S(1)} %collective-permute-done.15, bf16[8,4096]{1,0:T(8,128)(2,1)S(1)} %collective-permute-done.14), kind=kLoop, calls=%fused_computation.14 | loop fusion | flops 196608 | bytes 458752 | tf_op jit(solution)/shard_map/add | solution.py:324
  (26 shorter events, 0.7 us)
Async XLA Ops:
  0.6 12.0 %collective-permute-start.3 = (bf16[8,4096]{1,0:T(8,128)(2,1)}, bf16[8,4096]{1,0:T(8,128)(2,1)S(1)}, u32[]{:S(2)}, u32[]{:S(2)}) collective-permute-start(bf16[8,4096]{1,0:T(8,128)(2,1)} %teacher_ref.1), channel_id=1, source_target_pairs={{0,8},{1,9},{2,10},{3,11},{4,12},{5,13},{6,14},{7,15},{8,0},{9,1},... | collective-permute-start | bytes 196616 | tf_op jit(solution)/shard_map/ppermute | solution.py:253
  4.7 7.9 %collective-permute-start.4 = (bf16[8,4096]{1,0:T(8,128)(2,1)}, bf16[8,4096]{1,0:T(8,128)(2,1)S(1)}, u32[]{:S(2)}, u32[]{:S(2)}) collective-permute-start(bf16[8,4096]{1,0:T(8,128)(2,1)} %student_ref.1), channel_id=1, source_target_pairs={{0,8},{1,9},{2,10},{3,11},{4,12},{5,13},{6,14},{7,15},{8,0},{9,1},... | collective-permute-start | bytes 196616 | tf_op jit(solution)/shard_map/ppermute | solution.py:253
  5.7 8.2 %collective-permute-start.1 = (bf16[8,8192]{1,0:T(8,128)(2,1)S(1)}, bf16[8,8192]{1,0:T(8,128)(2,1)S(1)}, u32[]{:S(2)}, u32[]{:S(2)}) collective-permute-start(bf16[8,8192]{1,0:T(8,128)(2,1)S(1)} %shard_map.85), channel_id=1, source_target_pairs={{0,4},{1,5},{2,6},{3,7},{4,0},{5,1},{6,2},{7,3},{8,12},{9,13},{10,... | collective-permute-start | bytes 393224 | tf_op jit(solution)/shard_map/ppermute | solution.py:253
  7.6 12.0 %collective-permute-start = (bf16[8,8192]{1,0:T(8,128)(2,1)S(1)}, bf16[8,8192]{1,0:T(8,128)(2,1)S(1)}, u32[]{:S(2)}, u32[]{:S(2)}) collective-permute-start(bf16[8,8192]{1,0:T(8,128)(2,1)S(1)} %shard_map.85), channel_id=1, source_target_pairs={{0,2},{1,3},{2,0},{3,1},{4,6},{5,7},{6,4},{7,5},{8,10},{9,11},{10,... | collective-permute-start | bytes 393224 | tf_op jit(solution)/shard_map/ppermute | solution.py:253
  12.7 5.0 %collective-permute-start.6 = (bf16[8,8192]{1,0:T(8,128)(2,1)S(1)}, bf16[8,8192]{1,0:T(8,128)(2,1)S(1)}, u32[]{:S(2)}, u32[]{:S(2)}) collective-permute-start(bf16[8,8192]{1,0:T(8,128)(2,1)S(1)} %pad_maximum_fusion.1), channel_id=1, source_target_pairs={{0,4},{1,5},{2,6},{3,7},{4,0},{5,1},{6,2},{7,3},{8,12},{9,13},{10,... | collective-permute-start | bytes 393224 | tf_op jit(solution)/shard_map/ppermute | solution.py:253
  13.2 6.3 %collective-permute-start.5 = (bf16[8,8192]{1,0:T(8,128)(2,1)S(1)}, bf16[8,8192]{1,0:T(8,128)(2,1)S(1)}, u32[]{:S(2)}, u32[]{:S(2)}) collective-permute-start(bf16[8,8192]{1,0:T(8,128)(2,1)S(1)} %pad_maximum_fusion.1), channel_id=1, source_target_pairs={{0,2},{1,3},{2,0},{3,1},{4,6},{5,7},{6,4},{7,5},{8,10},{9,11},{10,... | collective-permute-start | bytes 393224 | tf_op jit(solution)/shard_map/ppermute | solution.py:253
  13.9 7.6 %collective-permute-start.2 = (bf16[8,8192]{1,0:T(8,128)(2,1)S(1)}, bf16[8,8192]{1,0:T(8,128)(2,1)S(1)}, u32[]{:S(2)}, u32[]{:S(2)}) collective-permute-start(bf16[8,8192]{1,0:T(8,128)(2,1)S(1)} %collective-permute-done.1), channel_id=1, source_target_pairs={{0,2},{1,3},{2,0},{3,1},{4,6},{5,7},{6,4},{7,5},{8,10},{9,11},{10,... | collective-permute-start | bytes 393224 | tf_op jit(solution)/shard_map/ppermute | solution.py:253
  17.7 5.2 %collective-permute-start.7 = (bf16[8,8192]{1,0:T(8,128)(2,1)S(1)}, bf16[8,8192]{1,0:T(8,128)(2,1)S(1)}, u32[]{:S(2)}, u32[]{:S(2)}) collective-permute-start(bf16[8,8192]{1,0:T(8,128)(2,1)S(1)} %collective-permute-done.6), channel_id=1, source_target_pairs={{0,2},{1,3},{2,0},{3,1},{4,6},{5,7},{6,4},{7,5},{8,10},{9,11},{10,... | collective-permute-start | bytes 393224 | tf_op jit(solution)/shard_map/ppermute | solution.py:253
  21.6 2.0 %collective-permute-start.8 = (bf16[32,8192]{1,0:T(8,128)(2,1)S(1)}, bf16[32,8192]{1,0:T(8,128)(2,1)S(1)}, u32[]{:S(2)}, u32[]{:S(2)}) collective-permute-start(bf16[32,8192]{1,0:T(8,128)(2,1)S(1)} %pad_maximum_fusion.refs_0_), channel_id=1, source_target_pairs={{0,1},{1,0},{2,3},{3,2},{4,5},{5,4},{6,7},{7,6},{8,9},{9,8},{10,11... | collective-permute-start | bytes 1572872 | tf_op jit(solution)/shard_map/ppermute | solution.py:253
  23.0 2.0 %collective-permute-start.9 = (bf16[32,8192]{1,0:T(8,128)(2,1)S(1)}, bf16[32,8192]{1,0:T(8,128)(2,1)S(1)}, u32[]{:S(2)}, u32[]{:S(2)}) collective-permute-start(bf16[32,8192]{1,0:T(8,128)(2,1)S(1)} %constant_dynamic-update-slice_fusion.refs_1_), channel_id=1, source_target_pairs={{0,1},{1,0},{2,3},{3,2},{4,5},{5,4},{6,7},{7,6},{8,9},{9,8},{10,11... | collective-permute-start | bytes 1572872 | tf_op jit(solution)/shard_map/ppermute | solution.py:253
  40.5 1.6 %collective-permute-start.11 = (bf16[32,4096]{1,0:T(8,128)(2,1)S(1)}, bf16[32,4096]{1,0:T(8,128)(2,1)S(1)}, u32[]{:S(2)}, u32[]{:S(2)}) collective-permute-start(bf16[32,4096]{1,0:T(8,128)(2,1)S(1)} %get-tuple-element.36), channel_id=1, source_target_pairs={{0,1},{1,0},{2,3},{3,2},{4,5},{5,4},{6,7},{7,6},{8,9},{9,8},{10,11... | collective-permute-start | bytes 786440 | tf_op jit(solution)/shard_map/ppermute | solution.py:253
  40.5 1.9 %collective-permute-start.10 = (bf16[32,4096]{1,0:T(8,128)(2,1)S(1)}, bf16[32,4096]{1,0:T(8,128)(2,1)S(1)}, u32[]{:S(2)}, u32[]{:S(2)}) collective-permute-start(bf16[32,4096]{1,0:T(8,128)(2,1)S(1)} %get-tuple-element.35), channel_id=1, source_target_pairs={{0,1},{1,0},{2,3},{3,2},{4,5},{5,4},{6,7},{7,6},{8,9},{9,8},{10,11... | collective-permute-start | bytes 786440 | tf_op jit(solution)/shard_map/ppermute | solution.py:253
  42.2 5.6 %collective-permute-start.13 = (bf16[16,4096]{1,0:T(8,128)(2,1)S(1)}, bf16[16,4096]{1,0:T(8,128)(2,1)S(1)}, u32[]{:S(2)}, u32[]{:S(2)}) collective-permute-start(bf16[16,4096]{1,0:T(8,128)(2,1)S(1)} %fusion), channel_id=1, source_target_pairs={{0,2},{1,3},{2,0},{3,1},{4,6},{5,7},{6,4},{7,5},{8,10},{9,11},{10,... | collective-permute-start | bytes 393224 | tf_op jit(solution)/shard_map/ppermute | solution.py:253
  44.9 5.6 %collective-permute-start.12 = (bf16[16,4096]{1,0:T(8,128)(2,1)S(1)}, bf16[16,4096]{1,0:T(8,128)(2,1)S(1)}, u32[]{:S(2)}, u32[]{:S(2)}) collective-permute-start(bf16[16,4096]{1,0:T(8,128)(2,1)S(1)} %fusion.1), channel_id=1, source_target_pairs={{0,2},{1,3},{2,0},{3,1},{4,6},{5,7},{6,4},{7,5},{8,10},{9,11},{10,... | collective-permute-start | bytes 393224 | tf_op jit(solution)/shard_map/ppermute | solution.py:253
  47.8 7.4 %collective-permute-start.14 = (bf16[8,4096]{1,0:T(8,128)(2,1)S(1)}, bf16[8,4096]{1,0:T(8,128)(2,1)S(1)}, u32[]{:S(2)}, u32[]{:S(2)}) collective-permute-start(bf16[8,4096]{1,0:T(8,128)(2,1)S(1)} %get-tuple-element.45), channel_id=1, source_target_pairs={{0,8},{1,9},{2,10},{3,11},{4,12},{5,13},{6,14},{7,15},{8,0},{9,1},... | collective-permute-start | bytes 196616 | tf_op jit(solution)/shard_map/ppermute | solution.py:253
  48.1 7.1 %collective-permute-start.15 = (bf16[8,4096]{1,0:T(8,128)(2,1)S(1)}, bf16[8,4096]{1,0:T(8,128)(2,1)S(1)}, u32[]{:S(2)}, u32[]{:S(2)}) collective-permute-start(bf16[8,4096]{1,0:T(8,128)(2,1)S(1)} %get-tuple-element.46), channel_id=1, source_target_pairs={{0,12},{1,13},{2,14},{3,15},{4,8},{5,9},{6,10},{7,11},{8,4},{9,5},... | collective-permute-start | bytes 196616 | tf_op jit(solution)/shard_map/ppermute | solution.py:253
  50.6 5.0 %collective-permute-start.16 = (bf16[8,4096]{1,0:T(8,128)(2,1)S(1)}, bf16[8,4096]{1,0:T(8,128)(2,1)S(1)}, u32[]{:S(2)}, u32[]{:S(2)}) collective-permute-start(bf16[8,4096]{1,0:T(8,128)(2,1)S(1)} %slice.72), channel_id=1, source_target_pairs={{0,4},{1,5},{2,6},{3,7},{4,0},{5,1},{6,2},{7,3},{8,12},{9,13},{10,... | collective-permute-start | bytes 196616 | tf_op jit(solution)/shard_map/ppermute | solution.py:253

commit v5 on v4

v5 whole, which is shorter than its diff:
```python
import functools

import jax
import jax.numpy as jnp
from jax import lax
from jax.experimental import pallas as pl
from jax.experimental.pallas import tpu as pltpu
from jax.sharding import PartitionSpec as P

CE_WEIGHT = 0.5
VMEM_LIMIT = 28 * 2**20
STATS = 8


def held_rows(shape, dim, me, rows_local, tuned):
    held = lax.broadcasted_iota(jnp.int32, shape, dim)
    if not tuned:
        return held
    step = rows_local.bit_length() - 1
    block = lax.shift_right_logical(held, step)
    distance = (block & 7) * 2 + lax.shift_right_logical(block, 3)
    return (me ^ distance) * rows_local + (held & (rows_local - 1))


def to_column(is_row, row):
    return jnp.sum(jnp.where(is_row, row, 0.0), axis=1, keepdims=True)


def prepare_kernel(rows_local, tuned, me_ref, order_ref, labels_ref, *refs):
    teacher_ref, student_ref, teacher_out, student_out, pick_out, label_out, *turned_out = refs[: -4]
    ids, id_sems, teacher_sem, student_sems = refs[-4:]
    id_copies = [
        pltpu.make_async_copy(source, ids.at[j], id_sems.at[j]) for j, source in enumerate((order_ref, labels_ref))
    ]
    pieces = student_sems.shape[0]
    rows = student_ref.shape[0] // pieces
    parts = [pl.ds(k * rows, rows) for k in range(pieces)]
    copies = [
        pltpu.make_async_copy(student_ref.at[part], student_out.at[part], student_sems.at[k])
        for k, part in enumerate(parts)
    ]
    copies.append(pltpu.make_async_copy(teacher_ref, teacher_out, teacher_sem))
    for copy in id_copies + copies:
        copy.start()
    me = me_ref[0]
    count = order_ref.shape[1]
    vocab = teacher_ref.shape[1]
    lanes = lax.broadcasted_iota(jnp.int32, (count, count), 1)
    is_row = held_rows((count, count), 0, me, rows_local, tuned) == lanes
    have = held_rows((count, count), 1, me, rows_local, tuned).astype(jnp.float32)
    for copy in id_copies:
        copy.wait()
    wanted = to_column(is_row, ids[0].astype(jnp.float32))
    pick_out[...] = jnp.where(wanted == have, 1.0, 0.0).astype(jnp.bfloat16)
    label = to_column(is_row, ids[1].astype(jnp.float32)) - (me * vocab).astype(jnp.float32)
    label_out[...] = jnp.broadcast_to(label, label_out.shape)
    for k, copy in enumerate(copies):
        copy.wait()
        if k < pieces:
            for out in turned_out:
                out[:, k * rows : (k + 1) * rows] = student_out[k * rows : (k + 1) * rows].T


def stay(value):
    return pltpu.with_memory_space_constraint(value, pltpu.HBM)


def prepare(me, order, labels, heads, rows_local, tuned):
    count = order.shape[0]
    vmem = pl.BlockSpec(memory_space=pltpu.VMEM)
    hbm = pl.BlockSpec(memory_space=pltpu.HBM)
    shapes = [
        jax.ShapeDtypeStruct(heads[0].shape, heads[0].dtype),
        jax.ShapeDtypeStruct(heads[1].shape, heads[1].dtype),
        jax.ShapeDtypeStruct((count, count), jnp.bfloat16),
        jax.ShapeDtypeStruct((count, 128), jnp.float32),
    ] + [jax.ShapeDtypeStruct(heads[1].shape[::-1], heads[1].dtype)] * tuned
    return pl.pallas_call(
        functools.partial(prepare_kernel, rows_local, tuned),
        in_specs=[pl.BlockSpec(memory_space=pltpu.SMEM)] + [hbm] * 4,
        out_specs=(vmem,) * len(shapes),
        out_shape=tuple(shapes),
        scratch_shapes=[
            pltpu.VMEM((2, 1, count), jnp.int32),
            pltpu.SemaphoreType.DMA((2,)),
            pltpu.SemaphoreType.DMA,
            pltpu.SemaphoreType.DMA((8,)),
        ],
        compiler_params=pltpu.CompilerParams(vmem_limit_bytes=24 * 2**20),
        cost_estimate=pl.CostEstimate(flops=0, bytes_accessed=heads[0].size * 8, transcendentals=0),
    )(me, stay(order[None]), stay(labels[None]), *map(stay, heads))


def logits_kernel(rows_local, tuned, parts, me_ref, pick_ref, label_ref, *refs):
    pieces = refs[:parts]
    teacher_head, student_head, teacher_out, student_out, stats_out, *away_out = refs[parts:]
    depth, vocab = student_head.shape

    def product(first, head):
        rows = jnp.concatenate([piece[:, first : first + depth] for piece in pieces], axis=0)
        return jnp.dot(rows, head[...], preferred_element_type=jnp.float32)

    me = me_ref[0]
    raw = product(0, teacher_head)
    student = product(depth, student_head)
    count = student.shape[0]
    high = raw.astype(jnp.bfloat16)
    rest = raw - high.astype(jnp.float32)
    middle = rest.astype(jnp.bfloat16)
    low = (rest - middle.astype(jnp.float32)).astype(jnp.bfloat16)
    pick = pick_ref[...]
    teacher = sum(jnp.dot(pick, piece, preferred_element_type=jnp.float32) for piece in (high, middle, low))
    teacher_out[...] = teacher
    student_out[...] = student
    for out in away_out:
        out[0] = teacher[count // 2 :]
        out[1] = student[count // 2 :]
    is_label = label_ref[:, 0:1].astype(jnp.int32) == lax.broadcasted_iota(jnp.int32, (count, vocab), 1)
    teacher_max = jnp.max(teacher, axis=1, keepdims=True)
    student_max = jnp.max(student, axis=1, keepdims=True)
    teacher_exp = jnp.exp(teacher - teacher_max)
    values = (
        teacher_max,
        student_max,
        jnp.sum(teacher_exp, axis=1, keepdims=True),
        jnp.sum(jnp.exp(student - student_max), axis=1, keepdims=True),
        jnp.sum(teacher_exp * (teacher - student), axis=1, keepdims=True),
        jnp.sum(jnp.where(is_label, student, 0.0), axis=1, keepdims=True),
    )
    lanes = lax.broadcasted_iota(jnp.int32, (count, count), 1)
    is_row = held_rows((count, count), 0, me, rows_local, tuned) == lanes
    block = [jnp.sum(jnp.where(is_row, value, 0.0), axis=0, keepdims=True) for value in values]
    block.append(jnp.zeros((STATS - len(block), count), jnp.float32))
    stats_out[...] = jnp.broadcast_to(jnp.concatenate(block, axis=0)[None], stats_out.shape)


def logits(me, pick, label, hidden, heads, n, rows_local, tuned):
    count = pick.shape[0]
    depth, vocab = heads[0].shape
    vmem = pl.BlockSpec(memory_space=pltpu.VMEM)
    shapes = [(count, vocab), (count, vocab), (n, STATS, count)] + [(2, count // 2, vocab)] * tuned
    return pl.pallas_call(
        functools.partial(logits_kernel, rows_local, tuned, len(hidden)),
        in_specs=[pl.BlockSpec(memory_space=pltpu.SMEM)] + [vmem] * (4 + len(hidden)),
        out_specs=(vmem,) * len(shapes),
        out_shape=tuple(jax.ShapeDtypeStruct(shape, jnp.float32) for shape in shapes),
        compiler_params=pltpu.CompilerParams(vmem_limit_bytes=VMEM_LIMIT),
        cost_estimate=pl.CostEstimate(
            flops=4 * count * depth * vocab, bytes_accessed=4 * depth * (vocab + count), transcendentals=2 * count * vocab
        ),
    )(me, pick, label, *hidden, *heads)


def merged(stats_ref):
    devices, _, count = stats_ref.shape
    top = stats_ref[0, 0:2]
    for d in range(1, devices):
        top = jnp.maximum(top, stats_ref[d, 0:2])
    totals = jnp.zeros((2, count), jnp.float32)
    cross = jnp.zeros((1, count), jnp.float32)
    label_logit = jnp.zeros((1, count), jnp.float32)
    for d in range(devices):
        weight = jnp.exp(stats_ref[d, 0:2] - top)
        totals += weight * stats_ref[d, 2:4]
        cross += weight[0:1] * stats_ref[d, 4:5]
        label_logit += stats_ref[d, 5:6]
    return top + jnp.log(totals), totals, cross, label_logit


def logit_gradient(teacher, student, norms, is_row, label):
    is_label = label.astype(jnp.int32) == lax.broadcasted_iota(jnp.int32, student.shape, 1)
    return (
        (1.0 + CE_WEIGHT) * jnp.exp(student - to_column(is_row, norms[1:2]))
        - jnp.exp(teacher - to_column(is_row, norms[0:1]))
        - jnp.where(is_label, CE_WEIGHT, 0.0)
    ).astype(jnp.bfloat16)


def times_transposed(grad, head):
    return lax.dot_general(grad, head, (((1,), (1,)), ((), ())), preferred_element_type=jnp.float32)


def grad_kernel(
    rows_local, me_ref, label_ref, stats_ref, teacher_ref, student_ref, away_ref, turned_ref, other_ref, *outs
):
    near_keep, near_send, far_keep, far_send = outs
    me = me_ref[0]
    count, vocab = student_ref.shape
    own = count // 2
    norms = merged(stats_ref)[0]
    is_row = held_rows((own, count), 0, me, rows_local, True) == lax.broadcasted_iota(jnp.int32, (own, count), 1)
    label = label_ref[:own, 0:1]
    grad = logit_gradient(teacher_ref[:own], student_ref[:own], norms, is_row, label)
    shift = jnp.where((me & 1) == 0, -vocab, vocab).astype(jnp.float32)
    other = logit_gradient(away_ref[0], away_ref[1], norms, is_row, label + shift)
    depth = turned_ref.shape[1]
    step = min(512, depth)
    for k in range(0, depth, step):
        part = jnp.dot(grad, turned_ref[:, k : k + step], preferred_element_type=jnp.float32)
        part += jnp.dot(other, other_ref[:, k : k + step], preferred_element_type=jnp.float32)
        blocks = [part[b * rows_local : (b + 1) * rows_local] for b in range(8)]
        for j, out in enumerate((near_keep, near_send, far_keep, far_send)):
            first = (j // 2) * 4 + j % 2
            out[:, k : k + step] = jnp.concatenate((blocks[first], blocks[first + 2]), axis=0).astype(out.dtype)


def whole_grad_kernel(rows_local, me_ref, label_ref, stats_ref, teacher_ref, student_ref, head_ref, out_ref):
    count, vocab = student_ref.shape
    norms = merged(stats_ref)[0]
    is_row = held_rows((count, count), 0, me_ref[0], rows_local, False) == lax.broadcasted_iota(
        jnp.int32, (count, count), 1
    )
    grad = logit_gradient(teacher_ref[...], student_ref[...], norms, is_row, label_ref[:, 0:1])
    depth = head_ref.shape[0]
    step = min(512, depth)
    for k in range(0, depth, step):
        out_ref[:, k : k + step] = times_transposed(grad, head_ref[k : k + step])


def gradient(me, label, stats, logits, heads, rows_local, tuned):
    count, vocab = logits[0].shape
    depth = heads[0].shape[1 if tuned else 0]
    vmem = pl.BlockSpec(memory_space=pltpu.VMEM)
    if tuned:
        shapes = [jax.ShapeDtypeStruct((2 * rows_local, depth), kind) for kind in (jnp.float32, jnp.bfloat16)] * 2
    else:
        shapes = [jax.ShapeDtypeStruct((count, depth), jnp.float32)]
    return pl.pallas_call(
        functools.partial(grad_kernel if tuned else whole_grad_kernel, rows_local),
        in_specs=[pl.BlockSpec(memory_space=pltpu.SMEM)] + [vmem] * (2 + len(logits) + len(heads)),
        out_specs=(vmem,) * len(shapes),
        out_shape=tuple(shapes),
        compiler_params=pltpu.CompilerParams(vmem_limit_bytes=VMEM_LIMIT),
        cost_estimate=pl.CostEstimate(
            flops=2 * count * depth * vocab, bytes_accessed=2 * depth * (vocab + 2 * count), transcendentals=2 * count * vocab
        ),
    )(me, label, stats, *logits, *heads)


def head_kernel(rows_local, tuned, me_ref, label_ref, stats_ref, teacher_ref, student_ref, *refs):
    *pieces, out_ref, loss_out, held, sems = refs
    me = me_ref[0]
    count = student_ref.shape[0]
    lanes = lax.broadcasted_iota(jnp.int32, (count, count), 1)
    is_row = held_rows((count, count), 0, me, rows_local, tuned) == lanes
    norms, totals, cross, label_logit = merged(stats_ref)
    grad = logit_gradient(teacher_ref[...], student_ref[...], norms, is_row, label_ref[:, 0:1])
    steps, step, _ = held.shape
    copies = []
    for k in range(steps):
        first = (steps + k) * step
        rows = jnp.concatenate([piece[:, first : first + step] for piece in pieces], axis=0)
        held[k] = lax.dot_general(rows, grad, (((0,), (0,)), ((), ())), preferred_element_type=jnp.float32).astype(
            jnp.bfloat16
        )
        copies.append(pltpu.make_async_copy(held.at[k], out_ref.at[pl.ds(k * step, step)], sems.at[k]))
        copies[-1].start()
    loss = cross / totals[0:1] - norms[0:1] + norms[1:2] + CE_WEIGHT * (norms[1:2] - label_logit)
    mine = lax.broadcasted_iota(jnp.int32, (count, count), 0) + me * rows_local == lanes
    by_lane = lax.broadcasted_iota(jnp.int32, (count, count), 0) == lanes
    loss_out[...] = jnp.sum(jnp.where(by_lane, to_column(mine, loss), 0.0), axis=0, keepdims=True)
    for copy in copies:
        copy.wait()


def head_gradient(me, label, stats, logits, hidden, depth, rows_local, tuned):
    count, vocab = logits[0].shape
    step = min(256, depth)
    vmem = pl.BlockSpec(memory_space=pltpu.VMEM)
    return pl.pallas_call(
        functools.partial(head_kernel, rows_local, tuned),
        in_specs=[pl.BlockSpec(memory_space=pltpu.SMEM)] + [vmem] * (4 + len(hidden)),
        out_specs=(pl.BlockSpec(memory_space=pltpu.HBM), vmem),
        out_shape=(jax.ShapeDtypeStruct((depth, vocab), jnp.bfloat16), jax.ShapeDtypeStruct((1, count), jnp.float32)),
        scratch_shapes=[
            pltpu.VMEM((depth // step, step, vocab), jnp.bfloat16),
            pltpu.SemaphoreType.DMA((depth // step,)),
        ],
        compiler_params=pltpu.CompilerParams(vmem_limit_bytes=VMEM_LIMIT),
        cost_estimate=pl.CostEstimate(
            flops=2 * count * depth * vocab, bytes_accessed=2 * depth * (vocab + count), transcendentals=2 * count * vocab
        ),
    )(me, label, stats, *logits, *hidden)


def swap(value, distance, n):
    return lax.ppermute(value, "dp", [(i, i ^ distance) for i in range(n)])


def after(value, *done):
    return lax.optimization_barrier((value, *done))[0]


def join_kernel(teacher_ref, student_ref, out_ref, sems):
    depth = teacher_ref.shape[1]
    copies = [
        pltpu.make_async_copy(ref, out_ref.at[:, pl.ds(j * depth, depth)], sems.at[j])
        for j, ref in enumerate((teacher_ref, student_ref))
    ]
    for copy in copies:
        copy.start()
    for copy in copies:
        copy.wait()


def join_rows(teacher_rows, student_rows):
    count, depth = teacher_rows.shape
    return pl.pallas_call(
        join_kernel,
        in_specs=[pl.BlockSpec(memory_space=pltpu.HBM)] * 2,
        out_specs=pl.BlockSpec(memory_space=pltpu.VMEM),
        out_shape=jax.ShapeDtypeStruct((count, 2 * depth), teacher_rows.dtype),
        scratch_shapes=[pltpu.SemaphoreType.DMA((2,))],
        compiler_params=pltpu.CompilerParams(vmem_limit_bytes=2**20),
        cost_estimate=pl.CostEstimate(flops=0, bytes_accessed=8 * count * depth, transcendentals=0),
    )(stay(teacher_rows), stay(student_rows))


def gather_rows(teacher_rows, student_rows, n, fetch):
    join = lambda pair: jnp.concatenate(pair, axis=1)
    stack = lambda *parts: jnp.concatenate(parts, axis=0)
    depth = teacher_rows.shape[1]
    far_teacher = swap(teacher_rows, 8, n)
    rows = join_rows(teacher_rows, student_rows)
    far_student = swap(student_rows, 8, n)
    near, side = swap(rows, 4, n), swap(rows, 2, n)
    fetched = fetch(rows)
    far = join((far_teacher, far_student))
    far_ready = after(far, *fetched)
    near_ready = near
    far, near = far_ready, near_ready
    far_near = swap(far, 4, n)
    *fetched, turned = fetched
    other_head = swap(after(turned, far, near), 1, n)
    far_side = swap(far, 2, n)
    near_side = swap(near, 2, n)
    far_near_side = swap(far_near, 2, n)
    held = [stack(rows, side, near, near_side), stack(far, far_side, far_near, far_near_side)]
    return held + [swap(piece, 1, n) for piece in held], fetched, (turned, other_head)


def scatter_rows(near_keep, near_send, far_keep, far_send, rows_local, n, head_gradient_of):
    low = jnp.bfloat16
    full = jnp.float32
    far_other = swap(far_send, 2, n)
    grad_head, loss = head_gradient_of(far_send)
    near_other = swap(after(near_send, grad_head), 2, n)
    far = (far_keep + far_other.astype(full)).astype(low)
    from_far = swap(far[:rows_local], 8, n)
    from_far_near = swap(far[rows_local:], 12, n)
    near = near_keep + near_other.astype(full)
    from_near = swap(near[rows_local:].astype(low), 4, n)
    total = near[:rows_local] + from_far.astype(full) + from_far_near.astype(full) + from_near.astype(full)
    return total, grad_head, loss


def per_device(n, teacher_hidden, student_hidden, teacher_head, student_head, labels, order):
    rows_local, depth = student_hidden.shape
    tuned = n == 16 and rows_local == 8
    me = lax.axis_index("dp").astype(jnp.int32).reshape(1)
    heads = (teacher_head, student_head)
    fetch = lambda *done: prepare(after(me, *done), order, labels, heads, rows_local, tuned)
    if tuned:
        hidden, fetched, turned = gather_rows(teacher_hidden, student_hidden, n, fetch)
    else:
        fetched = fetch(me)
        rows = jnp.concatenate([teacher_hidden, student_hidden], axis=1)
        hidden = [lax.all_gather(rows, "dp", axis=0, tiled=True)]
    *heads, pick, label = fetched
    *logit, stats = logits(me, pick, label, hidden, heads, n, rows_local, tuned)
    if tuned:
        stats, away = logit.pop(), swap(stats, 1, n)
    stats = lax.all_to_all(stats, "dp", 0, 0)
    head_gradient_of = lambda *done: head_gradient(after(me, *done), label, stats, logit, hidden, depth, rows_local, tuned)
    if tuned:
        parts = gradient(me, label, stats, (*logit, away), turned, rows_local, tuned)
        grad_hidden, grad_head, loss = scatter_rows(*parts, rows_local, n, head_gradient_of)
    else:
        (part,) = gradient(me, label, stats, logit, heads[1:], rows_local, tuned)
        grad_head, loss = head_gradient_of()
        grad_hidden = lax.psum_scatter(part, "dp", scatter_dimension=0, tiled=True)
    return (loss[0, :rows_local], grad_hidden, grad_head)


def solution(mesh):
    in_specs = (
        P(("groups", "dp"), None),
        P(("groups", "dp"), None),
        P(None, "dp"),
        P(None, "dp"),
        P("groups"),
        P("groups"),
    )
    out_specs = (P(("groups", "dp")), P(("groups", "dp"), None), P("groups", "dp"))
    return jax.shard_map(
        functools.partial(per_device, mesh.shape["dp"]),
        mesh=mesh,
        in_specs=in_specs,
        out_specs=out_specs,
        check_vma=False,
    )
```

time: 56.5 us -> 55 us (0.973)
  waiting for transfers between devices: 14.7 us -> 13.5 us
  blocking collectives: 12.3 us -> 11.7 us
    ppermute x17, waiting for transfers between devices: 14.7 us -> 13.5 us  [swap(): return lax.ppermute(value, 'dp', [(i, i ^ distance) for i in range(n)])]
    all_to_all x1, blocking collectives: 12.3 us -> 11.7 us  [per_device(): stats = lax.all_to_all(stats, 'dp', 0, 0)]
  transfers between devices with their start and end apart: 17 -> 17, of which waited for: 12 -> 9; matrix products, arithmetic and copies ran while one was open for 2% -> 1% of each run, Pallas kernels for 12% -> 16%
where the time goes in v5:
time: 55 us; the launch traced here: 54.8 us
  starting transfers between devices  17 us (31%)
  waiting for transfers between devices  13.5 us (25%)
  blocking collectives  11.7 us (21%)
  Pallas kernels  10.4 us (19%)
  other arithmetic  0.79 us (1%)
  between operations  0.79 us (1%)
  local copies, waits for them, and re-layouts  0.57 us (1%)
    ppermute x17, starting transfers between devices, swap(): return lax.ppermute(value, 'dp', [(i, i ^ distance) for i in range(n)])  17 us
    ppermute x17, waiting for transfers between devices, swap(): return lax.ppermute(value, 'dp', [(i, i ^ distance) for i in range(n)])  13.5 us
    all_to_all x1, blocking collectives, per_device(): stats = lax.all_to_all(stats, 'dp', 0, 0)  11.7 us
    pallas_call x1, Pallas kernels, prepare(): pl.pallas_call(functools.partial(prepare_kernel, rows_local, tuned), in_s...  3.6 us
    pallas_call x1, Pallas kernels, head_gradient(): pl.pallas_call(functools.partial(head_kernel, rows_local, tuned), in_spec...  2.58 us
    pallas_call x1, Pallas kernels, gradient(): pl.pallas_call(functools.partial(grad_kernel if tuned else whole_grad_ker...  1.75 us
    pallas_call x1, Pallas kernels, logits(): pl.pallas_call(functools.partial(logits_kernel, rows_local, tuned, len(hi...  1.59 us
  transfers between devices with their start and end apart: 17, of which 9 were waited for; matrix products, arithmetic and copies ran while one was open for 1% of the time, Pallas kernels for 16%

profile of v5, /device:TPU:0, one launch (start us, length us, event | category | flops | bytes accessed | tf_op | source)
XLA Modules:
  0.0 54.8 jit_solution(15484719008524422277)
XLA Ops:
  0.6 4.1 %collective-permute-start.3 = (bf16[8,4096]{1,0:T(8,128)(2,1)}, bf16[8,4096]{1,0:T(8,128)(2,1)S(1)}, u32[]{:S(2)}, u32[]{:S(2)}) collective-permute-start(bf16[8,4096]{1,0:T(8,128)(2,1)} %teacher_ref.1), channel_id=1, source_target_pairs={{0,8},{1,9},{2,10},{3,11},{4,12},{5,13},{6,14},{7,15},{8,0},{9,1},... | collective-permute-start | bytes 196616 | tf_op jit(solution)/shard_map/ppermute | solution.py:287
  4.7 0.1 collective-permute-start.4
  4.8 0.9 %shard_map.85 = bf16[8,8192]{1,0:T(8,128)(2,1)S(1)} custom-call(bf16[8,4096]{1,0:T(8,128)(2,1)} %teacher_ref.1, bf16[8,4096]{1,0:T(8,128)(2,1)} %student_ref.1), custom_call_target="tpu_custom_call" | custom-call | bytes 262144 | tf_op jit(solution)/shard_map/pallas_call | solution.py:308
  5.7 1.9 %collective-permute-start.1 = (bf16[8,8192]{1,0:T(8,128)(2,1)S(1)}, bf16[8,8192]{1,0:T(8,128)(2,1)S(1)}, u32[]{:S(2)}, u32[]{:S(2)}) collective-permute-start(bf16[8,8192]{1,0:T(8,128)(2,1)S(1)} %shard_map.85), channel_id=1, source_target_pairs={{0,4},{1,5},{2,6},{3,7},{4,0},{5,1},{6,2},{7,3},{8,12},{9,13},{10,... | collective-permute-start | bytes 393224 | tf_op jit(solution)/shard_map/ppermute | solution.py:287
  7.6 1.5 %collective-permute-start = (bf16[8,8192]{1,0:T(8,128)(2,1)S(1)}, bf16[8,8192]{1,0:T(8,128)(2,1)S(1)}, u32[]{:S(2)}, u32[]{:S(2)}) collective-permute-start(bf16[8,8192]{1,0:T(8,128)(2,1)S(1)} %shard_map.85), channel_id=1, source_target_pairs={{0,2},{1,3},{2,0},{3,1},{4,6},{5,7},{6,4},{7,5},{8,10},{9,11},{10,... | collective-permute-start | bytes 393224 | tf_op jit(solution)/shard_map/ppermute | solution.py:287
  9.1 3.6 %shard_map.86 = (bf16[4096,512]{1,0:T(8,128)(2,1)S(1)}, bf16[4096,512]{1,0:T(8,128)(2,1)S(1)}, bf16[128,128]{1,0:T(8,128)(2,1)S(1)}, f32[128,128]{1,0:T(8,128)S(1)}, bf16[512,4096]{1,0:T(8,128)(2,1)S(1)}) custom-call(s32[1]{0:T(128)} %bitcast.me_ref, s32[1,128]{1,0:T(1,128)} %bitcast.5, s32[1,128]{1,0:T(1,128)} %bitcast.6, bf16[4096,512]{1,0:T(8,128)(2,1)} %refs_0_.1, ...), custom_call_target="tpu_custom_call" | custom-call | bytes 16777216 | tf_op jit(solution)/shard_map/pallas_call | solution.py:78
  12.8 0.5 collective-permute-start.6
  13.3 0.6 %collective-permute-start.5 = (bf16[8,8192]{1,0:T(8,128)(2,1)S(1)}, bf16[8,8192]{1,0:T(8,128)(2,1)S(1)}, u32[]{:S(2)}, u32[]{:S(2)}) collective-permute-start(bf16[8,8192]{1,0:T(8,128)(2,1)S(1)} %pad_maximum_fusion.1), channel_id=1, source_target_pairs={{0,2},{1,3},{2,0},{3,1},{4,6},{5,7},{6,4},{7,5},{8,10},{9,11},{10,... | collective-permute-start | bytes 393224 | tf_op jit(solution)/shard_map/ppermute | solution.py:287
  13.9 0.1 collective-permute-start.11
  14.0 1.5 %collective-permute-start.2 = (bf16[8,8192]{1,0:T(8,128)(2,1)S(1)}, bf16[8,8192]{1,0:T(8,128)(2,1)S(1)}, u32[]{:S(2)}, u32[]{:S(2)}) collective-permute-start(bf16[8,8192]{1,0:T(8,128)(2,1)S(1)} %collective-permute-done.1), channel_id=1, source_target_pairs={{0,2},{1,3},{2,0},{3,1},{4,6},{5,7},{6,4},{7,5},{8,10},{9,11},{10,... | collective-permute-start | bytes 393224 | tf_op jit(solution)/shard_map/ppermute | solution.py:287
  15.5 2.3 %collective-permute-done.6 = bf16[8,8192]{1,0:T(8,128)(2,1)S(1)} collective-permute-done((bf16[8,8192]{1,0:T(8,128)(2,1)S(1)}, bf16[8,8192]{1,0:T(8,128)(2,1)S(1)}, u32[]{:S(2)}, u32[]{:S(2)}) %collective-permute-start.6) | collective-permute-done | bytes 131104 | tf_op jit(solution)/shard_map/ppermute | solution.py:287
  17.8 0.5 collective-permute-start.7
  18.3 1.1 %collective-permute-done.5 = bf16[8,8192]{1,0:T(8,128)(2,1)S(1)} collective-permute-done((bf16[8,8192]{1,0:T(8,128)(2,1)S(1)}, bf16[8,8192]{1,0:T(8,128)(2,1)S(1)}, u32[]{:S(2)}, u32[]{:S(2)}) %collective-permute-start.5) | collective-permute-done | bytes 131104 | tf_op jit(solution)/shard_map/ppermute | solution.py:287
  19.4 2.8 %collective-permute-done.2 = bf16[8,8192]{1,0:T(8,128)(2,1)S(1)} collective-permute-done((bf16[8,8192]{1,0:T(8,128)(2,1)S(1)}, bf16[8,8192]{1,0:T(8,128)(2,1)S(1)}, u32[]{:S(2)}, u32[]{:S(2)}) %collective-permute-start.2) | collective-permute-done | bytes 131104 | tf_op jit(solution)/shard_map/ppermute | solution.py:287
  22.3 1.5 %collective-permute-done.7 = bf16[8,8192]{1,0:T(8,128)(2,1)S(1)} collective-permute-done((bf16[8,8192]{1,0:T(8,128)(2,1)S(1)}, bf16[8,8192]{1,0:T(8,128)(2,1)S(1)}, u32[]{:S(2)}, u32[]{:S(2)}) %collective-permute-start.7) | collective-permute-done | bytes 131104 | tf_op jit(solution)/shard_map/ppermute | solution.py:287
  24.0 0.3 collective-permute-done.8.refs_2_
  24.2 1.6 %collective-permute-done.9.refs_3_ = bf16[32,8192]{1,0:T(8,128)(2,1)S(1)} collective-permute-done((bf16[32,8192]{1,0:T(8,128)(2,1)S(1)}, bf16[32,8192]{1,0:T(8,128)(2,1)S(1)}, u32[]{:S(2)}, u32[]{:S(2)}) %collective-permute-start.9) | collective-permute-done | bytes 524320 | tf_op jit(solution)/shard_map/ppermute | solution.py:287
  25.9 1.6 %shard_map.87 = (f32[128,512]{1,0:T(8,128)S(1)}, f32[128,512]{1,0:T(8,128)S(1)}, f32[16,8,128]{2,1,0:T(8,128)S(1)}, f32[2,64,512]{2,1,0:T(8,128)S(1)}) custom-call(s32[1]{0:T(128)} %bitcast.me_ref, bf16[128,128]{1,0:T(8,128)(2,1)S(1)} %get-tuple-element.25.pick_ref, f32[128,128]{1,0:T(8,128)S(1)} %get-tuple-element.24.label_ref, ...), custom_call_target="tpu_custom_call" | custom-call | flops 1073741824 | bytes 10485760 | tf_op jit(solution)/shard_map/pallas_call | solution.py:142
  27.5 0.2 collective-permute-start.10
  27.7 11.7 %all_to_all.5.stats_ref = f32[16,8,128]{2,1,0:T(8,128)S(1)} all-to-all(f32[16,8,128]{2,1,0:T(8,128)S(1)} %get-tuple-element.30), channel_id=1, replica_groups=mesh['groups'=2,'dp'=16] {'dp'}, dimensions={0} | all-to-all | bytes 131072 | tf_op jit(solution)/shard_map/all_to_all | solution.py:373
  39.3 1.8 %shard_map.88 = (f32[16,4096]{1,0:T(8,128)S(1)}, bf16[16,4096]{1,0:T(8,128)(2,1)S(1)}, f32[16,4096]{1,0:T(8,128)S(1)}, bf16[16,4096]{1,0:T(8,128)(2,1)S(1)}) custom-call(s32[1]{0:T(128)} %bitcast.me_ref, f32[128,128]{1,0:T(8,128)S(1)} %get-tuple-element.24.label_ref, f32[16,8,128]{2,1,0:T(8,128)S(1)} %all_to_all.5.stats_ref, ...), custom_call_target="tpu_custom_call" | custom-call | flops 536870912 | bytes 6291456 | tf_op jit(solution)/shard_map/pallas_call | solution.py:228
  41.1 0.2 collective-permute-start.13
  41.3 2.6 %shard_map.89 = (bf16[4096,512]{1,0:T(8,128)(2,1)}, f32[1,128]{1,0:T(1,128)S(1)}) custom-call(s32[1]{0:T(128)} %bitcast.me_ref, f32[128,128]{1,0:T(8,128)S(1)} %get-tuple-element.24.label_ref, f32[16,8,128]{2,1,0:T(8,128)S(1)} %all_to_all.5.stats_ref, f32[128,512]{1,0:T(8,128)S(1)} %get-tuple-element.31.teacher_ref, ...), custom_call_target="tpu_custom_call" | custom-call | flops 536870912 | bytes 5242880 | tf_op jit(solution)/shard_map/pallas_call | solution.py:270
  43.9 2.0 %collective-permute-start.12 = (bf16[16,4096]{1,0:T(8,128)(2,1)S(1)}, bf16[16,4096]{1,0:T(8,128)(2,1)S(1)}, u32[]{:S(2)}, u32[]{:S(2)}) collective-permute-start(bf16[16,4096]{1,0:T(8,128)(2,1)S(1)} %get-tuple-element.41), channel_id=1, source_target_pairs={{0,2},{1,3},{2,0},{3,1},{4,6},{5,7},{6,4},{7,5},{8,10},{9,11},{10,... | collective-permute-start | bytes 393224 | tf_op jit(solution)/shard_map/ppermute | solution.py:287
  45.9 0.3 collective-permute-done.13
  46.2 0.8 %collective-permute-start.14 = (bf16[8,4096]{1,0:T(8,128)(2,1)S(1)}, bf16[8,4096]{1,0:T(8,128)(2,1)S(1)}, u32[]{:S(2)}, u32[]{:S(2)}) collective-permute-start(bf16[8,4096]{1,0:T(8,128)(2,1)S(1)} %get-tuple-element.43), channel_id=1, source_target_pairs={{0,8},{1,9},{2,10},{3,11},{4,12},{5,13},{6,14},{7,15},{8,0},{9,1},... | collective-permute-start | bytes 196616 | tf_op jit(solution)/shard_map/ppermute | solution.py:287
  47.0 2.3 %collective-permute-start.15 = (bf16[8,4096]{1,0:T(8,128)(2,1)S(1)}, bf16[8,4096]{1,0:T(8,128)(2,1)S(1)}, u32[]{:S(2)}, u32[]{:S(2)}) collective-permute-start(bf16[8,4096]{1,0:T(8,128)(2,1)S(1)} %get-tuple-element.44), channel_id=1, source_target_pairs={{0,12},{1,13},{2,14},{3,15},{4,8},{5,9},{6,10},{7,11},{8,4},{9,5},... | collective-permute-start | bytes 196616 | tf_op jit(solution)/shard_map/ppermute | solution.py:287
  49.3 0.6 %collective-permute-start.16 = (bf16[8,4096]{1,0:T(8,128)(2,1)S(1)}, bf16[8,4096]{1,0:T(8,128)(2,1)S(1)}, u32[]{:S(2)}, u32[]{:S(2)}) collective-permute-start(bf16[8,4096]{1,0:T(8,128)(2,1)S(1)} %slice.32), channel_id=1, source_target_pairs={{0,4},{1,5},{2,6},{3,7},{4,0},{5,1},{6,2},{7,3},{8,12},{9,13},{10,... | collective-permute-start | bytes 196616 | tf_op jit(solution)/shard_map/ppermute | solution.py:287
  50.0 0.5 slice_bitcast_fusion
  50.5 3.0 %collective-permute-done.14 = bf16[8,4096]{1,0:T(8,128)(2,1)S(1)} collective-permute-done((bf16[8,4096]{1,0:T(8,128)(2,1)S(1)}, bf16[8,4096]{1,0:T(8,128)(2,1)S(1)}, u32[]{:S(2)}, u32[]{:S(2)}) %collective-permute-start.14) | collective-permute-done | bytes 65568 | tf_op jit(solution)/shard_map/ppermute | solution.py:287
  53.4 0.7 %collective-permute-done.16 = bf16[8,4096]{1,0:T(8,128)(2,1)S(1)} collective-permute-done((bf16[8,4096]{1,0:T(8,128)(2,1)S(1)}, bf16[8,4096]{1,0:T(8,128)(2,1)S(1)}, u32[]{:S(2)}, u32[]{:S(2)}) %collective-permute-start.16) | collective-permute-done | bytes 65568 | tf_op jit(solution)/shard_map/ppermute | solution.py:287
  54.1 0.7 %fusion.1 = f32[8,4096]{1,0:T(8,128)} fusion(f32[16,4096]{1,0:T(8,128)S(1)} %convert_add_fusion, bf16[8,4096]{1,0:T(8,128)(2,1)S(1)} %collective-permute-done.16, bf16[8,4096]{1,0:T(8,128)(2,1)S(1)} %collective-permute-done.15, bf16[8,4096]{1,0:T(8,128)(2,1)S(1)} %collective-permute-done.14), kind=kLoop, calls=%fused_computation.6 | loop fusion | flops 196608 | bytes 458752 | tf_op jit(solution)/shard_map/add | solution.py:353
  (20 shorter events, 0.3 us)
Async XLA Ops:
  0.6 12.1 %collective-permute-start.3 = (bf16[8,4096]{1,0:T(8,128)(2,1)}, bf16[8,4096]{1,0:T(8,128)(2,1)S(1)}, u32[]{:S(2)}, u32[]{:S(2)}) collective-permute-start(bf16[8,4096]{1,0:T(8,128)(2,1)} %teacher_ref.1), channel_id=1, source_target_pairs={{0,8},{1,9},{2,10},{3,11},{4,12},{5,13},{6,14},{7,15},{8,0},{9,1},... | collective-permute-start | bytes 196616 | tf_op jit(solution)/shard_map/ppermute | solution.py:287
  4.7 8.0 %collective-permute-start.4 = (bf16[8,4096]{1,0:T(8,128)(2,1)}, bf16[8,4096]{1,0:T(8,128)(2,1)S(1)}, u32[]{:S(2)}, u32[]{:S(2)}) collective-permute-start(bf16[8,4096]{1,0:T(8,128)(2,1)} %student_ref.1), channel_id=1, source_target_pairs={{0,8},{1,9},{2,10},{3,11},{4,12},{5,13},{6,14},{7,15},{8,0},{9,1},... | collective-permute-start | bytes 196616 | tf_op jit(solution)/shard_map/ppermute | solution.py:287
  5.7 8.2 %collective-permute-start.1 = (bf16[8,8192]{1,0:T(8,128)(2,1)S(1)}, bf16[8,8192]{1,0:T(8,128)(2,1)S(1)}, u32[]{:S(2)}, u32[]{:S(2)}) collective-permute-start(bf16[8,8192]{1,0:T(8,128)(2,1)S(1)} %shard_map.85), channel_id=1, source_target_pairs={{0,4},{1,5},{2,6},{3,7},{4,0},{5,1},{6,2},{7,3},{8,12},{9,13},{10,... | collective-permute-start | bytes 393224 | tf_op jit(solution)/shard_map/ppermute | solution.py:287
  7.6 11.8 %collective-permute-start = (bf16[8,8192]{1,0:T(8,128)(2,1)S(1)}, bf16[8,8192]{1,0:T(8,128)(2,1)S(1)}, u32[]{:S(2)}, u32[]{:S(2)}) collective-permute-start(bf16[8,8192]{1,0:T(8,128)(2,1)S(1)} %shard_map.85), channel_id=1, source_target_pairs={{0,2},{1,3},{2,0},{3,1},{4,6},{5,7},{6,4},{7,5},{8,10},{9,11},{10,... | collective-permute-start | bytes 393224 | tf_op jit(solution)/shard_map/ppermute | solution.py:287
  12.8 5.0 %collective-permute-start.6 = (bf16[8,8192]{1,0:T(8,128)(2,1)S(1)}, bf16[8,8192]{1,0:T(8,128)(2,1)S(1)}, u32[]{:S(2)}, u32[]{:S(2)}) collective-permute-start(bf16[8,8192]{1,0:T(8,128)(2,1)S(1)} %pad_maximum_fusion.1), channel_id=1, source_target_pairs={{0,4},{1,5},{2,6},{3,7},{4,0},{5,1},{6,2},{7,3},{8,12},{9,13},{10,... | collective-permute-start | bytes 393224 | tf_op jit(solution)/shard_map/ppermute | solution.py:287
  13.3 6.1 %collective-permute-start.5 = (bf16[8,8192]{1,0:T(8,128)(2,1)S(1)}, bf16[8,8192]{1,0:T(8,128)(2,1)S(1)}, u32[]{:S(2)}, u32[]{:S(2)}) collective-permute-start(bf16[8,8192]{1,0:T(8,128)(2,1)S(1)} %pad_maximum_fusion.1), channel_id=1, source_target_pairs={{0,2},{1,3},{2,0},{3,1},{4,6},{5,7},{6,4},{7,5},{8,10},{9,11},{10,... | collective-permute-start | bytes 393224 | tf_op jit(solution)/shard_map/ppermute | solution.py:287
  13.9 25.4 %collective-permute-start.11 = (bf16[512,4096]{1,0:T(8,128)(2,1)S(1)}, bf16[512,4096]{1,0:T(8,128)(2,1)S(1)}, u32[]{:S(2)}, u32[]{:S(2)}) collective-permute-start(bf16[512,4096]{1,0:T(8,128)(2,1)S(1)} %get-tuple-element.34.turned_ref), channel_id=1, source_target_pairs={{0,1},{1,0},{2,3},{3,2},{4,5},{5,4},{6,7},{7,6},{8,9},{9,8},{10,11... | collective-permute-start | bytes 12582920 | tf_op jit(solution)/shard_map/ppermute | solution.py:287
  14.0 8.2 %collective-permute-start.2 = (bf16[8,8192]{1,0:T(8,128)(2,1)S(1)}, bf16[8,8192]{1,0:T(8,128)(2,1)S(1)}, u32[]{:S(2)}, u32[]{:S(2)}) collective-permute-start(bf16[8,8192]{1,0:T(8,128)(2,1)S(1)} %collective-permute-done.1), channel_id=1, source_target_pairs={{0,2},{1,3},{2,0},{3,1},{4,6},{5,7},{6,4},{7,5},{8,10},{9,11},{10,... | collective-permute-start | bytes 393224 | tf_op jit(solution)/shard_map/ppermute | solution.py:287
  17.8 6.1 %collective-permute-start.7 = (bf16[8,8192]{1,0:T(8,128)(2,1)S(1)}, bf16[8,8192]{1,0:T(8,128)(2,1)S(1)}, u32[]{:S(2)}, u32[]{:S(2)}) collective-permute-start(bf16[8,8192]{1,0:T(8,128)(2,1)S(1)} %collective-permute-done.6), channel_id=1, source_target_pairs={{0,2},{1,3},{2,0},{3,1},{4,6},{5,7},{6,4},{7,5},{8,10},{9,11},{10,... | collective-permute-start | bytes 393224 | tf_op jit(solution)/shard_map/ppermute | solution.py:287
  22.2 2.0 %collective-permute-start.8 = (bf16[32,8192]{1,0:T(8,128)(2,1)S(1)}, bf16[32,8192]{1,0:T(8,128)(2,1)S(1)}, u32[]{:S(2)}, u32[]{:S(2)}) collective-permute-start(bf16[32,8192]{1,0:T(8,128)(2,1)S(1)} %pad_maximum_fusion.refs_0_), channel_id=1, source_target_pairs={{0,1},{1,0},{2,3},{3,2},{4,5},{5,4},{6,7},{7,6},{8,9},{9,8},{10,11... | collective-permute-start | bytes 1572872 | tf_op jit(solution)/shard_map/ppermute | solution.py:287
  23.9 2.0 %collective-permute-start.9 = (bf16[32,8192]{1,0:T(8,128)(2,1)S(1)}, bf16[32,8192]{1,0:T(8,128)(2,1)S(1)}, u32[]{:S(2)}, u32[]{:S(2)}) collective-permute-start(bf16[32,8192]{1,0:T(8,128)(2,1)S(1)} %constant_dynamic-update-slice_fusion.refs_1_), channel_id=1, source_target_pairs={{0,1},{1,0},{2,3},{3,2},{4,5},{5,4},{6,7},{7,6},{8,9},{9,8},{10,11... | collective-permute-start | bytes 1572872 | tf_op jit(solution)/shard_map/ppermute | solution.py:287
  27.5 11.9 %collective-permute-start.10 = (f32[2,64,512]{2,1,0:T(8,128)S(1)}, f32[2,64,512]{2,1,0:T(8,128)S(1)}, u32[]{:S(2)}, u32[]{:S(2)}) collective-permute-start(f32[2,64,512]{2,1,0:T(8,128)S(1)} %get-tuple-element.33), channel_id=1, source_target_pairs={{0,1},{1,0},{2,3},{3,2},{4,5},{5,4},{6,7},{7,6},{8,9},{9,8},{10,11... | collective-permute-start | bytes 786440 | tf_op jit(solution)/shard_map/ppermute | solution.py:287
  41.1 5.0 %collective-permute-start.13 = (bf16[16,4096]{1,0:T(8,128)(2,1)S(1)}, bf16[16,4096]{1,0:T(8,128)(2,1)S(1)}, u32[]{:S(2)}, u32[]{:S(2)}) collective-permute-start(bf16[16,4096]{1,0:T(8,128)(2,1)S(1)} %get-tuple-element.35), channel_id=1, source_target_pairs={{0,2},{1,3},{2,0},{3,1},{4,6},{5,7},{6,4},{7,5},{8,10},{9,11},{10,... | collective-permute-start | bytes 393224 | tf_op jit(solution)/shard_map/ppermute | solution.py:287
  43.9 5.4 %collective-permute-start.12 = (bf16[16,4096]{1,0:T(8,128)(2,1)S(1)}, bf16[16,4096]{1,0:T(8,128)(2,1)S(1)}, u32[]{:S(2)}, u32[]{:S(2)}) collective-permute-start(bf16[16,4096]{1,0:T(8,128)(2,1)S(1)} %get-tuple-element.41), channel_id=1, source_target_pairs={{0,2},{1,3},{2,0},{3,1},{4,6},{5,7},{6,4},{7,5},{8,10},{9,11},{10,... | collective-permute-start | bytes 393224 | tf_op jit(solution)/shard_map/ppermute | solution.py:287
  46.2 7.2 %collective-permute-start.14 = (bf16[8,4096]{1,0:T(8,128)(2,1)S(1)}, bf16[8,4096]{1,0:T(8,128)(2,1)S(1)}, u32[]{:S(2)}, u32[]{:S(2)}) collective-permute-start(bf16[8,4096]{1,0:T(8,128)(2,1)S(1)} %get-tuple-element.43), channel_id=1, source_target_pairs={{0,8},{1,9},{2,10},{3,11},{4,12},{5,13},{6,14},{7,15},{8,0},{9,1},... | collective-permute-start | bytes 196616 | tf_op jit(solution)/shard_map/ppermute | solution.py:287
  47.0 6.4 %collective-permute-start.15 = (bf16[8,4096]{1,0:T(8,128)(2,1)S(1)}, bf16[8,4096]{1,0:T(8,128)(2,1)S(1)}, u32[]{:S(2)}, u32[]{:S(2)}) collective-permute-start(bf16[8,4096]{1,0:T(8,128)(2,1)S(1)} %get-tuple-element.44), channel_id=1, source_target_pairs={{0,12},{1,13},{2,14},{3,15},{4,8},{5,9},{6,10},{7,11},{8,4},{9,5},... | collective-permute-start | bytes 196616 | tf_op jit(solution)/shard_map/ppermute | solution.py:287
  49.3 4.7 %collective-permute-start.16 = (bf16[8,4096]{1,0:T(8,128)(2,1)S(1)}, bf16[8,4096]{1,0:T(8,128)(2,1)S(1)}, u32[]{:S(2)}, u32[]{:S(2)}) collective-permute-start(bf16[8,4096]{1,0:T(8,128)(2,1)S(1)} %slice.32), channel_id=1, source_target_pairs={{0,4},{1,5},{2,6},{3,7},{4,0},{5,1},{6,2},{7,3},{8,12},{9,13},{10,... | collective-permute-start | bytes 196616 | tf_op jit(solution)/shard_map/ppermute | solution.py:287

commit v6 on v5

--- a/solution.py
+++ b/solution.py
@@ -319,23 +319,18 @@
 def gather_rows(teacher_rows, student_rows, n, fetch):
     join = lambda pair: jnp.concatenate(pair, axis=1)
     stack = lambda *parts: jnp.concatenate(parts, axis=0)
-    depth = teacher_rows.shape[1]
     far_teacher = swap(teacher_rows, 8, n)
     rows = join_rows(teacher_rows, student_rows)
     far_student = swap(student_rows, 8, n)
     near, side = swap(rows, 4, n), swap(rows, 2, n)
-    fetched = fetch(rows)
-    far = join((far_teacher, far_student))
-    far_ready = after(far, *fetched)
-    near_ready = near
-    far, near = far_ready, near_ready
+    *fetched, turned = fetch(rows)
+    far = after(join((far_teacher, far_student)), *fetched, turned)
     far_near = swap(far, 4, n)
-    *fetched, turned = fetched
-    other_head = swap(after(turned, far, near), 1, n)
+    other_head = swap(after(turned, far), 1, n)
     far_side = swap(far, 2, n)
-    near_side = swap(near, 2, n)
+    near_side = swap(side, 4, n)
     far_near_side = swap(far_near, 2, n)
-    held = [stack(rows, side, near, near_side), stack(far, far_side, far_near, far_near_side)]
+    held = [stack(rows, side, near, near_side, far, far_side), stack(far_near, far_near_side)]
     return held + [swap(piece, 1, n) for piece in held], fetched, (turned, other_head)
 
 

time: 55 us -> 53.4 us (0.971)
  blocking collectives: 11.7 us -> 10.7 us
  starting transfers between devices: 17 us -> 16.4 us
    all_to_all x1, blocking collectives: 11.7 us -> 10.7 us  [per_device(): stats = lax.all_to_all(stats, 'dp', 0, 0)]
    ppermute x17, starting transfers between devices: 17 us -> 16.4 us  [swap(): return lax.ppermute(value, 'dp', [(i, i ^ distance) for i in range(n)])]
  transfers between devices with their start and end apart: 17 -> 17, of which waited for: 9 -> 7; matrix products, arithmetic and copies ran while one was open for 1% -> 1% of each run, Pallas kernels for 16% -> 16%
where the time goes in v6:
time: 53.4 us; the launch traced here: 53.2 us
  starting transfers between devices  16.4 us (31%)
  waiting for transfers between devices  13.5 us (25%)
  blocking collectives  10.7 us (20%)
  Pallas kernels  10.5 us (20%)
  between operations  0.8 us (1%)
  other arithmetic  0.75 us (1%)
  local copies, waits for them, and re-layouts  0.61 us (1%)
    ppermute x17, starting transfers between devices, swap(): return lax.ppermute(value, 'dp', [(i, i ^ distance) for i in range(n)])  16.4 us
    ppermute x17, waiting for transfers between devices, swap(): return lax.ppermute(value, 'dp', [(i, i ^ distance) for i in range(n)])  13.5 us
    all_to_all x1, blocking collectives, per_device(): stats = lax.all_to_all(stats, 'dp', 0, 0)  10.7 us
    pallas_call x1, Pallas kernels, prepare(): pl.pallas_call(functools.partial(prepare_kernel, rows_local, tuned), in_s...  3.6 us
    pallas_call x1, Pallas kernels, head_gradient(): pl.pallas_call(functools.partial(head_kernel, rows_local, tuned), in_spec...  2.59 us
    pallas_call x1, Pallas kernels, gradient(): pl.pallas_call(functools.partial(grad_kernel if tuned else whole_grad_ker...  1.76 us
    pallas_call x1, Pallas kernels, logits(): pl.pallas_call(functools.partial(logits_kernel, rows_local, tuned, len(hi...  1.62 us
  transfers between devices with their start and end apart: 17, of which 7 were waited for; matrix products, arithmetic and copies ran while one was open for 1% of the time, Pallas kernels for 16%

profile of v6, /device:TPU:0, one launch (start us, length us, event | category | flops | bytes accessed | tf_op | source)
XLA Modules:
  0.0 53.2 jit_solution(17563270761600912601)
XLA Ops:
  0.6 4.1 %collective-permute-start.3 = (bf16[8,4096]{1,0:T(8,128)(2,1)}, bf16[8,4096]{1,0:T(8,128)(2,1)S(1)}, u32[]{:S(2)}, u32[]{:S(2)}) collective-permute-start(bf16[8,4096]{1,0:T(8,128)(2,1)} %teacher_ref.1), channel_id=1, source_target_pairs={{0,8},{1,9},{2,10},{3,11},{4,12},{5,13},{6,14},{7,15},{8,0},{9,1},... | collective-permute-start | bytes 196616 | tf_op jit(solution)/shard_map/ppermute | solution.py:287
  4.7 0.1 collective-permute-start.4
  4.8 0.9 %shard_map.85 = bf16[8,8192]{1,0:T(8,128)(2,1)S(1)} custom-call(bf16[8,4096]{1,0:T(8,128)(2,1)} %teacher_ref.1, bf16[8,4096]{1,0:T(8,128)(2,1)} %student_ref.1), custom_call_target="tpu_custom_call" | custom-call | bytes 262144 | tf_op jit(solution)/shard_map/pallas_call | solution.py:308
  5.7 1.9 %collective-permute-start.1 = (bf16[8,8192]{1,0:T(8,128)(2,1)S(1)}, bf16[8,8192]{1,0:T(8,128)(2,1)S(1)}, u32[]{:S(2)}, u32[]{:S(2)}) collective-permute-start(bf16[8,8192]{1,0:T(8,128)(2,1)S(1)} %shard_map.85), channel_id=1, source_target_pairs={{0,4},{1,5},{2,6},{3,7},{4,0},{5,1},{6,2},{7,3},{8,12},{9,13},{10,... | collective-permute-start | bytes 393224 | tf_op jit(solution)/shard_map/ppermute | solution.py:287
  7.6 1.5 %collective-permute-start = (bf16[8,8192]{1,0:T(8,128)(2,1)S(1)}, bf16[8,8192]{1,0:T(8,128)(2,1)S(1)}, u32[]{:S(2)}, u32[]{:S(2)}) collective-permute-start(bf16[8,8192]{1,0:T(8,128)(2,1)S(1)} %shard_map.85), channel_id=1, source_target_pairs={{0,2},{1,3},{2,0},{3,1},{4,6},{5,7},{6,4},{7,5},{8,10},{9,11},{10,... | collective-permute-start | bytes 393224 | tf_op jit(solution)/shard_map/ppermute | solution.py:287
  9.1 3.6 %shard_map.86 = (bf16[4096,512]{1,0:T(8,128)(2,1)S(1)}, bf16[4096,512]{1,0:T(8,128)(2,1)S(1)}, bf16[128,128]{1,0:T(8,128)(2,1)S(1)}, f32[128,128]{1,0:T(8,128)S(1)}, bf16[512,4096]{1,0:T(8,128)(2,1)S(1)}) custom-call(s32[1]{0:T(128)} %bitcast.me_ref, s32[1,128]{1,0:T(1,128)} %bitcast.5, s32[1,128]{1,0:T(1,128)} %bitcast.6, bf16[4096,512]{1,0:T(8,128)(2,1)} %refs_0_.1, ...), custom_call_target="tpu_custom_call" | custom-call | bytes 16777216 | tf_op jit(solution)/shard_map/pallas_call | solution.py:78
  12.8 0.0 collective-permute-done.3
  12.8 0.0 collective-permute-done.4
  12.8 0.5 collective-permute-start.6
  13.3 0.6 %collective-permute-start.5 = (bf16[8,8192]{1,0:T(8,128)(2,1)S(1)}, bf16[8,8192]{1,0:T(8,128)(2,1)S(1)}, u32[]{:S(2)}, u32[]{:S(2)}) collective-permute-start(bf16[8,8192]{1,0:T(8,128)(2,1)S(1)} %pad_maximum_fusion), channel_id=1, source_target_pairs={{0,2},{1,3},{2,0},{3,1},{4,6},{5,7},{6,4},{7,5},{8,10},{9,11},{10,... | collective-permute-start | bytes 393224 | tf_op jit(solution)/shard_map/ppermute | solution.py:287
  13.9 1.5 %collective-permute-start.2 = (bf16[8,8192]{1,0:T(8,128)(2,1)S(1)}, bf16[8,8192]{1,0:T(8,128)(2,1)S(1)}, u32[]{:S(2)}, u32[]{:S(2)}) collective-permute-start(bf16[8,8192]{1,0:T(8,128)(2,1)S(1)} %collective-permute-done), channel_id=1, source_target_pairs={{0,4},{1,5},{2,6},{3,7},{4,0},{5,1},{6,2},{7,3},{8,12},{9,13},{10,... | collective-permute-start | bytes 393224 | tf_op jit(solution)/shard_map/ppermute | solution.py:287
  15.4 3.3 %collective-permute-done.6 = bf16[8,8192]{1,0:T(8,128)(2,1)S(1)} collective-permute-done((bf16[8,8192]{1,0:T(8,128)(2,1)S(1)}, bf16[8,8192]{1,0:T(8,128)(2,1)S(1)}, u32[]{:S(2)}, u32[]{:S(2)}) %collective-permute-start.6) | collective-permute-done | bytes 131104 | tf_op jit(solution)/shard_map/ppermute | solution.py:287
  18.7 1.9 %collective-permute-done.2 = bf16[8,8192]{1,0:T(8,128)(2,1)S(1)} collective-permute-done((bf16[8,8192]{1,0:T(8,128)(2,1)S(1)}, bf16[8,8192]{1,0:T(8,128)(2,1)S(1)}, u32[]{:S(2)}, u32[]{:S(2)}) %collective-permute-start.2) | collective-permute-done | bytes 131104 | tf_op jit(solution)/shard_map/ppermute | solution.py:287
  20.7 0.1 collective-permute-start.8
  20.8 2.9 %collective-permute-done.7 = bf16[8,8192]{1,0:T(8,128)(2,1)S(1)} collective-permute-done((bf16[8,8192]{1,0:T(8,128)(2,1)S(1)}, bf16[8,8192]{1,0:T(8,128)(2,1)S(1)}, u32[]{:S(2)}, u32[]{:S(2)}) %collective-permute-start.7) | collective-permute-done | bytes 131104 | tf_op jit(solution)/shard_map/ppermute | solution.py:287
  23.7 0.1 collective-permute-start.9
  23.8 1.5 %collective-permute-done.9.refs_3_ = bf16[16,8192]{1,0:T(8,128)(2,1)S(1)} collective-permute-done((bf16[16,8192]{1,0:T(8,128)(2,1)S(1)}, bf16[16,8192]{1,0:T(8,128)(2,1)S(1)}, u32[]{:S(2)}, u32[]{:S(2)}) %collective-permute-start.9) | collective-permute-done | bytes 262176 | tf_op jit(solution)/shard_map/ppermute | solution.py:287
  25.3 1.6 %shard_map.87 = (f32[128,512]{1,0:T(8,128)S(1)}, f32[128,512]{1,0:T(8,128)S(1)}, f32[16,8,128]{2,1,0:T(8,128)S(1)}, f32[2,64,512]{2,1,0:T(8,128)S(1)}) custom-call(s32[1]{0:T(128)} %bitcast.me_ref, bf16[128,128]{1,0:T(8,128)(2,1)S(1)} %get-tuple-element.25.pick_ref, f32[128,128]{1,0:T(8,128)S(1)} %get-tuple-element.24.label_ref, ...), custom_call_target="tpu_custom_call" | custom-call | flops 1073741824 | bytes 10485760 | tf_op jit(solution)/shard_map/pallas_call | solution.py:142
  26.9 0.2 collective-permute-start.10
  27.1 10.7 %all_to_all.5.stats_ref = f32[16,8,128]{2,1,0:T(8,128)S(1)} all-to-all(f32[16,8,128]{2,1,0:T(8,128)S(1)} %get-tuple-element.30), channel_id=1, replica_groups=mesh['groups'=2,'dp'=16] {'dp'}, dimensions={0} | all-to-all | bytes 131072 | tf_op jit(solution)/shard_map/all_to_all | solution.py:368
  37.8 1.8 %shard_map.88 = (f32[16,4096]{1,0:T(8,128)S(1)}, bf16[16,4096]{1,0:T(8,128)(2,1)S(1)}, f32[16,4096]{1,0:T(8,128)S(1)}, bf16[16,4096]{1,0:T(8,128)(2,1)S(1)}) custom-call(s32[1]{0:T(128)} %bitcast.me_ref, f32[128,128]{1,0:T(8,128)S(1)} %get-tuple-element.24.label_ref, f32[16,8,128]{2,1,0:T(8,128)S(1)} %all_to_all.5.stats_ref, ...), custom_call_target="tpu_custom_call" | custom-call | flops 536870912 | bytes 6291456 | tf_op jit(solution)/shard_map/pallas_call | solution.py:228
  39.5 0.2 collective-permute-start.13
  39.7 2.6 %shard_map.89 = (bf16[4096,512]{1,0:T(8,128)(2,1)}, f32[1,128]{1,0:T(1,128)S(1)}) custom-call(s32[1]{0:T(128)} %bitcast.me_ref, f32[128,128]{1,0:T(8,128)S(1)} %get-tuple-element.24.label_ref, f32[16,8,128]{2,1,0:T(8,128)S(1)} %all_to_all.5.stats_ref, f32[128,512]{1,0:T(8,128)S(1)} %get-tuple-element.31.teacher_ref, ...), custom_call_target="tpu_custom_call" | custom-call | flops 536870912 | bytes 5242880 | tf_op jit(solution)/shard_map/pallas_call | solution.py:270
  42.3 2.0 %collective-permute-start.12 = (bf16[16,4096]{1,0:T(8,128)(2,1)S(1)}, bf16[16,4096]{1,0:T(8,128)(2,1)S(1)}, u32[]{:S(2)}, u32[]{:S(2)}) collective-permute-start(bf16[16,4096]{1,0:T(8,128)(2,1)S(1)} %get-tuple-element.41), channel_id=1, source_target_pairs={{0,2},{1,3},{2,0},{3,1},{4,6},{5,7},{6,4},{7,5},{8,10},{9,11},{10,... | collective-permute-start | bytes 393224 | tf_op jit(solution)/shard_map/ppermute | solution.py:287
  44.3 0.3 collective-permute-done.13
  44.6 0.8 %collective-permute-start.14 = (bf16[8,4096]{1,0:T(8,128)(2,1)S(1)}, bf16[8,4096]{1,0:T(8,128)(2,1)S(1)}, u32[]{:S(2)}, u32[]{:S(2)}) collective-permute-start(bf16[8,4096]{1,0:T(8,128)(2,1)S(1)} %get-tuple-element.43), channel_id=1, source_target_pairs={{0,8},{1,9},{2,10},{3,11},{4,12},{5,13},{6,14},{7,15},{8,0},{9,1},... | collective-permute-start | bytes 196616 | tf_op jit(solution)/shard_map/ppermute | solution.py:287
  45.5 2.3 %collective-permute-start.15 = (bf16[8,4096]{1,0:T(8,128)(2,1)S(1)}, bf16[8,4096]{1,0:T(8,128)(2,1)S(1)}, u32[]{:S(2)}, u32[]{:S(2)}) collective-permute-start(bf16[8,4096]{1,0:T(8,128)(2,1)S(1)} %get-tuple-element.44), channel_id=1, source_target_pairs={{0,12},{1,13},{2,14},{3,15},{4,8},{5,9},{6,10},{7,11},{8,4},{9,5},... | collective-permute-start | bytes 196616 | tf_op jit(solution)/shard_map/ppermute | solution.py:287
  47.8 0.6 %collective-permute-start.16 = (bf16[8,4096]{1,0:T(8,128)(2,1)S(1)}, bf16[8,4096]{1,0:T(8,128)(2,1)S(1)}, u32[]{:S(2)}, u32[]{:S(2)}) collective-permute-start(bf16[8,4096]{1,0:T(8,128)(2,1)S(1)} %slice.32), channel_id=1, source_target_pairs={{0,4},{1,5},{2,6},{3,7},{4,0},{5,1},{6,2},{7,3},{8,12},{9,13},{10,... | collective-permute-start | bytes 196616 | tf_op jit(solution)/shard_map/ppermute | solution.py:287
  48.4 0.5 slice_bitcast_fusion
  48.9 3.0 %collective-permute-done.14 = bf16[8,4096]{1,0:T(8,128)(2,1)S(1)} collective-permute-done((bf16[8,4096]{1,0:T(8,128)(2,1)S(1)}, bf16[8,4096]{1,0:T(8,128)(2,1)S(1)}, u32[]{:S(2)}, u32[]{:S(2)}) %collective-permute-start.14) | collective-permute-done | bytes 65568 | tf_op jit(solution)/shard_map/ppermute | solution.py:287
  51.9 0.7 %collective-permute-done.16 = bf16[8,4096]{1,0:T(8,128)(2,1)S(1)} collective-permute-done((bf16[8,4096]{1,0:T(8,128)(2,1)S(1)}, bf16[8,4096]{1,0:T(8,128)(2,1)S(1)}, u32[]{:S(2)}, u32[]{:S(2)}) %collective-permute-start.16) | collective-permute-done | bytes 65568 | tf_op jit(solution)/shard_map/ppermute | solution.py:287
  52.5 0.7 %fusion.1 = f32[8,4096]{1,0:T(8,128)} fusion(f32[16,4096]{1,0:T(8,128)S(1)} %convert_add_fusion, bf16[8,4096]{1,0:T(8,128)(2,1)S(1)} %collective-permute-done.16, bf16[8,4096]{1,0:T(8,128)(2,1)S(1)} %collective-permute-done.15, bf16[8,4096]{1,0:T(8,128)(2,1)S(1)} %collective-permute-done.14), kind=kLoop, calls=%fused_computation.5 | loop fusion | flops 196608 | bytes 458752 | tf_op jit(solution)/shard_map/add | solution.py:348
  (23 shorter events, 0.2 us)
Async XLA Ops:
  0.6 12.1 %collective-permute-start.3 = (bf16[8,4096]{1,0:T(8,128)(2,1)}, bf16[8,4096]{1,0:T(8,128)(2,1)S(1)}, u32[]{:S(2)}, u32[]{:S(2)}) collective-permute-start(bf16[8,4096]{1,0:T(8,128)(2,1)} %teacher_ref.1), channel_id=1, source_target_pairs={{0,8},{1,9},{2,10},{3,11},{4,12},{5,13},{6,14},{7,15},{8,0},{9,1},... | collective-permute-start | bytes 196616 | tf_op jit(solution)/shard_map/ppermute | solution.py:287
  4.7 8.0 %collective-permute-start.4 = (bf16[8,4096]{1,0:T(8,128)(2,1)}, bf16[8,4096]{1,0:T(8,128)(2,1)S(1)}, u32[]{:S(2)}, u32[]{:S(2)}) collective-permute-start(bf16[8,4096]{1,0:T(8,128)(2,1)} %student_ref.1), channel_id=1, source_target_pairs={{0,8},{1,9},{2,10},{3,11},{4,12},{5,13},{6,14},{7,15},{8,0},{9,1},... | collective-permute-start | bytes 196616 | tf_op jit(solution)/shard_map/ppermute | solution.py:287
  5.7 9.7 %collective-permute-start.1 = (bf16[8,8192]{1,0:T(8,128)(2,1)S(1)}, bf16[8,8192]{1,0:T(8,128)(2,1)S(1)}, u32[]{:S(2)}, u32[]{:S(2)}) collective-permute-start(bf16[8,8192]{1,0:T(8,128)(2,1)S(1)} %shard_map.85), channel_id=1, source_target_pairs={{0,4},{1,5},{2,6},{3,7},{4,0},{5,1},{6,2},{7,3},{8,12},{9,13},{10,... | collective-permute-start | bytes 393224 | tf_op jit(solution)/shard_map/ppermute | solution.py:287
  7.6 6.3 %collective-permute-start = (bf16[8,8192]{1,0:T(8,128)(2,1)S(1)}, bf16[8,8192]{1,0:T(8,128)(2,1)S(1)}, u32[]{:S(2)}, u32[]{:S(2)}) collective-permute-start(bf16[8,8192]{1,0:T(8,128)(2,1)S(1)} %shard_map.85), channel_id=1, source_target_pairs={{0,2},{1,3},{2,0},{3,1},{4,6},{5,7},{6,4},{7,5},{8,10},{9,11},{10,... | collective-permute-start | bytes 393224 | tf_op jit(solution)/shard_map/ppermute | solution.py:287
  12.8 5.9 %collective-permute-start.6 = (bf16[8,8192]{1,0:T(8,128)(2,1)S(1)}, bf16[8,8192]{1,0:T(8,128)(2,1)S(1)}, u32[]{:S(2)}, u32[]{:S(2)}) collective-permute-start(bf16[8,8192]{1,0:T(8,128)(2,1)S(1)} %pad_maximum_fusion), channel_id=1, source_target_pairs={{0,4},{1,5},{2,6},{3,7},{4,0},{5,1},{6,2},{7,3},{8,12},{9,13},{10,... | collective-permute-start | bytes 393224 | tf_op jit(solution)/shard_map/ppermute | solution.py:287
  13.3 7.4 %collective-permute-start.5 = (bf16[8,8192]{1,0:T(8,128)(2,1)S(1)}, bf16[8,8192]{1,0:T(8,128)(2,1)S(1)}, u32[]{:S(2)}, u32[]{:S(2)}) collective-permute-start(bf16[8,8192]{1,0:T(8,128)(2,1)S(1)} %pad_maximum_fusion), channel_id=1, source_target_pairs={{0,2},{1,3},{2,0},{3,1},{4,6},{5,7},{6,4},{7,5},{8,10},{9,11},{10,... | collective-permute-start | bytes 393224 | tf_op jit(solution)/shard_map/ppermute | solution.py:287
  13.9 23.9 %collective-permute-start.11 = (bf16[512,4096]{1,0:T(8,128)(2,1)S(1)}, bf16[512,4096]{1,0:T(8,128)(2,1)S(1)}, u32[]{:S(2)}, u32[]{:S(2)}) collective-permute-start(bf16[512,4096]{1,0:T(8,128)(2,1)S(1)} %get-tuple-element.34.turned_ref), channel_id=1, source_target_pairs={{0,1},{1,0},{2,3},{3,2},{4,5},{5,4},{6,7},{7,6},{8,9},{9,8},{10,11... | collective-permute-start | bytes 12582920 | tf_op jit(solution)/shard_map/ppermute | solution.py:287
  13.9 6.7 %collective-permute-start.2 = (bf16[8,8192]{1,0:T(8,128)(2,1)S(1)}, bf16[8,8192]{1,0:T(8,128)(2,1)S(1)}, u32[]{:S(2)}, u32[]{:S(2)}) collective-permute-start(bf16[8,8192]{1,0:T(8,128)(2,1)S(1)} %collective-permute-done), channel_id=1, source_target_pairs={{0,4},{1,5},{2,6},{3,7},{4,0},{5,1},{6,2},{7,3},{8,12},{9,13},{10,... | collective-permute-start | bytes 393224 | tf_op jit(solution)/shard_map/ppermute | solution.py:287
  18.7 5.0 %collective-permute-start.7 = (bf16[8,8192]{1,0:T(8,128)(2,1)S(1)}, bf16[8,8192]{1,0:T(8,128)(2,1)S(1)}, u32[]{:S(2)}, u32[]{:S(2)}) collective-permute-start(bf16[8,8192]{1,0:T(8,128)(2,1)S(1)} %collective-permute-done.6), channel_id=1, source_target_pairs={{0,2},{1,3},{2,0},{3,1},{4,6},{5,7},{6,4},{7,5},{8,10},{9,11},{10,... | collective-permute-start | bytes 393224 | tf_op jit(solution)/shard_map/ppermute | solution.py:287
  20.7 4.6 %collective-permute-start.8 = (bf16[48,8192]{1,0:T(8,128)(2,1)S(1)}, bf16[48,8192]{1,0:T(8,128)(2,1)S(1)}, u32[]{:S(2)}, u32[]{:S(2)}) collective-permute-start(bf16[48,8192]{1,0:T(8,128)(2,1)S(1)} %constant_dynamic-update-slice_fusion.refs_0_), channel_id=1, source_target_pairs={{0,1},{1,0},{2,3},{3,2},{4,5},{5,4},{6,7},{7,6},{8,9},{9,8},{10,11... | collective-permute-start | bytes 2359304 | tf_op jit(solution)/shard_map/ppermute | solution.py:287
  23.7 1.6 %collective-permute-start.9 = (bf16[16,8192]{1,0:T(8,128)(2,1)S(1)}, bf16[16,8192]{1,0:T(8,128)(2,1)S(1)}, u32[]{:S(2)}, u32[]{:S(2)}) collective-permute-start(bf16[16,8192]{1,0:T(8,128)(2,1)S(1)} %constant_dynamic-update-slice_fusion.6.refs_1_), channel_id=1, source_target_pairs={{0,1},{1,0},{2,3},{3,2},{4,5},{5,4},{6,7},{7,6},{8,9},{9,8},{10,11... | collective-permute-start | bytes 786440 | tf_op jit(solution)/shard_map/ppermute | solution.py:287
  26.9 10.9 %collective-permute-start.10 = (f32[2,64,512]{2,1,0:T(8,128)S(1)}, f32[2,64,512]{2,1,0:T(8,128)S(1)}, u32[]{:S(2)}, u32[]{:S(2)}) collective-permute-start(f32[2,64,512]{2,1,0:T(8,128)S(1)} %get-tuple-element.33), channel_id=1, source_target_pairs={{0,1},{1,0},{2,3},{3,2},{4,5},{5,4},{6,7},{7,6},{8,9},{9,8},{10,11... | collective-permute-start | bytes 786440 | tf_op jit(solution)/shard_map/ppermute | solution.py:287
  39.5 5.0 %collective-permute-start.13 = (bf16[16,4096]{1,0:T(8,128)(2,1)S(1)}, bf16[16,4096]{1,0:T(8,128)(2,1)S(1)}, u32[]{:S(2)}, u32[]{:S(2)}) collective-permute-start(bf16[16,4096]{1,0:T(8,128)(2,1)S(1)} %get-tuple-element.35), channel_id=1, source_target_pairs={{0,2},{1,3},{2,0},{3,1},{4,6},{5,7},{6,4},{7,5},{8,10},{9,11},{10,... | collective-permute-start | bytes 393224 | tf_op jit(solution)/shard_map/ppermute | solution.py:287
  42.3 5.4 %collective-permute-start.12 = (bf16[16,4096]{1,0:T(8,128)(2,1)S(1)}, bf16[16,4096]{1,0:T(8,128)(2,1)S(1)}, u32[]{:S(2)}, u32[]{:S(2)}) collective-permute-start(bf16[16,4096]{1,0:T(8,128)(2,1)S(1)} %get-tuple-element.41), channel_id=1, source_target_pairs={{0,2},{1,3},{2,0},{3,1},{4,6},{5,7},{6,4},{7,5},{8,10},{9,11},{10,... | collective-permute-start | bytes 393224 | tf_op jit(solution)/shard_map/ppermute | solution.py:287
  44.6 7.2 %collective-permute-start.14 = (bf16[8,4096]{1,0:T(8,128)(2,1)S(1)}, bf16[8,4096]{1,0:T(8,128)(2,1)S(1)}, u32[]{:S(2)}, u32[]{:S(2)}) collective-permute-start(bf16[8,4096]{1,0:T(8,128)(2,1)S(1)} %get-tuple-element.43), channel_id=1, source_target_pairs={{0,8},{1,9},{2,10},{3,11},{4,12},{5,13},{6,14},{7,15},{8,0},{9,1},... | collective-permute-start | bytes 196616 | tf_op jit(solution)/shard_map/ppermute | solution.py:287
  45.5 6.4 %collective-permute-start.15 = (bf16[8,4096]{1,0:T(8,128)(2,1)S(1)}, bf16[8,4096]{1,0:T(8,128)(2,1)S(1)}, u32[]{:S(2)}, u32[]{:S(2)}) collective-permute-start(bf16[8,4096]{1,0:T(8,128)(2,1)S(1)} %get-tuple-element.44), channel_id=1, source_target_pairs={{0,12},{1,13},{2,14},{3,15},{4,8},{5,9},{6,10},{7,11},{8,4},{9,5},... | collective-permute-start | bytes 196616 | tf_op jit(solution)/shard_map/ppermute | solution.py:287
  47.8 4.7 %collective-permute-start.16 = (bf16[8,4096]{1,0:T(8,128)(2,1)S(1)}, bf16[8,4096]{1,0:T(8,128)(2,1)S(1)}, u32[]{:S(2)}, u32[]{:S(2)}) collective-permute-start(bf16[8,4096]{1,0:T(8,128)(2,1)S(1)} %slice.32), channel_id=1, source_target_pairs={{0,4},{1,5},{2,6},{3,7},{4,0},{5,1},{6,2},{7,3},{8,12},{9,13},{10,... | collective-permute-start | bytes 196616 | tf_op jit(solution)/shard_map/ppermute | solution.py:287

commit v7 on v6

--- a/solution.py
+++ b/solution.py
@@ -9,7 +9,7 @@
 
 CE_WEIGHT = 0.5
 VMEM_LIMIT = 28 * 2**20
-STATS = 8
+STATS = 4
 
 
 def held_rows(shape, dim, me, rows_local, tuned):
@@ -119,18 +119,17 @@
     teacher_max = jnp.max(teacher, axis=1, keepdims=True)
     student_max = jnp.max(student, axis=1, keepdims=True)
     teacher_exp = jnp.exp(teacher - teacher_max)
+    teacher_total = jnp.sum(teacher_exp, axis=1, keepdims=True)
+    student_total = jnp.sum(jnp.exp(student - student_max), axis=1, keepdims=True)
     values = (
-        teacher_max,
-        student_max,
-        jnp.sum(teacher_exp, axis=1, keepdims=True),
-        jnp.sum(jnp.exp(student - student_max), axis=1, keepdims=True),
-        jnp.sum(teacher_exp * (teacher - student), axis=1, keepdims=True),
+        teacher_max + jnp.log(teacher_total),
+        student_max + jnp.log(student_total),
+        jnp.sum(teacher_exp * (teacher - student), axis=1, keepdims=True) / teacher_total,
         jnp.sum(jnp.where(is_label, student, 0.0), axis=1, keepdims=True),
     )
     lanes = lax.broadcasted_iota(jnp.int32, (count, count), 1)
     is_row = held_rows((count, count), 0, me, rows_local, tuned) == lanes
     block = [jnp.sum(jnp.where(is_row, value, 0.0), axis=0, keepdims=True) for value in values]
-    block.append(jnp.zeros((STATS - len(block), count), jnp.float32))
     stats_out[...] = jnp.broadcast_to(jnp.concatenate(block, axis=0)[None], stats_out.shape)
 
 
@@ -161,10 +160,10 @@
     label_logit = jnp.zeros((1, count), jnp.float32)
     for d in range(devices):
         weight = jnp.exp(stats_ref[d, 0:2] - top)
-        totals += weight * stats_ref[d, 2:4]
-        cross += weight[0:1] * stats_ref[d, 4:5]
-        label_logit += stats_ref[d, 5:6]
-    return top + jnp.log(totals), totals, cross, label_logit
+        totals += weight
+        cross += weight[0:1] * stats_ref[d, 2:3]
+        label_logit += stats_ref[d, 3:4]
+    return top + jnp.log(totals), cross / totals[0:1], label_logit
 
 
 def logit_gradient(teacher, student, norms, is_row, label):
@@ -199,9 +198,8 @@
         part = jnp.dot(grad, turned_ref[:, k : k + step], preferred_element_type=jnp.float32)
         part += jnp.dot(other, other_ref[:, k : k + step], preferred_element_type=jnp.float32)
         blocks = [part[b * rows_local : (b + 1) * rows_local] for b in range(8)]
-        for j, out in enumerate((near_keep, near_send, far_keep, far_send)):
-            first = (j // 2) * 4 + j % 2
-            out[:, k : k + step] = jnp.concatenate((blocks[first], blocks[first + 2]), axis=0).astype(out.dtype)
+        for out, first, second in ((near_keep, 0, 1), (near_send, 2, 3), (far_keep, 4, 6), (far_send, 5, 7)):
+            out[:, k : k + step] = jnp.concatenate((blocks[first], blocks[second]), axis=0).astype(out.dtype)
 
 
 def whole_grad_kernel(rows_local, me_ref, label_ref, stats_ref, teacher_ref, student_ref, head_ref, out_ref):
@@ -238,12 +236,12 @@
 
 
 def head_kernel(rows_local, tuned, me_ref, label_ref, stats_ref, teacher_ref, student_ref, *refs):
-    *pieces, out_ref, loss_out, held, sems = refs
+    *pieces, out_ref, held, sems = refs
     me = me_ref[0]
     count = student_ref.shape[0]
     lanes = lax.broadcasted_iota(jnp.int32, (count, count), 1)
     is_row = held_rows((count, count), 0, me, rows_local, tuned) == lanes
-    norms, totals, cross, label_logit = merged(stats_ref)
+    norms = merged(stats_ref)[0]
     grad = logit_gradient(teacher_ref[...], student_ref[...], norms, is_row, label_ref[:, 0:1])
     steps, step, _ = held.shape
     copies = []
@@ -255,10 +253,6 @@
         )
         copies.append(pltpu.make_async_copy(held.at[k], out_ref.at[pl.ds(k * step, step)], sems.at[k]))
         copies[-1].start()
-    loss = cross / totals[0:1] - norms[0:1] + norms[1:2] + CE_WEIGHT * (norms[1:2] - label_logit)
-    mine = lax.broadcasted_iota(jnp.int32, (count, count), 0) + me * rows_local == lanes
-    by_lane = lax.broadcasted_iota(jnp.int32, (count, count), 0) == lanes
-    loss_out[...] = jnp.sum(jnp.where(by_lane, to_column(mine, loss), 0.0), axis=0, keepdims=True)
     for copy in copies:
         copy.wait()
 
@@ -270,8 +264,8 @@
     return pl.pallas_call(
         functools.partial(head_kernel, rows_local, tuned),
         in_specs=[pl.BlockSpec(memory_space=pltpu.SMEM)] + [vmem] * (4 + len(hidden)),
-        out_specs=(pl.BlockSpec(memory_space=pltpu.HBM), vmem),
-        out_shape=(jax.ShapeDtypeStruct((depth, vocab), jnp.bfloat16), jax.ShapeDtypeStruct((1, count), jnp.float32)),
+        out_specs=pl.BlockSpec(memory_space=pltpu.HBM),
+        out_shape=jax.ShapeDtypeStruct((depth, vocab), jnp.bfloat16),
         scratch_shapes=[
             pltpu.VMEM((depth // step, step, vocab), jnp.bfloat16),
             pltpu.SemaphoreType.DMA((depth // step,)),
@@ -281,6 +275,28 @@
             flops=2 * count * depth * vocab, bytes_accessed=2 * depth * (vocab + count), transcendentals=2 * count * vocab
         ),
     )(me, label, stats, *logits, *hidden)
+
+
+def loss_kernel(rows_local, me_ref, stats_ref, loss_out):
+    count = stats_ref.shape[2]
+    norms, cross, label_logit = merged(stats_ref)
+    loss = cross - norms[0:1] + norms[1:2] + CE_WEIGHT * (norms[1:2] - label_logit)
+    lanes = lax.broadcasted_iota(jnp.int32, (count, count), 1)
+    mine = lax.broadcasted_iota(jnp.int32, (count, count), 0) + me_ref[0] * rows_local == lanes
+    by_lane = lax.broadcasted_iota(jnp.int32, (count, count), 0) == lanes
+    loss_out[...] = jnp.sum(jnp.where(by_lane, to_column(mine, loss), 0.0), axis=0, keepdims=True)
+
+
+def row_loss(me, stats, rows_local):
+    vmem = pl.BlockSpec(memory_space=pltpu.VMEM)
+    return pl.pallas_call(
+        functools.partial(loss_kernel, rows_local),
+        in_specs=[pl.BlockSpec(memory_space=pltpu.SMEM), vmem],
+        out_specs=vmem,
+        out_shape=jax.ShapeDtypeStruct((1, stats.shape[2]), jnp.float32),
+        compiler_params=pltpu.CompilerParams(vmem_limit_bytes=VMEM_LIMIT),
+        cost_estimate=pl.CostEstimate(flops=0, bytes_accessed=stats.size * 4, transcendentals=stats.size // 4),
+    )(me, stats)
 
 
 def swap(value, distance, n):
@@ -334,18 +350,20 @@
     return held + [swap(piece, 1, n) for piece in held], fetched, (turned, other_head)
 
 
-def scatter_rows(near_keep, near_send, far_keep, far_send, rows_local, n, head_gradient_of):
+def scatter_rows(near_keep, near_send, far_keep, far_send, rows_local, n, head_gradient_of, loss_of):
     low = jnp.bfloat16
     full = jnp.float32
     far_other = swap(far_send, 2, n)
-    grad_head, loss = head_gradient_of(far_send)
-    near_other = swap(after(near_send, grad_head), 2, n)
+    near_other = swap(near_send, 4, n)
+    grad_head = head_gradient_of(far_send)
     far = (far_keep + far_other.astype(full)).astype(low)
     from_far = swap(far[:rows_local], 8, n)
     from_far_near = swap(far[rows_local:], 12, n)
+    loss = loss_of(far_send)
     near = near_keep + near_other.astype(full)
-    from_near = swap(near[rows_local:].astype(low), 4, n)
-    total = near[:rows_local] + from_far.astype(full) + from_far_near.astype(full) + from_near.astype(full)
+    from_side = swap(near[rows_local:].astype(low), 2, n)
+    total = lax.optimization_barrier(near[:rows_local] + from_far.astype(full) + from_far_near.astype(full))
+    total = total + from_side.astype(full)
     return total, grad_head, loss
 
 
@@ -366,13 +384,16 @@
     if tuned:
         stats, away = logit.pop(), swap(stats, 1, n)
     stats = lax.all_to_all(stats, "dp", 0, 0)
-    head_gradient_of = lambda *done: head_gradient(after(me, *done), label, stats, logit, hidden, depth, rows_local, tuned)
+    head_gradient_of = lambda *done: head_gradient(
+        after(me, *done), label, stats, logit, hidden, depth, rows_local, tuned
+    )
+    loss_of = lambda *done: row_loss(after(me, *done), stats, rows_local)
     if tuned:
         parts = gradient(me, label, stats, (*logit, away), turned, rows_local, tuned)
-        grad_hidden, grad_head, loss = scatter_rows(*parts, rows_local, n, head_gradient_of)
+        grad_hidden, grad_head, loss = scatter_rows(*parts, rows_local, n, head_gradient_of, loss_of)
     else:
         (part,) = gradient(me, label, stats, logit, heads[1:], rows_local, tuned)
-        grad_head, loss = head_gradient_of()
+        grad_head, loss = head_gradient_of(part), loss_of(part)
         grad_hidden = lax.psum_scatter(part, "dp", scatter_dimension=0, tiled=True)
     return (loss[0, :rows_local], grad_hidden, grad_head)
 

time: 53.4 us -> 52.9 us (level)
    add x0 -> x1, other arithmetic: none -> 0.67 us  [scatter_rows(): total = total + from_side.astype(full)]
    add x1, other arithmetic: 0.69 us -> 0.02 us  [scatter_rows(): near[:rows_local] + from_far.astype(full) + from_far_near.astype(full)]
  transfers between devices with their start and end apart: 17 -> 17, of which waited for: 7 -> 7; matrix products, arithmetic and copies ran while one was open for 1% -> 1% of each run, Pallas kernels for 16% -> 17%
where the time goes in v7:
time: 52.9 us; the launch traced here: 52.7 us
  starting transfers between devices  16.3 us (31%)
  waiting for transfers between devices  13.3 us (25%)
  Pallas kernels  10.6 us (20%)
  blocking collectives  10.4 us (20%)
  between operations  0.82 us (2%)
  other arithmetic  0.75 us (1%)
  local copies, waits for them, and re-layouts  0.62 us (1%)
    ppermute x17, starting transfers between devices, swap(): return lax.ppermute(value, 'dp', [(i, i ^ distance) for i in range(n)])  16.3 us
    ppermute x17, waiting for transfers between devices, swap(): return lax.ppermute(value, 'dp', [(i, i ^ distance) for i in range(n)])  13.3 us
    all_to_all x1, blocking collectives, per_device(): stats = lax.all_to_all(stats, 'dp', 0, 0)  10.4 us
    pallas_call x1, Pallas kernels, prepare(): pl.pallas_call(functools.partial(prepare_kernel, rows_local, tuned), in_s...  3.6 us
    pallas_call x1, Pallas kernels, head_gradient(): pl.pallas_call(functools.partial(head_kernel, rows_local, tuned), in_spec...  2.59 us
    pallas_call x1, Pallas kernels, gradient(): pl.pallas_call(functools.partial(grad_kernel if tuned else whole_grad_ker...  1.75 us
    pallas_call x1, Pallas kernels, logits(): pl.pallas_call(functools.partial(logits_kernel, rows_local, tuned, len(hi...  1.62 us
  transfers between devices with their start and end apart: 17, of which 7 were waited for; matrix products, arithmetic and copies ran while one was open for 1% of the time, Pallas kernels for 17%

profile of v7, /device:TPU:0, one launch (start us, length us, event | category | flops | bytes accessed | tf_op | source)
XLA Modules:
  0.0 52.7 jit_solution(8324115965097144095)
XLA Ops:
  0.6 4.1 %collective-permute-start.3 = (bf16[8,4096]{1,0:T(8,128)(2,1)}, bf16[8,4096]{1,0:T(8,128)(2,1)S(1)}, u32[]{:S(2)}, u32[]{:S(2)}) collective-permute-start(bf16[8,4096]{1,0:T(8,128)(2,1)} %teacher_ref.1), channel_id=1, source_target_pairs={{0,8},{1,9},{2,10},{3,11},{4,12},{5,13},{6,14},{7,15},{8,0},{9,1},... | collective-permute-start | bytes 196616 | tf_op jit(solution)/shard_map/ppermute | solution.py:303
  4.7 0.1 collective-permute-start.4
  4.8 0.9 %shard_map.85 = bf16[8,8192]{1,0:T(8,128)(2,1)S(1)} custom-call(bf16[8,4096]{1,0:T(8,128)(2,1)} %teacher_ref.1, bf16[8,4096]{1,0:T(8,128)(2,1)} %student_ref.1), custom_call_target="tpu_custom_call" | custom-call | bytes 262144 | tf_op jit(solution)/shard_map/pallas_call | solution.py:324
  5.7 1.9 %collective-permute-start.1 = (bf16[8,8192]{1,0:T(8,128)(2,1)S(1)}, bf16[8,8192]{1,0:T(8,128)(2,1)S(1)}, u32[]{:S(2)}, u32[]{:S(2)}) collective-permute-start(bf16[8,8192]{1,0:T(8,128)(2,1)S(1)} %shard_map.85), channel_id=1, source_target_pairs={{0,4},{1,5},{2,6},{3,7},{4,0},{5,1},{6,2},{7,3},{8,12},{9,13},{10,... | collective-permute-start | bytes 393224 | tf_op jit(solution)/shard_map/ppermute | solution.py:303
  7.6 1.5 %collective-permute-start = (bf16[8,8192]{1,0:T(8,128)(2,1)S(1)}, bf16[8,8192]{1,0:T(8,128)(2,1)S(1)}, u32[]{:S(2)}, u32[]{:S(2)}) collective-permute-start(bf16[8,8192]{1,0:T(8,128)(2,1)S(1)} %shard_map.85), channel_id=1, source_target_pairs={{0,2},{1,3},{2,0},{3,1},{4,6},{5,7},{6,4},{7,5},{8,10},{9,11},{10,... | collective-permute-start | bytes 393224 | tf_op jit(solution)/shard_map/ppermute | solution.py:303
  9.1 3.6 %shard_map.86 = (bf16[4096,512]{1,0:T(8,128)(2,1)S(1)}, bf16[4096,512]{1,0:T(8,128)(2,1)S(1)}, bf16[128,128]{1,0:T(8,128)(2,1)S(1)}, f32[128,128]{1,0:T(8,128)S(1)}, bf16[512,4096]{1,0:T(8,128)(2,1)S(1)}) custom-call(s32[1]{0:T(128)} %bitcast.me_ref, s32[1,128]{1,0:T(1,128)} %bitcast.5, s32[1,128]{1,0:T(1,128)} %bitcast.6, bf16[4096,512]{1,0:T(8,128)(2,1)} %refs_0_.1, ...), custom_call_target="tpu_custom_call" | custom-call | bytes 16777216 | tf_op jit(solution)/shard_map/pallas_call | solution.py:78
  12.8 0.0 collective-permute-done.3
  12.8 0.5 collective-permute-start.6
  13.3 0.6 %collective-permute-start.5 = (bf16[8,8192]{1,0:T(8,128)(2,1)S(1)}, bf16[8,8192]{1,0:T(8,128)(2,1)S(1)}, u32[]{:S(2)}, u32[]{:S(2)}) collective-permute-start(bf16[8,8192]{1,0:T(8,128)(2,1)S(1)} %pad_maximum_fusion), channel_id=1, source_target_pairs={{0,2},{1,3},{2,0},{3,1},{4,6},{5,7},{6,4},{7,5},{8,10},{9,11},{10,... | collective-permute-start | bytes 393224 | tf_op jit(solution)/shard_map/ppermute | solution.py:303
  13.9 1.5 %collective-permute-start.2 = (bf16[8,8192]{1,0:T(8,128)(2,1)S(1)}, bf16[8,8192]{1,0:T(8,128)(2,1)S(1)}, u32[]{:S(2)}, u32[]{:S(2)}) collective-permute-start(bf16[8,8192]{1,0:T(8,128)(2,1)S(1)} %collective-permute-done), channel_id=1, source_target_pairs={{0,4},{1,5},{2,6},{3,7},{4,0},{5,1},{6,2},{7,3},{8,12},{9,13},{10,... | collective-permute-start | bytes 393224 | tf_op jit(solution)/shard_map/ppermute | solution.py:303
  15.4 3.3 %collective-permute-done.6 = bf16[8,8192]{1,0:T(8,128)(2,1)S(1)} collective-permute-done((bf16[8,8192]{1,0:T(8,128)(2,1)S(1)}, bf16[8,8192]{1,0:T(8,128)(2,1)S(1)}, u32[]{:S(2)}, u32[]{:S(2)}) %collective-permute-start.6) | collective-permute-done | bytes 131104 | tf_op jit(solution)/shard_map/ppermute | solution.py:303
  18.7 1.9 %collective-permute-done.2 = bf16[8,8192]{1,0:T(8,128)(2,1)S(1)} collective-permute-done((bf16[8,8192]{1,0:T(8,128)(2,1)S(1)}, bf16[8,8192]{1,0:T(8,128)(2,1)S(1)}, u32[]{:S(2)}, u32[]{:S(2)}) %collective-permute-start.2) | collective-permute-done | bytes 131104 | tf_op jit(solution)/shard_map/ppermute | solution.py:303
  20.7 0.1 collective-permute-start.8
  20.8 2.9 %collective-permute-done.7 = bf16[8,8192]{1,0:T(8,128)(2,1)S(1)} collective-permute-done((bf16[8,8192]{1,0:T(8,128)(2,1)S(1)}, bf16[8,8192]{1,0:T(8,128)(2,1)S(1)}, u32[]{:S(2)}, u32[]{:S(2)}) %collective-permute-start.7) | collective-permute-done | bytes 131104 | tf_op jit(solution)/shard_map/ppermute | solution.py:303
  23.7 0.1 collective-permute-start.9
  23.8 1.5 %collective-permute-done.9.refs_3_ = bf16[16,8192]{1,0:T(8,128)(2,1)S(1)} collective-permute-done((bf16[16,8192]{1,0:T(8,128)(2,1)S(1)}, bf16[16,8192]{1,0:T(8,128)(2,1)S(1)}, u32[]{:S(2)}, u32[]{:S(2)}) %collective-permute-start.9) | collective-permute-done | bytes 262176 | tf_op jit(solution)/shard_map/ppermute | solution.py:303
  25.3 1.6 %shard_map.87 = (f32[128,512]{1,0:T(8,128)S(1)}, f32[128,512]{1,0:T(8,128)S(1)}, f32[16,4,128]{2,1,0:T(4,128)S(1)}, f32[2,64,512]{2,1,0:T(8,128)S(1)}) custom-call(s32[1]{0:T(128)} %bitcast.me_ref, bf16[128,128]{1,0:T(8,128)(2,1)S(1)} %get-tuple-element.22.pick_ref, f32[128,128]{1,0:T(8,128)S(1)} %get-tuple-element.21.label_ref, ...), custom_call_target="tpu_custom_call" | custom-call | flops 1073741824 | bytes 10485760 | tf_op jit(solution)/shard_map/pallas_call | solution.py:141
  26.9 0.2 collective-permute-start.10
  27.1 10.4 %all_to_all.5.stats_ref = f32[16,4,128]{2,1,0:T(4,128)S(1)} all-to-all(f32[16,4,128]{2,1,0:T(4,128)S(1)} %get-tuple-element.27), channel_id=1, replica_groups=mesh['groups'=2,'dp'=16] {'dp'}, dimensions={0} | all-to-all | bytes 65536 | tf_op jit(solution)/shard_map/all_to_all | solution.py:386
  37.5 1.8 %shard_map.88 = (f32[16,4096]{1,0:T(8,128)S(1)}, bf16[16,4096]{1,0:T(8,128)(2,1)S(1)}, f32[16,4096]{1,0:T(8,128)S(1)}, bf16[16,4096]{1,0:T(8,128)(2,1)S(1)}) custom-call(s32[1]{0:T(128)} %bitcast.me_ref, f32[128,128]{1,0:T(8,128)S(1)} %get-tuple-element.21.label_ref, f32[16,4,128]{2,1,0:T(4,128)S(1)} %all_to_all.5.stats_ref, ...), custom_call_target="tpu_custom_call" | custom-call | flops 536870912 | bytes 6291456 | tf_op jit(solution)/shard_map/pallas_call | solution.py:226
  39.3 0.4 collective-permute-start.13
  39.7 0.1 shard_map.89
  39.8 0.5 slice_bitcast_fusion
  40.4 0.6 %collective-permute-start.12 = (bf16[16,4096]{1,0:T(8,128)(2,1)S(1)}, bf16[16,4096]{1,0:T(8,128)(2,1)S(1)}, u32[]{:S(2)}, u32[]{:S(2)}) collective-permute-start(bf16[16,4096]{1,0:T(8,128)(2,1)S(1)} %get-tuple-element.35), channel_id=1, source_target_pairs={{0,4},{1,5},{2,6},{3,7},{4,0},{5,1},{6,2},{7,3},{8,12},{9,13},{10,... | collective-permute-start | bytes 393224 | tf_op jit(solution)/shard_map/ppermute | solution.py:303
  41.0 2.6 %shard_map.90 = bf16[4096,512]{1,0:T(8,128)(2,1)} custom-call(s32[1]{0:T(128)} %bitcast.me_ref, f32[128,128]{1,0:T(8,128)S(1)} %get-tuple-element.21.label_ref, f32[16,4,128]{2,1,0:T(4,128)S(1)} %all_to_all.5.stats_ref, f32[128,512]{1,0:T(8,128)S(1)} %get-tuple-element.28.teacher_ref, f32[128,512]{1,0:T(8,128)S(1)} %get-tuple-element.29.student_ref, ...), custom_call_target="tpu_custom_call" | custom-call | flops 536870912 | bytes 5242880 | tf_op jit(solution)/shard_map/pallas_call | solution.py:264
  43.6 0.9 %collective-permute-done.13 = bf16[16,4096]{1,0:T(8,128)(2,1)S(1)} collective-permute-done((bf16[16,4096]{1,0:T(8,128)(2,1)S(1)}, bf16[16,4096]{1,0:T(8,128)(2,1)S(1)}, u32[]{:S(2)}, u32[]{:S(2)}) %collective-permute-start.13) | collective-permute-done | bytes 131104 | tf_op jit(solution)/shard_map/ppermute | solution.py:303
  44.5 0.9 %collective-permute-start.14 = (bf16[8,4096]{1,0:T(8,128)(2,1)S(1)}, bf16[8,4096]{1,0:T(8,128)(2,1)S(1)}, u32[]{:S(2)}, u32[]{:S(2)}) collective-permute-start(bf16[8,4096]{1,0:T(8,128)(2,1)S(1)} %get-tuple-element.37), channel_id=1, source_target_pairs={{0,8},{1,9},{2,10},{3,11},{4,12},{5,13},{6,14},{7,15},{8,0},{9,1},... | collective-permute-start | bytes 196616 | tf_op jit(solution)/shard_map/ppermute | solution.py:303
  45.4 2.3 %collective-permute-start.15 = (bf16[8,4096]{1,0:T(8,128)(2,1)S(1)}, bf16[8,4096]{1,0:T(8,128)(2,1)S(1)}, u32[]{:S(2)}, u32[]{:S(2)}) collective-permute-start(bf16[8,4096]{1,0:T(8,128)(2,1)S(1)} %get-tuple-element.38), channel_id=1, source_target_pairs={{0,12},{1,13},{2,14},{3,15},{4,8},{5,9},{6,10},{7,11},{8,4},{9,5},... | collective-permute-start | bytes 196616 | tf_op jit(solution)/shard_map/ppermute | solution.py:303
  47.7 1.5 %collective-permute-start.16 = (bf16[8,4096]{1,0:T(8,128)(2,1)S(1)}, bf16[8,4096]{1,0:T(8,128)(2,1)S(1)}, u32[]{:S(2)}, u32[]{:S(2)}) collective-permute-start(bf16[8,4096]{1,0:T(8,128)(2,1)S(1)} %slice.30), channel_id=1, source_target_pairs={{0,2},{1,3},{2,0},{3,1},{4,6},{5,7},{6,4},{7,5},{8,10},{9,11},{10,... | collective-permute-start | bytes 196616 | tf_op jit(solution)/shard_map/ppermute | solution.py:303
  49.3 2.5 %collective-permute-done.14 = bf16[8,4096]{1,0:T(8,128)(2,1)S(1)} collective-permute-done((bf16[8,4096]{1,0:T(8,128)(2,1)S(1)}, bf16[8,4096]{1,0:T(8,128)(2,1)S(1)}, u32[]{:S(2)}, u32[]{:S(2)}) %collective-permute-start.14) | collective-permute-done | bytes 65568 | tf_op jit(solution)/shard_map/ppermute | solution.py:303
  51.8 0.3 collective-permute-done.16
  52.1 0.7 %convert_add_fusion.1 = f32[8,4096]{1,0:T(8,128)} fusion(f32[8,4096]{1,0:T(8,128)S(1)} %fusion, bf16[8,4096]{1,0:T(8,128)(2,1)S(1)} %collective-permute-done.16), kind=kLoop, calls=%fused_computation.6 | loop fusion | flops 65536 | bytes 327680 | tf_op jit(solution)/shard_map/add | solution.py:366
  (25 shorter events, 0.2 us)
Async XLA Ops:
  0.6 12.1 %collective-permute-start.3 = (bf16[8,4096]{1,0:T(8,128)(2,1)}, bf16[8,4096]{1,0:T(8,128)(2,1)S(1)}, u32[]{:S(2)}, u32[]{:S(2)}) collective-permute-start(bf16[8,4096]{1,0:T(8,128)(2,1)} %teacher_ref.1), channel_id=1, source_target_pairs={{0,8},{1,9},{2,10},{3,11},{4,12},{5,13},{6,14},{7,15},{8,0},{9,1},... | collective-permute-start | bytes 196616 | tf_op jit(solution)/shard_map/ppermute | solution.py:303
  4.7 8.0 %collective-permute-start.4 = (bf16[8,4096]{1,0:T(8,128)(2,1)}, bf16[8,4096]{1,0:T(8,128)(2,1)S(1)}, u32[]{:S(2)}, u32[]{:S(2)}) collective-permute-start(bf16[8,4096]{1,0:T(8,128)(2,1)} %student_ref.1), channel_id=1, source_target_pairs={{0,8},{1,9},{2,10},{3,11},{4,12},{5,13},{6,14},{7,15},{8,0},{9,1},... | collective-permute-start | bytes 196616 | tf_op jit(solution)/shard_map/ppermute | solution.py:303
  5.7 9.7 %collective-permute-start.1 = (bf16[8,8192]{1,0:T(8,128)(2,1)S(1)}, bf16[8,8192]{1,0:T(8,128)(2,1)S(1)}, u32[]{:S(2)}, u32[]{:S(2)}) collective-permute-start(bf16[8,8192]{1,0:T(8,128)(2,1)S(1)} %shard_map.85), channel_id=1, source_target_pairs={{0,4},{1,5},{2,6},{3,7},{4,0},{5,1},{6,2},{7,3},{8,12},{9,13},{10,... | collective-permute-start | bytes 393224 | tf_op jit(solution)/shard_map/ppermute | solution.py:303
  7.6 6.3 %collective-permute-start = (bf16[8,8192]{1,0:T(8,128)(2,1)S(1)}, bf16[8,8192]{1,0:T(8,128)(2,1)S(1)}, u32[]{:S(2)}, u32[]{:S(2)}) collective-permute-start(bf16[8,8192]{1,0:T(8,128)(2,1)S(1)} %shard_map.85), channel_id=1, source_target_pairs={{0,2},{1,3},{2,0},{3,1},{4,6},{5,7},{6,4},{7,5},{8,10},{9,11},{10,... | collective-permute-start | bytes 393224 | tf_op jit(solution)/shard_map/ppermute | solution.py:303
  12.8 5.9 %collective-permute-start.6 = (bf16[8,8192]{1,0:T(8,128)(2,1)S(1)}, bf16[8,8192]{1,0:T(8,128)(2,1)S(1)}, u32[]{:S(2)}, u32[]{:S(2)}) collective-permute-start(bf16[8,8192]{1,0:T(8,128)(2,1)S(1)} %pad_maximum_fusion), channel_id=1, source_target_pairs={{0,4},{1,5},{2,6},{3,7},{4,0},{5,1},{6,2},{7,3},{8,12},{9,13},{10,... | collective-permute-start | bytes 393224 | tf_op jit(solution)/shard_map/ppermute | solution.py:303
  13.3 7.4 %collective-permute-start.5 = (bf16[8,8192]{1,0:T(8,128)(2,1)S(1)}, bf16[8,8192]{1,0:T(8,128)(2,1)S(1)}, u32[]{:S(2)}, u32[]{:S(2)}) collective-permute-start(bf16[8,8192]{1,0:T(8,128)(2,1)S(1)} %pad_maximum_fusion), channel_id=1, source_target_pairs={{0,2},{1,3},{2,0},{3,1},{4,6},{5,7},{6,4},{7,5},{8,10},{9,11},{10,... | collective-permute-start | bytes 393224 | tf_op jit(solution)/shard_map/ppermute | solution.py:303
  13.9 23.6 %collective-permute-start.11 = (bf16[512,4096]{1,0:T(8,128)(2,1)S(1)}, bf16[512,4096]{1,0:T(8,128)(2,1)S(1)}, u32[]{:S(2)}, u32[]{:S(2)}) collective-permute-start(bf16[512,4096]{1,0:T(8,128)(2,1)S(1)} %get-tuple-element.31.turned_ref), channel_id=1, source_target_pairs={{0,1},{1,0},{2,3},{3,2},{4,5},{5,4},{6,7},{7,6},{8,9},{9,8},{10,11... | collective-permute-start | bytes 12582920 | tf_op jit(solution)/shard_map/ppermute | solution.py:303
  13.9 6.7 %collective-permute-start.2 = (bf16[8,8192]{1,0:T(8,128)(2,1)S(1)}, bf16[8,8192]{1,0:T(8,128)(2,1)S(1)}, u32[]{:S(2)}, u32[]{:S(2)}) collective-permute-start(bf16[8,8192]{1,0:T(8,128)(2,1)S(1)} %collective-permute-done), channel_id=1, source_target_pairs={{0,4},{1,5},{2,6},{3,7},{4,0},{5,1},{6,2},{7,3},{8,12},{9,13},{10,... | collective-permute-start | bytes 393224 | tf_op jit(solution)/shard_map/ppermute | solution.py:303
  18.7 5.0 %collective-permute-start.7 = (bf16[8,8192]{1,0:T(8,128)(2,1)S(1)}, bf16[8,8192]{1,0:T(8,128)(2,1)S(1)}, u32[]{:S(2)}, u32[]{:S(2)}) collective-permute-start(bf16[8,8192]{1,0:T(8,128)(2,1)S(1)} %collective-permute-done.6), channel_id=1, source_target_pairs={{0,2},{1,3},{2,0},{3,1},{4,6},{5,7},{6,4},{7,5},{8,10},{9,11},{10,... | collective-permute-start | bytes 393224 | tf_op jit(solution)/shard_map/ppermute | solution.py:303
  20.7 4.6 %collective-permute-start.8 = (bf16[48,8192]{1,0:T(8,128)(2,1)S(1)}, bf16[48,8192]{1,0:T(8,128)(2,1)S(1)}, u32[]{:S(2)}, u32[]{:S(2)}) collective-permute-start(bf16[48,8192]{1,0:T(8,128)(2,1)S(1)} %constant_dynamic-update-slice_fusion.refs_0_), channel_id=1, source_target_pairs={{0,1},{1,0},{2,3},{3,2},{4,5},{5,4},{6,7},{7,6},{8,9},{9,8},{10,11... | collective-permute-start | bytes 2359304 | tf_op jit(solution)/shard_map/ppermute | solution.py:303
  23.7 1.6 %collective-permute-start.9 = (bf16[16,8192]{1,0:T(8,128)(2,1)S(1)}, bf16[16,8192]{1,0:T(8,128)(2,1)S(1)}, u32[]{:S(2)}, u32[]{:S(2)}) collective-permute-start(bf16[16,8192]{1,0:T(8,128)(2,1)S(1)} %constant_dynamic-update-slice_fusion.6.refs_1_), channel_id=1, source_target_pairs={{0,1},{1,0},{2,3},{3,2},{4,5},{5,4},{6,7},{7,6},{8,9},{9,8},{10,11... | collective-permute-start | bytes 786440 | tf_op jit(solution)/shard_map/ppermute | solution.py:303
  26.9 10.6 %collective-permute-start.10 = (f32[2,64,512]{2,1,0:T(8,128)S(1)}, f32[2,64,512]{2,1,0:T(8,128)S(1)}, u32[]{:S(2)}, u32[]{:S(2)}) collective-permute-start(f32[2,64,512]{2,1,0:T(8,128)S(1)} %get-tuple-element.30), channel_id=1, source_target_pairs={{0,1},{1,0},{2,3},{3,2},{4,5},{5,4},{6,7},{7,6},{8,9},{9,8},{10,11... | collective-permute-start | bytes 786440 | tf_op jit(solution)/shard_map/ppermute | solution.py:303
  39.3 5.2 %collective-permute-start.13 = (bf16[16,4096]{1,0:T(8,128)(2,1)S(1)}, bf16[16,4096]{1,0:T(8,128)(2,1)S(1)}, u32[]{:S(2)}, u32[]{:S(2)}) collective-permute-start(bf16[16,4096]{1,0:T(8,128)(2,1)S(1)} %get-tuple-element.32), channel_id=1, source_target_pairs={{0,2},{1,3},{2,0},{3,1},{4,6},{5,7},{6,4},{7,5},{8,10},{9,11},{10,... | collective-permute-start | bytes 393224 | tf_op jit(solution)/shard_map/ppermute | solution.py:303
  40.4 7.3 %collective-permute-start.12 = (bf16[16,4096]{1,0:T(8,128)(2,1)S(1)}, bf16[16,4096]{1,0:T(8,128)(2,1)S(1)}, u32[]{:S(2)}, u32[]{:S(2)}) collective-permute-start(bf16[16,4096]{1,0:T(8,128)(2,1)S(1)} %get-tuple-element.35), channel_id=1, source_target_pairs={{0,4},{1,5},{2,6},{3,7},{4,0},{5,1},{6,2},{7,3},{8,12},{9,13},{10,... | collective-permute-start | bytes 393224 | tf_op jit(solution)/shard_map/ppermute | solution.py:303
  44.5 7.3 %collective-permute-start.14 = (bf16[8,4096]{1,0:T(8,128)(2,1)S(1)}, bf16[8,4096]{1,0:T(8,128)(2,1)S(1)}, u32[]{:S(2)}, u32[]{:S(2)}) collective-permute-start(bf16[8,4096]{1,0:T(8,128)(2,1)S(1)} %get-tuple-element.37), channel_id=1, source_target_pairs={{0,8},{1,9},{2,10},{3,11},{4,12},{5,13},{6,14},{7,15},{8,0},{9,1},... | collective-permute-start | bytes 196616 | tf_op jit(solution)/shard_map/ppermute | solution.py:303
  45.4 6.4 %collective-permute-start.15 = (bf16[8,4096]{1,0:T(8,128)(2,1)S(1)}, bf16[8,4096]{1,0:T(8,128)(2,1)S(1)}, u32[]{:S(2)}, u32[]{:S(2)}) collective-permute-start(bf16[8,4096]{1,0:T(8,128)(2,1)S(1)} %get-tuple-element.38), channel_id=1, source_target_pairs={{0,12},{1,13},{2,14},{3,15},{4,8},{5,9},{6,10},{7,11},{8,4},{9,5},... | collective-permute-start | bytes 196616 | tf_op jit(solution)/shard_map/ppermute | solution.py:303
  47.7 4.3 %collective-permute-start.16 = (bf16[8,4096]{1,0:T(8,128)(2,1)S(1)}, bf16[8,4096]{1,0:T(8,128)(2,1)S(1)}, u32[]{:S(2)}, u32[]{:S(2)}) collective-permute-start(bf16[8,4096]{1,0:T(8,128)(2,1)S(1)} %slice.30), channel_id=1, source_target_pairs={{0,2},{1,3},{2,0},{3,1},{4,6},{5,7},{6,4},{7,5},{8,10},{9,11},{10,... | collective-permute-start | bytes 196616 | tf_op jit(solution)/shard_map/ppermute | solution.py:303

commit v8 on v7

--- a/solution.py
+++ b/solution.py
@@ -307,36 +307,11 @@
     return lax.optimization_barrier((value, *done))[0]
 
 
-def join_kernel(teacher_ref, student_ref, out_ref, sems):
-    depth = teacher_ref.shape[1]
-    copies = [
-        pltpu.make_async_copy(ref, out_ref.at[:, pl.ds(j * depth, depth)], sems.at[j])
-        for j, ref in enumerate((teacher_ref, student_ref))
-    ]
-    for copy in copies:
-        copy.start()
-    for copy in copies:
-        copy.wait()
-
-
-def join_rows(teacher_rows, student_rows):
-    count, depth = teacher_rows.shape
-    return pl.pallas_call(
-        join_kernel,
-        in_specs=[pl.BlockSpec(memory_space=pltpu.HBM)] * 2,
-        out_specs=pl.BlockSpec(memory_space=pltpu.VMEM),
-        out_shape=jax.ShapeDtypeStruct((count, 2 * depth), teacher_rows.dtype),
-        scratch_shapes=[pltpu.SemaphoreType.DMA((2,))],
-        compiler_params=pltpu.CompilerParams(vmem_limit_bytes=2**20),
-        cost_estimate=pl.CostEstimate(flops=0, bytes_accessed=8 * count * depth, transcendentals=0),
-    )(stay(teacher_rows), stay(student_rows))
-
-
 def gather_rows(teacher_rows, student_rows, n, fetch):
     join = lambda pair: jnp.concatenate(pair, axis=1)
     stack = lambda *parts: jnp.concatenate(parts, axis=0)
     far_teacher = swap(teacher_rows, 8, n)
-    rows = join_rows(teacher_rows, student_rows)
+    rows = join((teacher_rows, student_rows))
     far_student = swap(student_rows, 8, n)
     near, side = swap(rows, 4, n), swap(rows, 2, n)
     *fetched, turned = fetch(rows)

time: 52.9 us -> 53.9 us (1.019)
  local copies, waits for them, and re-layouts: 0.62 us -> 2.31 us
  Pallas kernels: 10.6 us -> 9.7 us
    unnamed x6 -> x7, local copies, waits for them, and re-layouts: 0.06 us -> 1.75 us
    pallas_call x1 -> x0, Pallas kernels: 0.89 us -> none  [join_rows(): pl.pallas_call(join_kernel, in_specs=[pl.BlockSpec(memory_space=pltpu.HBM...]
  transfers between devices with their start and end apart: 17 -> 17, of which waited for: 7 -> 7; matrix products, arithmetic and copies ran while one was open for 1% -> 4% of each run, Pallas kernels for 17% -> 15%
where the time goes in v8:
time: 53.9 us; the launch traced here: 53.6 us
  starting transfers between devices  16.3 us (30%)
  waiting for transfers between devices  13.4 us (25%)
  blocking collectives  10.3 us (19%)
  Pallas kernels  9.7 us (18%)
  local copies, waits for them, and re-layouts  2.31 us (4%)
  between operations  0.81 us (2%)
  other arithmetic  0.75 us (1%)
    ppermute x17, starting transfers between devices, swap(): return lax.ppermute(value, 'dp', [(i, i ^ distance) for i in range(n)])  16.3 us
    ppermute x17, waiting for transfers between devices, swap(): return lax.ppermute(value, 'dp', [(i, i ^ distance) for i in range(n)])  13.4 us
    all_to_all x1, blocking collectives, per_device(): stats = lax.all_to_all(stats, 'dp', 0, 0)  10.3 us
    pallas_call x1, Pallas kernels, prepare(): pl.pallas_call(functools.partial(prepare_kernel, rows_local, tuned), in_s...  3.6 us
    pallas_call x1, Pallas kernels, head_gradient(): pl.pallas_call(functools.partial(head_kernel, rows_local, tuned), in_spec...  2.59 us
    pallas_call x1, Pallas kernels, gradient(): pl.pallas_call(functools.partial(grad_kernel if tuned else whole_grad_ker...  1.76 us
    unnamed x7, local copies, waits for them, and re-layouts  1.75 us
    pallas_call x1, Pallas kernels, logits(): pl.pallas_call(functools.partial(logits_kernel, rows_local, tuned, len(hi...  1.62 us
  transfers between devices with their start and end apart: 17, of which 7 were waited for; matrix products, arithmetic and copies ran while one was open for 4% of the time, Pallas kernels for 15%

profile of v8, /device:TPU:0, one launch (start us, length us, event | category | flops | bytes accessed | tf_op | source)
XLA Modules:
  0.0 53.6 jit_solution(138424494079383086)
XLA Ops:
  0.6 4.1 %collective-permute-start.3 = (bf16[8,4096]{1,0:T(8,128)(2,1)}, bf16[8,4096]{1,0:T(8,128)(2,1)S(1)}, u32[]{:S(2)}, u32[]{:S(2)}) collective-permute-start(bf16[8,4096]{1,0:T(8,128)(2,1)} %param.6), channel_id=1, source_target_pairs={{0,8},{1,9},{2,10},{3,11},{4,12},{5,13},{6,14},{7,15},{8,0},{9,1},... | collective-permute-start | bytes 196616 | tf_op jit(solution)/shard_map/ppermute | solution.py:303
  4.7 0.1 collective-permute-start.4
  4.8 0.8 %constant_dynamic-update-slice_fusion.8 = (bf16[48,8192]{1,0:T(8,128)(2,1)S(1)}, bf16[8,8192]{1,0:T(8,128)(2,1)S(1)}) fusion(bf16[8,4096]{1,0:T(8,128)(2,1)} %param.6), kind=kLoop, calls=%fused_computation.15 | loop fusion | bytes 196608
  5.7 0.9 %constant_dynamic-update-slice_fusion.7 = (bf16[48,8192]{1,0:T(8,128)(2,1)S(1)}, bf16[8,8192]{1,0:T(8,128)(2,1)S(1)}) fusion(bf16[48,8192]{1,0:T(8,128)(2,1)S(1)} %get-tuple-element.41, bf16[8,4096]{1,0:T(8,128)(2,1)} %param.7, bf16[8,8192]{1,0:T(8,128)(2,1)S(1)} %get-tuple-element.42), kind=kLoop, calls=%fused_computation.14 | loop fusion | bytes 196608
  6.5 1.9 %collective-permute-start.1 = (bf16[8,8192]{1,0:T(8,128)(2,1)S(1)}, bf16[8,8192]{1,0:T(8,128)(2,1)S(1)}, u32[]{:S(2)}, u32[]{:S(2)}) collective-permute-start(bf16[8,8192]{1,0:T(8,128)(2,1)S(1)} %get-tuple-element.40), channel_id=1, source_target_pairs={{0,4},{1,5},{2,6},{3,7},{4,0},{5,1},{6,2},{7,3},{8,12},{9,13},{10,... | collective-permute-start | bytes 393224 | tf_op jit(solution)/shard_map/ppermute | solution.py:303
  8.4 1.5 %collective-permute-start = (bf16[8,8192]{1,0:T(8,128)(2,1)S(1)}, bf16[8,8192]{1,0:T(8,128)(2,1)S(1)}, u32[]{:S(2)}, u32[]{:S(2)}) collective-permute-start(bf16[8,8192]{1,0:T(8,128)(2,1)S(1)} %get-tuple-element.40), channel_id=1, source_target_pairs={{0,2},{1,3},{2,0},{3,1},{4,6},{5,7},{6,4},{7,5},{8,10},{9,11},{10,... | collective-permute-start | bytes 393224 | tf_op jit(solution)/shard_map/ppermute | solution.py:303
  9.9 3.6 %shard_map.85 = (bf16[4096,512]{1,0:T(8,128)(2,1)S(1)}, bf16[4096,512]{1,0:T(8,128)(2,1)S(1)}, bf16[128,128]{1,0:T(8,128)(2,1)S(1)}, f32[128,128]{1,0:T(8,128)S(1)}, bf16[512,4096]{1,0:T(8,128)(2,1)S(1)}) custom-call(s32[1]{0:T(128)} %bitcast.me_ref, s32[1,128]{1,0:T(1,128)} %bitcast.5, s32[1,128]{1,0:T(1,128)} %bitcast.6, bf16[4096,512]{1,0:T(8,128)(2,1)} %refs_0_.1, ...), custom_call_target="tpu_custom_call" | custom-call | bytes 16777216 | tf_op jit(solution)/shard_map/pallas_call | solution.py:78
  13.6 0.5 collective-permute-start.6
  14.1 0.2 collective-permute-start.5
  14.3 1.8 %collective-permute-start.2 = (bf16[8,8192]{1,0:T(8,128)(2,1)S(1)}, bf16[8,8192]{1,0:T(8,128)(2,1)S(1)}, u32[]{:S(2)}, u32[]{:S(2)}) collective-permute-start(bf16[8,8192]{1,0:T(8,128)(2,1)S(1)} %collective-permute-done), channel_id=1, source_target_pairs={{0,4},{1,5},{2,6},{3,7},{4,0},{5,1},{6,2},{7,3},{8,12},{9,13},{10,... | collective-permute-start | bytes 393224 | tf_op jit(solution)/shard_map/ppermute | solution.py:303
  16.2 3.4 %collective-permute-done.6 = bf16[8,8192]{1,0:T(8,128)(2,1)S(1)} collective-permute-done((bf16[8,8192]{1,0:T(8,128)(2,1)S(1)}, bf16[8,8192]{1,0:T(8,128)(2,1)S(1)}, u32[]{:S(2)}, u32[]{:S(2)}) %collective-permute-start.6) | collective-permute-done | bytes 131104 | tf_op jit(solution)/shard_map/ppermute | solution.py:303
  19.7 1.7 %collective-permute-done.2 = bf16[8,8192]{1,0:T(8,128)(2,1)S(1)} collective-permute-done((bf16[8,8192]{1,0:T(8,128)(2,1)S(1)}, bf16[8,8192]{1,0:T(8,128)(2,1)S(1)}, u32[]{:S(2)}, u32[]{:S(2)}) %collective-permute-start.2) | collective-permute-done | bytes 131104 | tf_op jit(solution)/shard_map/ppermute | solution.py:303
  21.5 0.1 collective-permute-start.8
  21.6 3.1 %collective-permute-done.7 = bf16[8,8192]{1,0:T(8,128)(2,1)S(1)} collective-permute-done((bf16[8,8192]{1,0:T(8,128)(2,1)S(1)}, bf16[8,8192]{1,0:T(8,128)(2,1)S(1)}, u32[]{:S(2)}, u32[]{:S(2)}) %collective-permute-start.7) | collective-permute-done | bytes 131104 | tf_op jit(solution)/shard_map/ppermute | solution.py:303
  24.7 0.1 collective-permute-start.9
  24.7 1.5 %collective-permute-done.9.refs_3_ = bf16[16,8192]{1,0:T(8,128)(2,1)S(1)} collective-permute-done((bf16[16,8192]{1,0:T(8,128)(2,1)S(1)}, bf16[16,8192]{1,0:T(8,128)(2,1)S(1)}, u32[]{:S(2)}, u32[]{:S(2)}) %collective-permute-start.9) | collective-permute-done | bytes 262176 | tf_op jit(solution)/shard_map/ppermute | solution.py:303
  26.3 1.6 %shard_map.86 = (f32[128,512]{1,0:T(8,128)S(1)}, f32[128,512]{1,0:T(8,128)S(1)}, f32[16,4,128]{2,1,0:T(4,128)S(1)}, f32[2,64,512]{2,1,0:T(8,128)S(1)}) custom-call(s32[1]{0:T(128)} %bitcast.me_ref, bf16[128,128]{1,0:T(8,128)(2,1)S(1)} %get-tuple-element.22.pick_ref, f32[128,128]{1,0:T(8,128)S(1)} %get-tuple-element.21.label_ref, ...), custom_call_target="tpu_custom_call" | custom-call | flops 1073741824 | bytes 10485760 | tf_op jit(solution)/shard_map/pallas_call | solution.py:141
  27.9 0.2 collective-permute-start.10
  28.1 10.3 %all_to_all.5.stats_ref = f32[16,4,128]{2,1,0:T(4,128)S(1)} all-to-all(f32[16,4,128]{2,1,0:T(4,128)S(1)} %get-tuple-element.27), channel_id=1, replica_groups=mesh['groups'=2,'dp'=16] {'dp'}, dimensions={0} | all-to-all | bytes 65536 | tf_op jit(solution)/shard_map/all_to_all | solution.py:361
  38.4 1.8 %shard_map.87 = (f32[16,4096]{1,0:T(8,128)S(1)}, bf16[16,4096]{1,0:T(8,128)(2,1)S(1)}, f32[16,4096]{1,0:T(8,128)S(1)}, bf16[16,4096]{1,0:T(8,128)(2,1)S(1)}) custom-call(s32[1]{0:T(128)} %bitcast.me_ref, f32[128,128]{1,0:T(8,128)S(1)} %get-tuple-element.21.label_ref, f32[16,4,128]{2,1,0:T(4,128)S(1)} %all_to_all.5.stats_ref, ...), custom_call_target="tpu_custom_call" | custom-call | flops 536870912 | bytes 6291456 | tf_op jit(solution)/shard_map/pallas_call | solution.py:226
  40.2 0.4 collective-permute-start.13
  40.6 0.1 shard_map.88
  40.7 0.5 slice_bitcast_fusion
  41.2 0.6 %collective-permute-start.12 = (bf16[16,4096]{1,0:T(8,128)(2,1)S(1)}, bf16[16,4096]{1,0:T(8,128)(2,1)S(1)}, u32[]{:S(2)}, u32[]{:S(2)}) collective-permute-start(bf16[16,4096]{1,0:T(8,128)(2,1)S(1)} %get-tuple-element.35), channel_id=1, source_target_pairs={{0,4},{1,5},{2,6},{3,7},{4,0},{5,1},{6,2},{7,3},{8,12},{9,13},{10,... | collective-permute-start | bytes 393224 | tf_op jit(solution)/shard_map/ppermute | solution.py:303
  41.9 2.6 %shard_map.89 = bf16[4096,512]{1,0:T(8,128)(2,1)} custom-call(s32[1]{0:T(128)} %bitcast.me_ref, f32[128,128]{1,0:T(8,128)S(1)} %get-tuple-element.21.label_ref, f32[16,4,128]{2,1,0:T(4,128)S(1)} %all_to_all.5.stats_ref, f32[128,512]{1,0:T(8,128)S(1)} %get-tuple-element.28.teacher_ref, f32[128,512]{1,0:T(8,128)S(1)} %get-tuple-element.29.student_ref, ...), custom_call_target="tpu_custom_call" | custom-call | flops 536870912 | bytes 5242880 | tf_op jit(solution)/shard_map/pallas_call | solution.py:264
  44.5 0.9 %collective-permute-done.13 = bf16[16,4096]{1,0:T(8,128)(2,1)S(1)} collective-permute-done((bf16[16,4096]{1,0:T(8,128)(2,1)S(1)}, bf16[16,4096]{1,0:T(8,128)(2,1)S(1)}, u32[]{:S(2)}, u32[]{:S(2)}) %collective-permute-start.13) | collective-permute-done | bytes 131104 | tf_op jit(solution)/shard_map/ppermute | solution.py:303
  45.4 0.9 %collective-permute-start.14 = (bf16[8,4096]{1,0:T(8,128)(2,1)S(1)}, bf16[8,4096]{1,0:T(8,128)(2,1)S(1)}, u32[]{:S(2)}, u32[]{:S(2)}) collective-permute-start(bf16[8,4096]{1,0:T(8,128)(2,1)S(1)} %get-tuple-element.37), channel_id=1, source_target_pairs={{0,8},{1,9},{2,10},{3,11},{4,12},{5,13},{6,14},{7,15},{8,0},{9,1},... | collective-permute-start | bytes 196616 | tf_op jit(solution)/shard_map/ppermute | solution.py:303
  46.3 2.3 %collective-permute-start.15 = (bf16[8,4096]{1,0:T(8,128)(2,1)S(1)}, bf16[8,4096]{1,0:T(8,128)(2,1)S(1)}, u32[]{:S(2)}, u32[]{:S(2)}) collective-permute-start(bf16[8,4096]{1,0:T(8,128)(2,1)S(1)} %get-tuple-element.38), channel_id=1, source_target_pairs={{0,12},{1,13},{2,14},{3,15},{4,8},{5,9},{6,10},{7,11},{8,4},{9,5},... | collective-permute-start | bytes 196616 | tf_op jit(solution)/shard_map/ppermute | solution.py:303
  48.6 1.5 %collective-permute-start.16 = (bf16[8,4096]{1,0:T(8,128)(2,1)S(1)}, bf16[8,4096]{1,0:T(8,128)(2,1)S(1)}, u32[]{:S(2)}, u32[]{:S(2)}) collective-permute-start(bf16[8,4096]{1,0:T(8,128)(2,1)S(1)} %slice.30), channel_id=1, source_target_pairs={{0,2},{1,3},{2,0},{3,1},{4,6},{5,7},{6,4},{7,5},{8,10},{9,11},{10,... | collective-permute-start | bytes 196616 | tf_op jit(solution)/shard_map/ppermute | solution.py:303
  50.2 2.5 %collective-permute-done.14 = bf16[8,4096]{1,0:T(8,128)(2,1)S(1)} collective-permute-done((bf16[8,4096]{1,0:T(8,128)(2,1)S(1)}, bf16[8,4096]{1,0:T(8,128)(2,1)S(1)}, u32[]{:S(2)}, u32[]{:S(2)}) %collective-permute-start.14) | collective-permute-done | bytes 65568 | tf_op jit(solution)/shard_map/ppermute | solution.py:303
  52.7 0.3 collective-permute-done.16
  53.0 0.7 %convert_add_fusion.1 = f32[8,4096]{1,0:T(8,128)} fusion(f32[8,4096]{1,0:T(8,128)S(1)} %fusion, bf16[8,4096]{1,0:T(8,128)(2,1)S(1)} %collective-permute-done.16), kind=kLoop, calls=%fused_computation.6 | loop fusion | flops 65536 | bytes 327680 | tf_op jit(solution)/shard_map/add | solution.py:341
  (25 shorter events, 0.2 us)
Async XLA Ops:
  0.6 12.9 %collective-permute-start.3 = (bf16[8,4096]{1,0:T(8,128)(2,1)}, bf16[8,4096]{1,0:T(8,128)(2,1)S(1)}, u32[]{:S(2)}, u32[]{:S(2)}) collective-permute-start(bf16[8,4096]{1,0:T(8,128)(2,1)} %param.6), channel_id=1, source_target_pairs={{0,8},{1,9},{2,10},{3,11},{4,12},{5,13},{6,14},{7,15},{8,0},{9,1},... | collective-permute-start | bytes 196616 | tf_op jit(solution)/shard_map/ppermute | solution.py:303
  4.7 8.8 %collective-permute-start.4 = (bf16[8,4096]{1,0:T(8,128)(2,1)}, bf16[8,4096]{1,0:T(8,128)(2,1)S(1)}, u32[]{:S(2)}, u32[]{:S(2)}) collective-permute-start(bf16[8,4096]{1,0:T(8,128)(2,1)} %param.7), channel_id=1, source_target_pairs={{0,8},{1,9},{2,10},{3,11},{4,12},{5,13},{6,14},{7,15},{8,0},{9,1},... | collective-permute-start | bytes 196616 | tf_op jit(solution)/shard_map/ppermute | solution.py:303
  6.5 9.7 %collective-permute-start.1 = (bf16[8,8192]{1,0:T(8,128)(2,1)S(1)}, bf16[8,8192]{1,0:T(8,128)(2,1)S(1)}, u32[]{:S(2)}, u32[]{:S(2)}) collective-permute-start(bf16[8,8192]{1,0:T(8,128)(2,1)S(1)} %get-tuple-element.40), channel_id=1, source_target_pairs={{0,4},{1,5},{2,6},{3,7},{4,0},{5,1},{6,2},{7,3},{8,12},{9,13},{10,... | collective-permute-start | bytes 393224 | tf_op jit(solution)/shard_map/ppermute | solution.py:303
  8.4 5.9 %collective-permute-start = (bf16[8,8192]{1,0:T(8,128)(2,1)S(1)}, bf16[8,8192]{1,0:T(8,128)(2,1)S(1)}, u32[]{:S(2)}, u32[]{:S(2)}) collective-permute-start(bf16[8,8192]{1,0:T(8,128)(2,1)S(1)} %get-tuple-element.40), channel_id=1, source_target_pairs={{0,2},{1,3},{2,0},{3,1},{4,6},{5,7},{6,4},{7,5},{8,10},{9,11},{10,... | collective-permute-start | bytes 393224 | tf_op jit(solution)/shard_map/ppermute | solution.py:303
  13.6 6.1 %collective-permute-start.6 = (bf16[8,8192]{1,0:T(8,128)(2,1)S(1)}, bf16[8,8192]{1,0:T(8,128)(2,1)S(1)}, u32[]{:S(2)}, u32[]{:S(2)}) collective-permute-start(bf16[8,8192]{1,0:T(8,128)(2,1)S(1)} %pad_maximum_fusion), channel_id=1, source_target_pairs={{0,4},{1,5},{2,6},{3,7},{4,0},{5,1},{6,2},{7,3},{8,12},{9,13},{10,... | collective-permute-start | bytes 393224 | tf_op jit(solution)/shard_map/ppermute | solution.py:303
  14.1 7.4 %collective-permute-start.5 = (bf16[8,8192]{1,0:T(8,128)(2,1)S(1)}, bf16[8,8192]{1,0:T(8,128)(2,1)S(1)}, u32[]{:S(2)}, u32[]{:S(2)}) collective-permute-start(bf16[8,8192]{1,0:T(8,128)(2,1)S(1)} %pad_maximum_fusion), channel_id=1, source_target_pairs={{0,2},{1,3},{2,0},{3,1},{4,6},{5,7},{6,4},{7,5},{8,10},{9,11},{10,... | collective-permute-start | bytes 393224 | tf_op jit(solution)/shard_map/ppermute | solution.py:303
  14.3 24.1 %collective-permute-start.11 = (bf16[512,4096]{1,0:T(8,128)(2,1)S(1)}, bf16[512,4096]{1,0:T(8,128)(2,1)S(1)}, u32[]{:S(2)}, u32[]{:S(2)}) collective-permute-start(bf16[512,4096]{1,0:T(8,128)(2,1)S(1)} %get-tuple-element.31.turned_ref), channel_id=1, source_target_pairs={{0,1},{1,0},{2,3},{3,2},{4,5},{5,4},{6,7},{7,6},{8,9},{9,8},{10,11... | collective-permute-start | bytes 12582920 | tf_op jit(solution)/shard_map/ppermute | solution.py:303
  14.3 7.1 %collective-permute-start.2 = (bf16[8,8192]{1,0:T(8,128)(2,1)S(1)}, bf16[8,8192]{1,0:T(8,128)(2,1)S(1)}, u32[]{:S(2)}, u32[]{:S(2)}) collective-permute-start(bf16[8,8192]{1,0:T(8,128)(2,1)S(1)} %collective-permute-done), channel_id=1, source_target_pairs={{0,4},{1,5},{2,6},{3,7},{4,0},{5,1},{6,2},{7,3},{8,12},{9,13},{10,... | collective-permute-start | bytes 393224 | tf_op jit(solution)/shard_map/ppermute | solution.py:303
  19.7 5.0 %collective-permute-start.7 = (bf16[8,8192]{1,0:T(8,128)(2,1)S(1)}, bf16[8,8192]{1,0:T(8,128)(2,1)S(1)}, u32[]{:S(2)}, u32[]{:S(2)}) collective-permute-start(bf16[8,8192]{1,0:T(8,128)(2,1)S(1)} %collective-permute-done.6), channel_id=1, source_target_pairs={{0,2},{1,3},{2,0},{3,1},{4,6},{5,7},{6,4},{7,5},{8,10},{9,11},{10,... | collective-permute-start | bytes 393224 | tf_op jit(solution)/shard_map/ppermute | solution.py:303
  21.5 4.8 %collective-permute-start.8 = (bf16[48,8192]{1,0:T(8,128)(2,1)S(1)}, bf16[48,8192]{1,0:T(8,128)(2,1)S(1)}, u32[]{:S(2)}, u32[]{:S(2)}) collective-permute-start(bf16[48,8192]{1,0:T(8,128)(2,1)S(1)} %constant_dynamic-update-slice_fusion.2.refs_0_), channel_id=1, source_target_pairs={{0,1},{1,0},{2,3},{3,2},{4,5},{5,4},{6,7},{7,6},{8,9},{9,8},{10,11... | collective-permute-start | bytes 2359304 | tf_op jit(solution)/shard_map/ppermute | solution.py:303
  24.7 1.6 %collective-permute-start.9 = (bf16[16,8192]{1,0:T(8,128)(2,1)S(1)}, bf16[16,8192]{1,0:T(8,128)(2,1)S(1)}, u32[]{:S(2)}, u32[]{:S(2)}) collective-permute-start(bf16[16,8192]{1,0:T(8,128)(2,1)S(1)} %constant_dynamic-update-slice_fusion.9.refs_1_), channel_id=1, source_target_pairs={{0,1},{1,0},{2,3},{3,2},{4,5},{5,4},{6,7},{7,6},{8,9},{9,8},{10,11... | collective-permute-start | bytes 786440 | tf_op jit(solution)/shard_map/ppermute | solution.py:303
  27.9 10.5 %collective-permute-start.10 = (f32[2,64,512]{2,1,0:T(8,128)S(1)}, f32[2,64,512]{2,1,0:T(8,128)S(1)}, u32[]{:S(2)}, u32[]{:S(2)}) collective-permute-start(f32[2,64,512]{2,1,0:T(8,128)S(1)} %get-tuple-element.30), channel_id=1, source_target_pairs={{0,1},{1,0},{2,3},{3,2},{4,5},{5,4},{6,7},{7,6},{8,9},{9,8},{10,11... | collective-permute-start | bytes 786440 | tf_op jit(solution)/shard_map/ppermute | solution.py:303
  40.2 5.2 %collective-permute-start.13 = (bf16[16,4096]{1,0:T(8,128)(2,1)S(1)}, bf16[16,4096]{1,0:T(8,128)(2,1)S(1)}, u32[]{:S(2)}, u32[]{:S(2)}) collective-permute-start(bf16[16,4096]{1,0:T(8,128)(2,1)S(1)} %get-tuple-element.32), channel_id=1, source_target_pairs={{0,2},{1,3},{2,0},{3,1},{4,6},{5,7},{6,4},{7,5},{8,10},{9,11},{10,... | collective-permute-start | bytes 393224 | tf_op jit(solution)/shard_map/ppermute | solution.py:303
  41.2 7.3 %collective-permute-start.12 = (bf16[16,4096]{1,0:T(8,128)(2,1)S(1)}, bf16[16,4096]{1,0:T(8,128)(2,1)S(1)}, u32[]{:S(2)}, u32[]{:S(2)}) collective-permute-start(bf16[16,4096]{1,0:T(8,128)(2,1)S(1)} %get-tuple-element.35), channel_id=1, source_target_pairs={{0,4},{1,5},{2,6},{3,7},{4,0},{5,1},{6,2},{7,3},{8,12},{9,13},{10,... | collective-permute-start | bytes 393224 | tf_op jit(solution)/shard_map/ppermute | solution.py:303
  45.4 7.3 %collective-permute-start.14 = (bf16[8,4096]{1,0:T(8,128)(2,1)S(1)}, bf16[8,4096]{1,0:T(8,128)(2,1)S(1)}, u32[]{:S(2)}, u32[]{:S(2)}) collective-permute-start(bf16[8,4096]{1,0:T(8,128)(2,1)S(1)} %get-tuple-element.37), channel_id=1, source_target_pairs={{0,8},{1,9},{2,10},{3,11},{4,12},{5,13},{6,14},{7,15},{8,0},{9,1},... | collective-permute-start | bytes 196616 | tf_op jit(solution)/shard_map/ppermute | solution.py:303
  46.3 6.4 %collective-permute-start.15 = (bf16[8,4096]{1,0:T(8,128)(2,1)S(1)}, bf16[8,4096]{1,0:T(8,128)(2,1)S(1)}, u32[]{:S(2)}, u32[]{:S(2)}) collective-permute-start(bf16[8,4096]{1,0:T(8,128)(2,1)S(1)} %get-tuple-element.38), channel_id=1, source_target_pairs={{0,12},{1,13},{2,14},{3,15},{4,8},{5,9},{6,10},{7,11},{8,4},{9,5},... | collective-permute-start | bytes 196616 | tf_op jit(solution)/shard_map/ppermute | solution.py:303
  48.6 4.3 %collective-permute-start.16 = (bf16[8,4096]{1,0:T(8,128)(2,1)S(1)}, bf16[8,4096]{1,0:T(8,128)(2,1)S(1)}, u32[]{:S(2)}, u32[]{:S(2)}) collective-permute-start(bf16[8,4096]{1,0:T(8,128)(2,1)S(1)} %slice.30), channel_id=1, source_target_pairs={{0,2},{1,3},{2,0},{3,1},{4,6},{5,7},{6,4},{7,5},{8,10},{9,11},{10,... | collective-permute-start | bytes 196616 | tf_op jit(solution)/shard_map/ppermute | solution.py:303

commit v9 on v7

--- a/solution.py
+++ b/solution.py
@@ -109,7 +109,11 @@
     middle = rest.astype(jnp.bfloat16)
     low = (rest - middle.astype(jnp.float32)).astype(jnp.bfloat16)
     pick = pick_ref[...]
-    teacher = sum(jnp.dot(pick, piece, preferred_element_type=jnp.float32) for piece in (high, middle, low))
+    teacher = jnp.dot(
+        jnp.concatenate((pick, pick, pick), axis=1),
+        jnp.concatenate((high, middle, low), axis=0),
+        preferred_element_type=jnp.float32,
+    )
     teacher_out[...] = teacher
     student_out[...] = student
     for out in away_out:
@@ -192,11 +196,12 @@
     grad = logit_gradient(teacher_ref[:own], student_ref[:own], norms, is_row, label)
     shift = jnp.where((me & 1) == 0, -vocab, vocab).astype(jnp.float32)
     other = logit_gradient(away_ref[0], away_ref[1], norms, is_row, label + shift)
+    grads = jnp.concatenate((grad, other), axis=1)
     depth = turned_ref.shape[1]
     step = min(512, depth)
     for k in range(0, depth, step):
-        part = jnp.dot(grad, turned_ref[:, k : k + step], preferred_element_type=jnp.float32)
-        part += jnp.dot(other, other_ref[:, k : k + step], preferred_element_type=jnp.float32)
+        heads = jnp.concatenate((turned_ref[:, k : k + step], other_ref[:, k : k + step]), axis=0)
+        part = jnp.dot(grads, heads, preferred_element_type=jnp.float32)
         blocks = [part[b * rows_local : (b + 1) * rows_local] for b in range(8)]
         for out, first, second in ((near_keep, 0, 1), (near_send, 2, 3), (far_keep, 4, 6), (far_send, 5, 7)):
             out[:, k : k + step] = jnp.concatenate((blocks[first], blocks[second]), axis=0).astype(out.dtype)

time: 52.9 us -> 52.9 us (level)
  no operation moved by 1% of the time
where the time goes in v9:
time: 52.9 us; the launch traced here: 52.7 us
  starting transfers between devices  16.3 us (31%)
  waiting for transfers between devices  13.3 us (25%)
  Pallas kernels  10.6 us (20%)
  blocking collectives  10.4 us (20%)
  between operations  0.82 us (2%)
  other arithmetic  0.75 us (1%)
  local copies, waits for them, and re-layouts  0.62 us (1%)
    ppermute x17, starting transfers between devices, swap(): return lax.ppermute(value, 'dp', [(i, i ^ distance) for i in range(n)])  16.3 us
    ppermute x17, waiting for transfers between devices, swap(): return lax.ppermute(value, 'dp', [(i, i ^ distance) for i in range(n)])  13.3 us
    all_to_all x1, blocking collectives, per_device(): stats = lax.all_to_all(stats, 'dp', 0, 0)  10.4 us
    pallas_call x1, Pallas kernels, prepare(): pl.pallas_call(functools.partial(prepare_kernel, rows_local, tuned), in_s...  3.6 us
    pallas_call x1, Pallas kernels, head_gradient(): pl.pallas_call(functools.partial(head_kernel, rows_local, tuned), in_spec...  2.59 us
    pallas_call x1, Pallas kernels, gradient(): pl.pallas_call(functools.partial(grad_kernel if tuned else whole_grad_ker...  1.75 us
    pallas_call x1, Pallas kernels, logits(): pl.pallas_call(functools.partial(logits_kernel, rows_local, tuned, len(hi...  1.58 us
  transfers between devices with their start and end apart: 17, of which 7 were waited for; matrix products, arithmetic and copies ran while one was open for 1% of the time, Pallas kernels for 17%

profile of v9, /device:TPU:0, one launch (start us, length us, event | category | flops | bytes accessed | tf_op | source)
XLA Modules:
  0.0 52.7 jit_solution(17601367247879291860)
XLA Ops:
  0.6 4.1 %collective-permute-start.3 = (bf16[8,4096]{1,0:T(8,128)(2,1)}, bf16[8,4096]{1,0:T(8,128)(2,1)S(1)}, u32[]{:S(2)}, u32[]{:S(2)}) collective-permute-start(bf16[8,4096]{1,0:T(8,128)(2,1)} %teacher_ref.1), channel_id=1, source_target_pairs={{0,8},{1,9},{2,10},{3,11},{4,12},{5,13},{6,14},{7,15},{8,0},{9,1},... | collective-permute-start | bytes 196616 | tf_op jit(solution)/shard_map/ppermute | solution.py:308
  4.7 0.1 collective-permute-start.4
  4.8 0.9 %shard_map.85 = bf16[8,8192]{1,0:T(8,128)(2,1)S(1)} custom-call(bf16[8,4096]{1,0:T(8,128)(2,1)} %teacher_ref.1, bf16[8,4096]{1,0:T(8,128)(2,1)} %student_ref.1), custom_call_target="tpu_custom_call" | custom-call | bytes 262144 | tf_op jit(solution)/shard_map/pallas_call | solution.py:329
  5.7 1.9 %collective-permute-start.1 = (bf16[8,8192]{1,0:T(8,128)(2,1)S(1)}, bf16[8,8192]{1,0:T(8,128)(2,1)S(1)}, u32[]{:S(2)}, u32[]{:S(2)}) collective-permute-start(bf16[8,8192]{1,0:T(8,128)(2,1)S(1)} %shard_map.85), channel_id=1, source_target_pairs={{0,4},{1,5},{2,6},{3,7},{4,0},{5,1},{6,2},{7,3},{8,12},{9,13},{10,... | collective-permute-start | bytes 393224 | tf_op jit(solution)/shard_map/ppermute | solution.py:308
  7.6 1.5 %collective-permute-start = (bf16[8,8192]{1,0:T(8,128)(2,1)S(1)}, bf16[8,8192]{1,0:T(8,128)(2,1)S(1)}, u32[]{:S(2)}, u32[]{:S(2)}) collective-permute-start(bf16[8,8192]{1,0:T(8,128)(2,1)S(1)} %shard_map.85), channel_id=1, source_target_pairs={{0,2},{1,3},{2,0},{3,1},{4,6},{5,7},{6,4},{7,5},{8,10},{9,11},{10,... | collective-permute-start | bytes 393224 | tf_op jit(solution)/shard_map/ppermute | solution.py:308
  9.1 3.6 %shard_map.86 = (bf16[4096,512]{1,0:T(8,128)(2,1)S(1)}, bf16[4096,512]{1,0:T(8,128)(2,1)S(1)}, bf16[128,128]{1,0:T(8,128)(2,1)S(1)}, f32[128,128]{1,0:T(8,128)S(1)}, bf16[512,4096]{1,0:T(8,128)(2,1)S(1)}) custom-call(s32[1]{0:T(128)} %bitcast.me_ref, s32[1,128]{1,0:T(1,128)} %bitcast.5, s32[1,128]{1,0:T(1,128)} %bitcast.6, bf16[4096,512]{1,0:T(8,128)(2,1)} %refs_0_.1, ...), custom_call_target="tpu_custom_call" | custom-call | bytes 16777216 | tf_op jit(solution)/shard_map/pallas_call | solution.py:78
  12.8 0.0 collective-permute-done.4
  12.8 0.5 collective-permute-start.6
  13.3 0.6 %collective-permute-start.5 = (bf16[8,8192]{1,0:T(8,128)(2,1)S(1)}, bf16[8,8192]{1,0:T(8,128)(2,1)S(1)}, u32[]{:S(2)}, u32[]{:S(2)}) collective-permute-start(bf16[8,8192]{1,0:T(8,128)(2,1)S(1)} %pad_maximum_fusion), channel_id=1, source_target_pairs={{0,2},{1,3},{2,0},{3,1},{4,6},{5,7},{6,4},{7,5},{8,10},{9,11},{10,... | collective-permute-start | bytes 393224 | tf_op jit(solution)/shard_map/ppermute | solution.py:308
  13.9 1.5 %collective-permute-start.2 = (bf16[8,8192]{1,0:T(8,128)(2,1)S(1)}, bf16[8,8192]{1,0:T(8,128)(2,1)S(1)}, u32[]{:S(2)}, u32[]{:S(2)}) collective-permute-start(bf16[8,8192]{1,0:T(8,128)(2,1)S(1)} %collective-permute-done), channel_id=1, source_target_pairs={{0,4},{1,5},{2,6},{3,7},{4,0},{5,1},{6,2},{7,3},{8,12},{9,13},{10,... | collective-permute-start | bytes 393224 | tf_op jit(solution)/shard_map/ppermute | solution.py:308
  15.4 3.3 %collective-permute-done.6 = bf16[8,8192]{1,0:T(8,128)(2,1)S(1)} collective-permute-done((bf16[8,8192]{1,0:T(8,128)(2,1)S(1)}, bf16[8,8192]{1,0:T(8,128)(2,1)S(1)}, u32[]{:S(2)}, u32[]{:S(2)}) %collective-permute-start.6) | collective-permute-done | bytes 131104 | tf_op jit(solution)/shard_map/ppermute | solution.py:308
  18.7 1.9 %collective-permute-done.2 = bf16[8,8192]{1,0:T(8,128)(2,1)S(1)} collective-permute-done((bf16[8,8192]{1,0:T(8,128)(2,1)S(1)}, bf16[8,8192]{1,0:T(8,128)(2,1)S(1)}, u32[]{:S(2)}, u32[]{:S(2)}) %collective-permute-start.2) | collective-permute-done | bytes 131104 | tf_op jit(solution)/shard_map/ppermute | solution.py:308
  20.7 0.1 collective-permute-start.8
  20.8 2.9 %collective-permute-done.7 = bf16[8,8192]{1,0:T(8,128)(2,1)S(1)} collective-permute-done((bf16[8,8192]{1,0:T(8,128)(2,1)S(1)}, bf16[8,8192]{1,0:T(8,128)(2,1)S(1)}, u32[]{:S(2)}, u32[]{:S(2)}) %collective-permute-start.7) | collective-permute-done | bytes 131104 | tf_op jit(solution)/shard_map/ppermute | solution.py:308
  23.7 0.1 collective-permute-start.9
  23.8 1.5 %collective-permute-done.9.refs_3_ = bf16[16,8192]{1,0:T(8,128)(2,1)S(1)} collective-permute-done((bf16[16,8192]{1,0:T(8,128)(2,1)S(1)}, bf16[16,8192]{1,0:T(8,128)(2,1)S(1)}, u32[]{:S(2)}, u32[]{:S(2)}) %collective-permute-start.9) | collective-permute-done | bytes 262176 | tf_op jit(solution)/shard_map/ppermute | solution.py:308
  25.3 1.6 %shard_map.87 = (f32[128,512]{1,0:T(8,128)S(1)}, f32[128,512]{1,0:T(8,128)S(1)}, f32[16,4,128]{2,1,0:T(4,128)S(1)}, f32[2,64,512]{2,1,0:T(8,128)S(1)}) custom-call(s32[1]{0:T(128)} %bitcast.me_ref, bf16[128,128]{1,0:T(8,128)(2,1)S(1)} %get-tuple-element.22.pick_ref, f32[128,128]{1,0:T(8,128)S(1)} %get-tuple-element.21.label_ref, ...), custom_call_target="tpu_custom_call" | custom-call | flops 1073741824 | bytes 10485760 | tf_op jit(solution)/shard_map/pallas_call | solution.py:145
  26.9 0.2 collective-permute-start.10
  27.1 10.4 %all_to_all.5.stats_ref = f32[16,4,128]{2,1,0:T(4,128)S(1)} all-to-all(f32[16,4,128]{2,1,0:T(4,128)S(1)} %get-tuple-element.27), channel_id=1, replica_groups=mesh['groups'=2,'dp'=16] {'dp'}, dimensions={0} | all-to-all | bytes 65536 | tf_op jit(solution)/shard_map/all_to_all | solution.py:391
  37.5 1.8 %shard_map.88 = (f32[16,4096]{1,0:T(8,128)S(1)}, bf16[16,4096]{1,0:T(8,128)(2,1)S(1)}, f32[16,4096]{1,0:T(8,128)S(1)}, bf16[16,4096]{1,0:T(8,128)(2,1)S(1)}) custom-call(s32[1]{0:T(128)} %bitcast.me_ref, f32[128,128]{1,0:T(8,128)S(1)} %get-tuple-element.21.label_ref, f32[16,4,128]{2,1,0:T(4,128)S(1)} %all_to_all.5.stats_ref, ...), custom_call_target="tpu_custom_call" | custom-call | flops 536870912 | bytes 6291456 | tf_op jit(solution)/shard_map/pallas_call | solution.py:231
  39.2 0.4 collective-permute-start.13
  39.7 0.1 shard_map.89
  39.8 0.5 slice_bitcast_fusion
  40.3 0.6 %collective-permute-start.12 = (bf16[16,4096]{1,0:T(8,128)(2,1)S(1)}, bf16[16,4096]{1,0:T(8,128)(2,1)S(1)}, u32[]{:S(2)}, u32[]{:S(2)}) collective-permute-start(bf16[16,4096]{1,0:T(8,128)(2,1)S(1)} %get-tuple-element.35), channel_id=1, source_target_pairs={{0,4},{1,5},{2,6},{3,7},{4,0},{5,1},{6,2},{7,3},{8,12},{9,13},{10,... | collective-permute-start | bytes 393224 | tf_op jit(solution)/shard_map/ppermute | solution.py:308
  40.9 2.6 %shard_map.90 = bf16[4096,512]{1,0:T(8,128)(2,1)} custom-call(s32[1]{0:T(128)} %bitcast.me_ref, f32[128,128]{1,0:T(8,128)S(1)} %get-tuple-element.21.label_ref, f32[16,4,128]{2,1,0:T(4,128)S(1)} %all_to_all.5.stats_ref, f32[128,512]{1,0:T(8,128)S(1)} %get-tuple-element.28.teacher_ref, f32[128,512]{1,0:T(8,128)S(1)} %get-tuple-element.29.student_ref, ...), custom_call_target="tpu_custom_call" | custom-call | flops 536870912 | bytes 5242880 | tf_op jit(solution)/shard_map/pallas_call | solution.py:269
  43.5 0.9 %collective-permute-done.13 = bf16[16,4096]{1,0:T(8,128)(2,1)S(1)} collective-permute-done((bf16[16,4096]{1,0:T(8,128)(2,1)S(1)}, bf16[16,4096]{1,0:T(8,128)(2,1)S(1)}, u32[]{:S(2)}, u32[]{:S(2)}) %collective-permute-start.13) | collective-permute-done | bytes 131104 | tf_op jit(solution)/shard_map/ppermute | solution.py:308
  44.5 0.9 %collective-permute-start.14 = (bf16[8,4096]{1,0:T(8,128)(2,1)S(1)}, bf16[8,4096]{1,0:T(8,128)(2,1)S(1)}, u32[]{:S(2)}, u32[]{:S(2)}) collective-permute-start(bf16[8,4096]{1,0:T(8,128)(2,1)S(1)} %get-tuple-element.37), channel_id=1, source_target_pairs={{0,8},{1,9},{2,10},{3,11},{4,12},{5,13},{6,14},{7,15},{8,0},{9,1},... | collective-permute-start | bytes 196616 | tf_op jit(solution)/shard_map/ppermute | solution.py:308
  45.3 2.3 %collective-permute-start.15 = (bf16[8,4096]{1,0:T(8,128)(2,1)S(1)}, bf16[8,4096]{1,0:T(8,128)(2,1)S(1)}, u32[]{:S(2)}, u32[]{:S(2)}) collective-permute-start(bf16[8,4096]{1,0:T(8,128)(2,1)S(1)} %get-tuple-element.38), channel_id=1, source_target_pairs={{0,12},{1,13},{2,14},{3,15},{4,8},{5,9},{6,10},{7,11},{8,4},{9,5},... | collective-permute-start | bytes 196616 | tf_op jit(solution)/shard_map/ppermute | solution.py:308
  47.7 1.5 %collective-permute-start.16 = (bf16[8,4096]{1,0:T(8,128)(2,1)S(1)}, bf16[8,4096]{1,0:T(8,128)(2,1)S(1)}, u32[]{:S(2)}, u32[]{:S(2)}) collective-permute-start(bf16[8,4096]{1,0:T(8,128)(2,1)S(1)} %slice.30), channel_id=1, source_target_pairs={{0,2},{1,3},{2,0},{3,1},{4,6},{5,7},{6,4},{7,5},{8,10},{9,11},{10,... | collective-permute-start | bytes 196616 | tf_op jit(solution)/shard_map/ppermute | solution.py:308
  49.2 2.5 %collective-permute-done.14 = bf16[8,4096]{1,0:T(8,128)(2,1)S(1)} collective-permute-done((bf16[8,4096]{1,0:T(8,128)(2,1)S(1)}, bf16[8,4096]{1,0:T(8,128)(2,1)S(1)}, u32[]{:S(2)}, u32[]{:S(2)}) %collective-permute-start.14) | collective-permute-done | bytes 65568 | tf_op jit(solution)/shard_map/ppermute | solution.py:308
  51.8 0.3 collective-permute-done.16
  52.0 0.7 %convert_add_fusion.1 = f32[8,4096]{1,0:T(8,128)} fusion(f32[8,4096]{1,0:T(8,128)S(1)} %fusion, bf16[8,4096]{1,0:T(8,128)(2,1)S(1)} %collective-permute-done.16), kind=kLoop, calls=%fused_computation.6 | loop fusion | flops 65536 | bytes 327680 | tf_op jit(solution)/shard_map/add | solution.py:371
  (25 shorter events, 0.2 us)
Async XLA Ops:
  0.6 12.1 %collective-permute-start.3 = (bf16[8,4096]{1,0:T(8,128)(2,1)}, bf16[8,4096]{1,0:T(8,128)(2,1)S(1)}, u32[]{:S(2)}, u32[]{:S(2)}) collective-permute-start(bf16[8,4096]{1,0:T(8,128)(2,1)} %teacher_ref.1), channel_id=1, source_target_pairs={{0,8},{1,9},{2,10},{3,11},{4,12},{5,13},{6,14},{7,15},{8,0},{9,1},... | collective-permute-start | bytes 196616 | tf_op jit(solution)/shard_map/ppermute | solution.py:308
  4.7 8.0 %collective-permute-start.4 = (bf16[8,4096]{1,0:T(8,128)(2,1)}, bf16[8,4096]{1,0:T(8,128)(2,1)S(1)}, u32[]{:S(2)}, u32[]{:S(2)}) collective-permute-start(bf16[8,4096]{1,0:T(8,128)(2,1)} %student_ref.1), channel_id=1, source_target_pairs={{0,8},{1,9},{2,10},{3,11},{4,12},{5,13},{6,14},{7,15},{8,0},{9,1},... | collective-permute-start | bytes 196616 | tf_op jit(solution)/shard_map/ppermute | solution.py:308
  5.7 9.7 %collective-permute-start.1 = (bf16[8,8192]{1,0:T(8,128)(2,1)S(1)}, bf16[8,8192]{1,0:T(8,128)(2,1)S(1)}, u32[]{:S(2)}, u32[]{:S(2)}) collective-permute-start(bf16[8,8192]{1,0:T(8,128)(2,1)S(1)} %shard_map.85), channel_id=1, source_target_pairs={{0,4},{1,5},{2,6},{3,7},{4,0},{5,1},{6,2},{7,3},{8,12},{9,13},{10,... | collective-permute-start | bytes 393224 | tf_op jit(solution)/shard_map/ppermute | solution.py:308
  7.6 6.3 %collective-permute-start = (bf16[8,8192]{1,0:T(8,128)(2,1)S(1)}, bf16[8,8192]{1,0:T(8,128)(2,1)S(1)}, u32[]{:S(2)}, u32[]{:S(2)}) collective-permute-start(bf16[8,8192]{1,0:T(8,128)(2,1)S(1)} %shard_map.85), channel_id=1, source_target_pairs={{0,2},{1,3},{2,0},{3,1},{4,6},{5,7},{6,4},{7,5},{8,10},{9,11},{10,... | collective-permute-start | bytes 393224 | tf_op jit(solution)/shard_map/ppermute | solution.py:308
  12.8 5.9 %collective-permute-start.6 = (bf16[8,8192]{1,0:T(8,128)(2,1)S(1)}, bf16[8,8192]{1,0:T(8,128)(2,1)S(1)}, u32[]{:S(2)}, u32[]{:S(2)}) collective-permute-start(bf16[8,8192]{1,0:T(8,128)(2,1)S(1)} %pad_maximum_fusion), channel_id=1, source_target_pairs={{0,4},{1,5},{2,6},{3,7},{4,0},{5,1},{6,2},{7,3},{8,12},{9,13},{10,... | collective-permute-start | bytes 393224 | tf_op jit(solution)/shard_map/ppermute | solution.py:308
  13.3 7.4 %collective-permute-start.5 = (bf16[8,8192]{1,0:T(8,128)(2,1)S(1)}, bf16[8,8192]{1,0:T(8,128)(2,1)S(1)}, u32[]{:S(2)}, u32[]{:S(2)}) collective-permute-start(bf16[8,8192]{1,0:T(8,128)(2,1)S(1)} %pad_maximum_fusion), channel_id=1, source_target_pairs={{0,2},{1,3},{2,0},{3,1},{4,6},{5,7},{6,4},{7,5},{8,10},{9,11},{10,... | collective-permute-start | bytes 393224 | tf_op jit(solution)/shard_map/ppermute | solution.py:308
  13.9 23.6 %collective-permute-start.11 = (bf16[512,4096]{1,0:T(8,128)(2,1)S(1)}, bf16[512,4096]{1,0:T(8,128)(2,1)S(1)}, u32[]{:S(2)}, u32[]{:S(2)}) collective-permute-start(bf16[512,4096]{1,0:T(8,128)(2,1)S(1)} %get-tuple-element.31.turned_ref), channel_id=1, source_target_pairs={{0,1},{1,0},{2,3},{3,2},{4,5},{5,4},{6,7},{7,6},{8,9},{9,8},{10,11... | collective-permute-start | bytes 12582920 | tf_op jit(solution)/shard_map/ppermute | solution.py:308
  13.9 6.7 %collective-permute-start.2 = (bf16[8,8192]{1,0:T(8,128)(2,1)S(1)}, bf16[8,8192]{1,0:T(8,128)(2,1)S(1)}, u32[]{:S(2)}, u32[]{:S(2)}) collective-permute-start(bf16[8,8192]{1,0:T(8,128)(2,1)S(1)} %collective-permute-done), channel_id=1, source_target_pairs={{0,4},{1,5},{2,6},{3,7},{4,0},{5,1},{6,2},{7,3},{8,12},{9,13},{10,... | collective-permute-start | bytes 393224 | tf_op jit(solution)/shard_map/ppermute | solution.py:308
  18.7 5.0 %collective-permute-start.7 = (bf16[8,8192]{1,0:T(8,128)(2,1)S(1)}, bf16[8,8192]{1,0:T(8,128)(2,1)S(1)}, u32[]{:S(2)}, u32[]{:S(2)}) collective-permute-start(bf16[8,8192]{1,0:T(8,128)(2,1)S(1)} %collective-permute-done.6), channel_id=1, source_target_pairs={{0,2},{1,3},{2,0},{3,1},{4,6},{5,7},{6,4},{7,5},{8,10},{9,11},{10,... | collective-permute-start | bytes 393224 | tf_op jit(solution)/shard_map/ppermute | solution.py:308
  20.7 4.6 %collective-permute-start.8 = (bf16[48,8192]{1,0:T(8,128)(2,1)S(1)}, bf16[48,8192]{1,0:T(8,128)(2,1)S(1)}, u32[]{:S(2)}, u32[]{:S(2)}) collective-permute-start(bf16[48,8192]{1,0:T(8,128)(2,1)S(1)} %constant_dynamic-update-slice_fusion.refs_0_), channel_id=1, source_target_pairs={{0,1},{1,0},{2,3},{3,2},{4,5},{5,4},{6,7},{7,6},{8,9},{9,8},{10,11... | collective-permute-start | bytes 2359304 | tf_op jit(solution)/shard_map/ppermute | solution.py:308
  23.7 1.6 %collective-permute-start.9 = (bf16[16,8192]{1,0:T(8,128)(2,1)S(1)}, bf16[16,8192]{1,0:T(8,128)(2,1)S(1)}, u32[]{:S(2)}, u32[]{:S(2)}) collective-permute-start(bf16[16,8192]{1,0:T(8,128)(2,1)S(1)} %constant_dynamic-update-slice_fusion.6.refs_1_), channel_id=1, source_target_pairs={{0,1},{1,0},{2,3},{3,2},{4,5},{5,4},{6,7},{7,6},{8,9},{9,8},{10,11... | collective-permute-start | bytes 786440 | tf_op jit(solution)/shard_map/ppermute | solution.py:308
  26.9 10.6 %collective-permute-start.10 = (f32[2,64,512]{2,1,0:T(8,128)S(1)}, f32[2,64,512]{2,1,0:T(8,128)S(1)}, u32[]{:S(2)}, u32[]{:S(2)}) collective-permute-start(f32[2,64,512]{2,1,0:T(8,128)S(1)} %get-tuple-element.30), channel_id=1, source_target_pairs={{0,1},{1,0},{2,3},{3,2},{4,5},{5,4},{6,7},{7,6},{8,9},{9,8},{10,11... | collective-permute-start | bytes 786440 | tf_op jit(solution)/shard_map/ppermute | solution.py:308
  39.2 5.2 %collective-permute-start.13 = (bf16[16,4096]{1,0:T(8,128)(2,1)S(1)}, bf16[16,4096]{1,0:T(8,128)(2,1)S(1)}, u32[]{:S(2)}, u32[]{:S(2)}) collective-permute-start(bf16[16,4096]{1,0:T(8,128)(2,1)S(1)} %get-tuple-element.32), channel_id=1, source_target_pairs={{0,2},{1,3},{2,0},{3,1},{4,6},{5,7},{6,4},{7,5},{8,10},{9,11},{10,... | collective-permute-start | bytes 393224 | tf_op jit(solution)/shard_map/ppermute | solution.py:308
  40.3 7.3 %collective-permute-start.12 = (bf16[16,4096]{1,0:T(8,128)(2,1)S(1)}, bf16[16,4096]{1,0:T(8,128)(2,1)S(1)}, u32[]{:S(2)}, u32[]{:S(2)}) collective-permute-start(bf16[16,4096]{1,0:T(8,128)(2,1)S(1)} %get-tuple-element.35), channel_id=1, source_target_pairs={{0,4},{1,5},{2,6},{3,7},{4,0},{5,1},{6,2},{7,3},{8,12},{9,13},{10,... | collective-permute-start | bytes 393224 | tf_op jit(solution)/shard_map/ppermute | solution.py:308
  44.5 7.3 %collective-permute-start.14 = (bf16[8,4096]{1,0:T(8,128)(2,1)S(1)}, bf16[8,4096]{1,0:T(8,128)(2,1)S(1)}, u32[]{:S(2)}, u32[]{:S(2)}) collective-permute-start(bf16[8,4096]{1,0:T(8,128)(2,1)S(1)} %get-tuple-element.37), channel_id=1, source_target_pairs={{0,8},{1,9},{2,10},{3,11},{4,12},{5,13},{6,14},{7,15},{8,0},{9,1},... | collective-permute-start | bytes 196616 | tf_op jit(solution)/shard_map/ppermute | solution.py:308
  45.3 6.4 %collective-permute-start.15 = (bf16[8,4096]{1,0:T(8,128)(2,1)S(1)}, bf16[8,4096]{1,0:T(8,128)(2,1)S(1)}, u32[]{:S(2)}, u32[]{:S(2)}) collective-permute-start(bf16[8,4096]{1,0:T(8,128)(2,1)S(1)} %get-tuple-element.38), channel_id=1, source_target_pairs={{0,12},{1,13},{2,14},{3,15},{4,8},{5,9},{6,10},{7,11},{8,4},{9,5},... | collective-permute-start | bytes 196616 | tf_op jit(solution)/shard_map/ppermute | solution.py:308
  47.7 4.3 %collective-permute-start.16 = (bf16[8,4096]{1,0:T(8,128)(2,1)S(1)}, bf16[8,4096]{1,0:T(8,128)(2,1)S(1)}, u32[]{:S(2)}, u32[]{:S(2)}) collective-permute-start(bf16[8,4096]{1,0:T(8,128)(2,1)S(1)} %slice.30), channel_id=1, source_target_pairs={{0,2},{1,3},{2,0},{3,1},{4,6},{5,7},{6,4},{7,5},{8,10},{9,11},{10,... | collective-permute-start | bytes 196616 | tf_op jit(solution)/shard_map/ppermute | solution.py:308

commit v10 on v9

--- a/solution.py
+++ b/solution.py
@@ -186,11 +186,12 @@
 def grad_kernel(
     rows_local, me_ref, label_ref, stats_ref, teacher_ref, student_ref, away_ref, turned_ref, other_ref, *outs
 ):
-    near_keep, near_send, far_keep, far_send = outs
+    near_keep, near_send, far_keep, far_send, norms_out = outs
     me = me_ref[0]
     count, vocab = student_ref.shape
     own = count // 2
     norms = merged(stats_ref)[0]
+    norms_out[...] = norms
     is_row = held_rows((own, count), 0, me, rows_local, True) == lax.broadcasted_iota(jnp.int32, (own, count), 1)
     label = label_ref[:own, 0:1]
     grad = logit_gradient(teacher_ref[:own], student_ref[:own], norms, is_row, label)
@@ -207,9 +208,10 @@
             out[:, k : k + step] = jnp.concatenate((blocks[first], blocks[second]), axis=0).astype(out.dtype)
 
 
-def whole_grad_kernel(rows_local, me_ref, label_ref, stats_ref, teacher_ref, student_ref, head_ref, out_ref):
+def whole_grad_kernel(rows_local, me_ref, label_ref, stats_ref, teacher_ref, student_ref, head_ref, out_ref, norms_out):
     count, vocab = student_ref.shape
     norms = merged(stats_ref)[0]
+    norms_out[...] = norms
     is_row = held_rows((count, count), 0, me_ref[0], rows_local, False) == lax.broadcasted_iota(
         jnp.int32, (count, count), 1
     )
@@ -228,6 +230,7 @@
         shapes = [jax.ShapeDtypeStruct((2 * rows_local, depth), kind) for kind in (jnp.float32, jnp.bfloat16)] * 2
     else:
         shapes = [jax.ShapeDtypeStruct((count, depth), jnp.float32)]
+    shapes.append(jax.ShapeDtypeStruct((2, count), jnp.float32))
     return pl.pallas_call(
         functools.partial(grad_kernel if tuned else whole_grad_kernel, rows_local),
         in_specs=[pl.BlockSpec(memory_space=pltpu.SMEM)] + [vmem] * (2 + len(logits) + len(heads)),
@@ -240,13 +243,13 @@
     )(me, label, stats, *logits, *heads)
 
 
-def head_kernel(rows_local, tuned, me_ref, label_ref, stats_ref, teacher_ref, student_ref, *refs):
+def head_kernel(rows_local, tuned, me_ref, label_ref, norms_ref, teacher_ref, student_ref, *refs):
     *pieces, out_ref, held, sems = refs
     me = me_ref[0]
     count = student_ref.shape[0]
     lanes = lax.broadcasted_iota(jnp.int32, (count, count), 1)
     is_row = held_rows((count, count), 0, me, rows_local, tuned) == lanes
-    norms = merged(stats_ref)[0]
+    norms = norms_ref[...]
     grad = logit_gradient(teacher_ref[...], student_ref[...], norms, is_row, label_ref[:, 0:1])
     steps, step, _ = held.shape
     copies = []
@@ -262,7 +265,7 @@
         copy.wait()
 
 
-def head_gradient(me, label, stats, logits, hidden, depth, rows_local, tuned):
+def head_gradient(me, label, norms, logits, hidden, depth, rows_local, tuned):
     count, vocab = logits[0].shape
     step = min(256, depth)
     vmem = pl.BlockSpec(memory_space=pltpu.VMEM)
@@ -279,7 +282,7 @@
         cost_estimate=pl.CostEstimate(
             flops=2 * count * depth * vocab, bytes_accessed=2 * depth * (vocab + count), transcendentals=2 * count * vocab
         ),
-    )(me, label, stats, *logits, *hidden)
+    )(me, label, norms, *logits, *hidden)
 
 
 def loss_kernel(rows_local, me_ref, stats_ref, loss_out):
@@ -390,14 +393,14 @@
         stats, away = logit.pop(), swap(stats, 1, n)
     stats = lax.all_to_all(stats, "dp", 0, 0)
     head_gradient_of = lambda *done: head_gradient(
-        after(me, *done), label, stats, logit, hidden, depth, rows_local, tuned
+        after(me, *done), label, norms, logit, hidden, depth, rows_local, tuned
     )
     loss_of = lambda *done: row_loss(after(me, *done), stats, rows_local)
     if tuned:
-        parts = gradient(me, label, stats, (*logit, away), turned, rows_local, tuned)
+        *parts, norms = gradient(me, label, stats, (*logit, away), turned, rows_local, tuned)
         grad_hidden, grad_head, loss = scatter_rows(*parts, rows_local, n, head_gradient_of, loss_of)
     else:
-        (part,) = gradient(me, label, stats, logit, heads[1:], rows_local, tuned)
+        part, norms = gradient(me, label, stats, logit, heads[1:], rows_local, tuned)
         grad_head, loss = head_gradient_of(part), loss_of(part)
         grad_hidden = lax.psum_scatter(part, "dp", scatter_dimension=0, tiled=True)
     return (loss[0, :rows_local], grad_hidden, grad_head)

time: 52.9 us -> 52.9 us (level)
  no operation moved by 1% of the time
where the time goes in v10:
time: 52.9 us; the launch traced here: 52.7 us
  starting transfers between devices  16.3 us (31%)
  waiting for transfers between devices  13.3 us (25%)
  Pallas kernels  10.5 us (20%)
  blocking collectives  10.4 us (20%)
  between operations  0.82 us (2%)
  other arithmetic  0.75 us (1%)
  local copies, waits for them, and re-layouts  0.62 us (1%)
    ppermute x17, starting transfers between devices, swap(): return lax.ppermute(value, 'dp', [(i, i ^ distance) for i in range(n)])  16.3 us
    ppermute x17, waiting for transfers between devices, swap(): return lax.ppermute(value, 'dp', [(i, i ^ distance) for i in range(n)])  13.3 us
    all_to_all x1, blocking collectives, per_device(): stats = lax.all_to_all(stats, 'dp', 0, 0)  10.4 us
    pallas_call x1, Pallas kernels, prepare(): pl.pallas_call(functools.partial(prepare_kernel, rows_local, tuned), in_s...  3.6 us
    pallas_call x1, Pallas kernels, head_gradient(): pl.pallas_call(functools.partial(head_kernel, rows_local, tuned), in_spec...  2.55 us
    pallas_call x1, Pallas kernels, gradient(): pl.pallas_call(functools.partial(grad_kernel if tuned else whole_grad_ker...  1.76 us
    pallas_call x1, Pallas kernels, logits(): pl.pallas_call(functools.partial(logits_kernel, rows_local, tuned, len(hi...  1.58 us
  transfers between devices with their start and end apart: 17, of which 7 were waited for; matrix products, arithmetic and copies ran while one was open for 1% of the time, Pallas kernels for 17%

profile of v10, /device:TPU:0, one launch (start us, length us, event | category | flops | bytes accessed | tf_op | source)
XLA Modules:
  0.0 52.7 jit_solution(2766420675841623739)
XLA Ops:
  0.6 4.1 %collective-permute-start.3 = (bf16[8,4096]{1,0:T(8,128)(2,1)}, bf16[8,4096]{1,0:T(8,128)(2,1)S(1)}, u32[]{:S(2)}, u32[]{:S(2)}) collective-permute-start(bf16[8,4096]{1,0:T(8,128)(2,1)} %teacher_ref.1), channel_id=1, source_target_pairs={{0,8},{1,9},{2,10},{3,11},{4,12},{5,13},{6,14},{7,15},{8,0},{9,1},... | collective-permute-start | bytes 196616 | tf_op jit(solution)/shard_map/ppermute | solution.py:311
  4.7 0.1 collective-permute-start.4
  4.8 0.9 %shard_map.85 = bf16[8,8192]{1,0:T(8,128)(2,1)S(1)} custom-call(bf16[8,4096]{1,0:T(8,128)(2,1)} %teacher_ref.1, bf16[8,4096]{1,0:T(8,128)(2,1)} %student_ref.1), custom_call_target="tpu_custom_call" | custom-call | bytes 262144 | tf_op jit(solution)/shard_map/pallas_call | solution.py:332
  5.7 1.9 %collective-permute-start.1 = (bf16[8,8192]{1,0:T(8,128)(2,1)S(1)}, bf16[8,8192]{1,0:T(8,128)(2,1)S(1)}, u32[]{:S(2)}, u32[]{:S(2)}) collective-permute-start(bf16[8,8192]{1,0:T(8,128)(2,1)S(1)} %shard_map.85), channel_id=1, source_target_pairs={{0,4},{1,5},{2,6},{3,7},{4,0},{5,1},{6,2},{7,3},{8,12},{9,13},{10,... | collective-permute-start | bytes 393224 | tf_op jit(solution)/shard_map/ppermute | solution.py:311
  7.6 1.5 %collective-permute-start = (bf16[8,8192]{1,0:T(8,128)(2,1)S(1)}, bf16[8,8192]{1,0:T(8,128)(2,1)S(1)}, u32[]{:S(2)}, u32[]{:S(2)}) collective-permute-start(bf16[8,8192]{1,0:T(8,128)(2,1)S(1)} %shard_map.85), channel_id=1, source_target_pairs={{0,2},{1,3},{2,0},{3,1},{4,6},{5,7},{6,4},{7,5},{8,10},{9,11},{10,... | collective-permute-start | bytes 393224 | tf_op jit(solution)/shard_map/ppermute | solution.py:311
  9.1 3.6 %shard_map.86 = (bf16[4096,512]{1,0:T(8,128)(2,1)S(1)}, bf16[4096,512]{1,0:T(8,128)(2,1)S(1)}, bf16[128,128]{1,0:T(8,128)(2,1)S(1)}, f32[128,128]{1,0:T(8,128)S(1)}, bf16[512,4096]{1,0:T(8,128)(2,1)S(1)}) custom-call(s32[1]{0:T(128)} %bitcast.me_ref, s32[1,128]{1,0:T(1,128)} %bitcast.5, s32[1,128]{1,0:T(1,128)} %bitcast.6, bf16[4096,512]{1,0:T(8,128)(2,1)} %refs_0_.1, ...), custom_call_target="tpu_custom_call" | custom-call | bytes 16777216 | tf_op jit(solution)/shard_map/pallas_call | solution.py:78
  12.8 0.5 collective-permute-start.6
  13.3 0.6 %collective-permute-start.5 = (bf16[8,8192]{1,0:T(8,128)(2,1)S(1)}, bf16[8,8192]{1,0:T(8,128)(2,1)S(1)}, u32[]{:S(2)}, u32[]{:S(2)}) collective-permute-start(bf16[8,8192]{1,0:T(8,128)(2,1)S(1)} %pad_maximum_fusion), channel_id=1, source_target_pairs={{0,2},{1,3},{2,0},{3,1},{4,6},{5,7},{6,4},{7,5},{8,10},{9,11},{10,... | collective-permute-start | bytes 393224 | tf_op jit(solution)/shard_map/ppermute | solution.py:311
  13.9 1.5 %collective-permute-start.2 = (bf16[8,8192]{1,0:T(8,128)(2,1)S(1)}, bf16[8,8192]{1,0:T(8,128)(2,1)S(1)}, u32[]{:S(2)}, u32[]{:S(2)}) collective-permute-start(bf16[8,8192]{1,0:T(8,128)(2,1)S(1)} %collective-permute-done), channel_id=1, source_target_pairs={{0,4},{1,5},{2,6},{3,7},{4,0},{5,1},{6,2},{7,3},{8,12},{9,13},{10,... | collective-permute-start | bytes 393224 | tf_op jit(solution)/shard_map/ppermute | solution.py:311
  15.4 0.0 collective-permute-done.1
  15.4 3.3 %collective-permute-done.6 = bf16[8,8192]{1,0:T(8,128)(2,1)S(1)} collective-permute-done((bf16[8,8192]{1,0:T(8,128)(2,1)S(1)}, bf16[8,8192]{1,0:T(8,128)(2,1)S(1)}, u32[]{:S(2)}, u32[]{:S(2)}) %collective-permute-start.6) | collective-permute-done | bytes 131104 | tf_op jit(solution)/shard_map/ppermute | solution.py:311
  18.7 1.9 %collective-permute-done.2 = bf16[8,8192]{1,0:T(8,128)(2,1)S(1)} collective-permute-done((bf16[8,8192]{1,0:T(8,128)(2,1)S(1)}, bf16[8,8192]{1,0:T(8,128)(2,1)S(1)}, u32[]{:S(2)}, u32[]{:S(2)}) %collective-permute-start.2) | collective-permute-done | bytes 131104 | tf_op jit(solution)/shard_map/ppermute | solution.py:311
  20.7 0.1 collective-permute-start.8
  20.8 2.9 %collective-permute-done.7 = bf16[8,8192]{1,0:T(8,128)(2,1)S(1)} collective-permute-done((bf16[8,8192]{1,0:T(8,128)(2,1)S(1)}, bf16[8,8192]{1,0:T(8,128)(2,1)S(1)}, u32[]{:S(2)}, u32[]{:S(2)}) %collective-permute-start.7) | collective-permute-done | bytes 131104 | tf_op jit(solution)/shard_map/ppermute | solution.py:311
  23.7 0.1 collective-permute-start.9
  23.8 1.5 %collective-permute-done.9.refs_3_ = bf16[16,8192]{1,0:T(8,128)(2,1)S(1)} collective-permute-done((bf16[16,8192]{1,0:T(8,128)(2,1)S(1)}, bf16[16,8192]{1,0:T(8,128)(2,1)S(1)}, u32[]{:S(2)}, u32[]{:S(2)}) %collective-permute-start.9) | collective-permute-done | bytes 262176 | tf_op jit(solution)/shard_map/ppermute | solution.py:311
  25.3 1.6 %shard_map.87 = (f32[128,512]{1,0:T(8,128)S(1)}, f32[128,512]{1,0:T(8,128)S(1)}, f32[16,4,128]{2,1,0:T(4,128)S(1)}, f32[2,64,512]{2,1,0:T(8,128)S(1)}) custom-call(s32[1]{0:T(128)} %bitcast.me_ref, bf16[128,128]{1,0:T(8,128)(2,1)S(1)} %get-tuple-element.23.pick_ref, f32[128,128]{1,0:T(8,128)S(1)} %get-tuple-element.22.label_ref, ...), custom_call_target="tpu_custom_call" | custom-call | flops 1073741824 | bytes 10485760 | tf_op jit(solution)/shard_map/pallas_call | solution.py:145
  26.9 0.2 collective-permute-start.10
  27.1 10.4 %all_to_all.5.stats_ref = f32[16,4,128]{2,1,0:T(4,128)S(1)} all-to-all(f32[16,4,128]{2,1,0:T(4,128)S(1)} %get-tuple-element.28), channel_id=1, replica_groups=mesh['groups'=2,'dp'=16] {'dp'}, dimensions={0} | all-to-all | bytes 65536 | tf_op jit(solution)/shard_map/all_to_all | solution.py:394
  37.5 1.8 %shard_map.88 = (f32[16,4096]{1,0:T(8,128)S(1)}, bf16[16,4096]{1,0:T(8,128)(2,1)S(1)}, f32[16,4096]{1,0:T(8,128)S(1)}, bf16[16,4096]{1,0:T(8,128)(2,1)S(1)}, f32[2,128]{1,0:T(2,128)S(1)}) custom-call(s32[1]{0:T(128)} %bitcast.me_ref, f32[128,128]{1,0:T(8,128)S(1)} %get-tuple-element.22.label_ref, f32[16,4,128]{2,1,0:T(4,128)S(1)} %all_to_all.5.stats_ref, ...), custom_call_target="tpu_custom_call" | custom-call | flops 536870912 | bytes 6291456 | tf_op jit(solution)/shard_map/pallas_call | solution.py:234
  39.2 0.4 collective-permute-start.13
  39.7 0.1 shard_map.89
  39.8 0.5 slice_bitcast_fusion
  40.3 0.6 %collective-permute-start.12 = (bf16[16,4096]{1,0:T(8,128)(2,1)S(1)}, bf16[16,4096]{1,0:T(8,128)(2,1)S(1)}, u32[]{:S(2)}, u32[]{:S(2)}) collective-permute-start(bf16[16,4096]{1,0:T(8,128)(2,1)S(1)} %get-tuple-element.36), channel_id=1, source_target_pairs={{0,4},{1,5},{2,6},{3,7},{4,0},{5,1},{6,2},{7,3},{8,12},{9,13},{10,... | collective-permute-start | bytes 393224 | tf_op jit(solution)/shard_map/ppermute | solution.py:311
  40.9 2.6 %shard_map.90 = bf16[4096,512]{1,0:T(8,128)(2,1)} custom-call(s32[1]{0:T(128)} %bitcast.me_ref, f32[128,128]{1,0:T(8,128)S(1)} %get-tuple-element.22.label_ref, f32[2,128]{1,0:T(2,128)S(1)} %get-tuple-element.38.norms_ref, f32[128,512]{1,0:T(8,128)S(1)} %get-tuple-element.29.teacher_ref, f32[128,512]{1,0:T(8,128)S(1)} %get-tuple-element.30.student_ref, ...), custom_call_target="tpu_custom_call" | custom-call | flops 536870912 | bytes 5242880 | tf_op jit(solution)/shard_map/pallas_call | solution.py:272
  43.5 0.9 %collective-permute-done.13 = bf16[16,4096]{1,0:T(8,128)(2,1)S(1)} collective-permute-done((bf16[16,4096]{1,0:T(8,128)(2,1)S(1)}, bf16[16,4096]{1,0:T(8,128)(2,1)S(1)}, u32[]{:S(2)}, u32[]{:S(2)}) %collective-permute-start.13) | collective-permute-done | bytes 131104 | tf_op jit(solution)/shard_map/ppermute | solution.py:311
  44.5 0.9 %collective-permute-start.14 = (bf16[8,4096]{1,0:T(8,128)(2,1)S(1)}, bf16[8,4096]{1,0:T(8,128)(2,1)S(1)}, u32[]{:S(2)}, u32[]{:S(2)}) collective-permute-start(bf16[8,4096]{1,0:T(8,128)(2,1)S(1)} %get-tuple-element.39), channel_id=1, source_target_pairs={{0,8},{1,9},{2,10},{3,11},{4,12},{5,13},{6,14},{7,15},{8,0},{9,1},... | collective-permute-start | bytes 196616 | tf_op jit(solution)/shard_map/ppermute | solution.py:311
  45.3 2.3 %collective-permute-start.15 = (bf16[8,4096]{1,0:T(8,128)(2,1)S(1)}, bf16[8,4096]{1,0:T(8,128)(2,1)S(1)}, u32[]{:S(2)}, u32[]{:S(2)}) collective-permute-start(bf16[8,4096]{1,0:T(8,128)(2,1)S(1)} %get-tuple-element.40), channel_id=1, source_target_pairs={{0,12},{1,13},{2,14},{3,15},{4,8},{5,9},{6,10},{7,11},{8,4},{9,5},... | collective-permute-start | bytes 196616 | tf_op jit(solution)/shard_map/ppermute | solution.py:311
  47.7 1.5 %collective-permute-start.16 = (bf16[8,4096]{1,0:T(8,128)(2,1)S(1)}, bf16[8,4096]{1,0:T(8,128)(2,1)S(1)}, u32[]{:S(2)}, u32[]{:S(2)}) collective-permute-start(bf16[8,4096]{1,0:T(8,128)(2,1)S(1)} %slice.30), channel_id=1, source_target_pairs={{0,2},{1,3},{2,0},{3,1},{4,6},{5,7},{6,4},{7,5},{8,10},{9,11},{10,... | collective-permute-start | bytes 196616 | tf_op jit(solution)/shard_map/ppermute | solution.py:311
  49.2 2.5 %collective-permute-done.14 = bf16[8,4096]{1,0:T(8,128)(2,1)S(1)} collective-permute-done((bf16[8,4096]{1,0:T(8,128)(2,1)S(1)}, bf16[8,4096]{1,0:T(8,128)(2,1)S(1)}, u32[]{:S(2)}, u32[]{:S(2)}) %collective-permute-start.14) | collective-permute-done | bytes 65568 | tf_op jit(solution)/shard_map/ppermute | solution.py:311
  51.8 0.3 collective-permute-done.16
  52.0 0.7 %convert_add_fusion.1 = f32[8,4096]{1,0:T(8,128)} fusion(f32[8,4096]{1,0:T(8,128)S(1)} %fusion, bf16[8,4096]{1,0:T(8,128)(2,1)S(1)} %collective-permute-done.16), kind=kLoop, calls=%fused_computation.6 | loop fusion | flops 65536 | bytes 327680 | tf_op jit(solution)/shard_map/add | solution.py:374
  (25 shorter events, 0.2 us)
Async XLA Ops:
  0.6 12.1 %collective-permute-start.3 = (bf16[8,4096]{1,0:T(8,128)(2,1)}, bf16[8,4096]{1,0:T(8,128)(2,1)S(1)}, u32[]{:S(2)}, u32[]{:S(2)}) collective-permute-start(bf16[8,4096]{1,0:T(8,128)(2,1)} %teacher_ref.1), channel_id=1, source_target_pairs={{0,8},{1,9},{2,10},{3,11},{4,12},{5,13},{6,14},{7,15},{8,0},{9,1},... | collective-permute-start | bytes 196616 | tf_op jit(solution)/shard_map/ppermute | solution.py:311
  4.7 8.0 %collective-permute-start.4 = (bf16[8,4096]{1,0:T(8,128)(2,1)}, bf16[8,4096]{1,0:T(8,128)(2,1)S(1)}, u32[]{:S(2)}, u32[]{:S(2)}) collective-permute-start(bf16[8,4096]{1,0:T(8,128)(2,1)} %student_ref.1), channel_id=1, source_target_pairs={{0,8},{1,9},{2,10},{3,11},{4,12},{5,13},{6,14},{7,15},{8,0},{9,1},... | collective-permute-start | bytes 196616 | tf_op jit(solution)/shard_map/ppermute | solution.py:311
  5.7 9.7 %collective-permute-start.1 = (bf16[8,8192]{1,0:T(8,128)(2,1)S(1)}, bf16[8,8192]{1,0:T(8,128)(2,1)S(1)}, u32[]{:S(2)}, u32[]{:S(2)}) collective-permute-start(bf16[8,8192]{1,0:T(8,128)(2,1)S(1)} %shard_map.85), channel_id=1, source_target_pairs={{0,4},{1,5},{2,6},{3,7},{4,0},{5,1},{6,2},{7,3},{8,12},{9,13},{10,... | collective-permute-start | bytes 393224 | tf_op jit(solution)/shard_map/ppermute | solution.py:311
  7.6 6.3 %collective-permute-start = (bf16[8,8192]{1,0:T(8,128)(2,1)S(1)}, bf16[8,8192]{1,0:T(8,128)(2,1)S(1)}, u32[]{:S(2)}, u32[]{:S(2)}) collective-permute-start(bf16[8,8192]{1,0:T(8,128)(2,1)S(1)} %shard_map.85), channel_id=1, source_target_pairs={{0,2},{1,3},{2,0},{3,1},{4,6},{5,7},{6,4},{7,5},{8,10},{9,11},{10,... | collective-permute-start | bytes 393224 | tf_op jit(solution)/shard_map/ppermute | solution.py:311
  12.8 5.9 %collective-permute-start.6 = (bf16[8,8192]{1,0:T(8,128)(2,1)S(1)}, bf16[8,8192]{1,0:T(8,128)(2,1)S(1)}, u32[]{:S(2)}, u32[]{:S(2)}) collective-permute-start(bf16[8,8192]{1,0:T(8,128)(2,1)S(1)} %pad_maximum_fusion), channel_id=1, source_target_pairs={{0,4},{1,5},{2,6},{3,7},{4,0},{5,1},{6,2},{7,3},{8,12},{9,13},{10,... | collective-permute-start | bytes 393224 | tf_op jit(solution)/shard_map/ppermute | solution.py:311
  13.3 7.4 %collective-permute-start.5 = (bf16[8,8192]{1,0:T(8,128)(2,1)S(1)}, bf16[8,8192]{1,0:T(8,128)(2,1)S(1)}, u32[]{:S(2)}, u32[]{:S(2)}) collective-permute-start(bf16[8,8192]{1,0:T(8,128)(2,1)S(1)} %pad_maximum_fusion), channel_id=1, source_target_pairs={{0,2},{1,3},{2,0},{3,1},{4,6},{5,7},{6,4},{7,5},{8,10},{9,11},{10,... | collective-permute-start | bytes 393224 | tf_op jit(solution)/shard_map/ppermute | solution.py:311
  13.9 23.6 %collective-permute-start.11 = (bf16[512,4096]{1,0:T(8,128)(2,1)S(1)}, bf16[512,4096]{1,0:T(8,128)(2,1)S(1)}, u32[]{:S(2)}, u32[]{:S(2)}) collective-permute-start(bf16[512,4096]{1,0:T(8,128)(2,1)S(1)} %get-tuple-element.32.turned_ref), channel_id=1, source_target_pairs={{0,1},{1,0},{2,3},{3,2},{4,5},{5,4},{6,7},{7,6},{8,9},{9,8},{10,11... | collective-permute-start | bytes 12582920 | tf_op jit(solution)/shard_map/ppermute | solution.py:311
  13.9 6.7 %collective-permute-start.2 = (bf16[8,8192]{1,0:T(8,128)(2,1)S(1)}, bf16[8,8192]{1,0:T(8,128)(2,1)S(1)}, u32[]{:S(2)}, u32[]{:S(2)}) collective-permute-start(bf16[8,8192]{1,0:T(8,128)(2,1)S(1)} %collective-permute-done), channel_id=1, source_target_pairs={{0,4},{1,5},{2,6},{3,7},{4,0},{5,1},{6,2},{7,3},{8,12},{9,13},{10,... | collective-permute-start | bytes 393224 | tf_op jit(solution)/shard_map/ppermute | solution.py:311
  18.7 5.0 %collective-permute-start.7 = (bf16[8,8192]{1,0:T(8,128)(2,1)S(1)}, bf16[8,8192]{1,0:T(8,128)(2,1)S(1)}, u32[]{:S(2)}, u32[]{:S(2)}) collective-permute-start(bf16[8,8192]{1,0:T(8,128)(2,1)S(1)} %collective-permute-done.6), channel_id=1, source_target_pairs={{0,2},{1,3},{2,0},{3,1},{4,6},{5,7},{6,4},{7,5},{8,10},{9,11},{10,... | collective-permute-start | bytes 393224 | tf_op jit(solution)/shard_map/ppermute | solution.py:311
  20.7 4.6 %collective-permute-start.8 = (bf16[48,8192]{1,0:T(8,128)(2,1)S(1)}, bf16[48,8192]{1,0:T(8,128)(2,1)S(1)}, u32[]{:S(2)}, u32[]{:S(2)}) collective-permute-start(bf16[48,8192]{1,0:T(8,128)(2,1)S(1)} %constant_dynamic-update-slice_fusion.refs_0_), channel_id=1, source_target_pairs={{0,1},{1,0},{2,3},{3,2},{4,5},{5,4},{6,7},{7,6},{8,9},{9,8},{10,11... | collective-permute-start | bytes 2359304 | tf_op jit(solution)/shard_map/ppermute | solution.py:311
  23.7 1.6 %collective-permute-start.9 = (bf16[16,8192]{1,0:T(8,128)(2,1)S(1)}, bf16[16,8192]{1,0:T(8,128)(2,1)S(1)}, u32[]{:S(2)}, u32[]{:S(2)}) collective-permute-start(bf16[16,8192]{1,0:T(8,128)(2,1)S(1)} %constant_dynamic-update-slice_fusion.6.refs_1_), channel_id=1, source_target_pairs={{0,1},{1,0},{2,3},{3,2},{4,5},{5,4},{6,7},{7,6},{8,9},{9,8},{10,11... | collective-permute-start | bytes 786440 | tf_op jit(solution)/shard_map/ppermute | solution.py:311
  26.9 10.6 %collective-permute-start.10 = (f32[2,64,512]{2,1,0:T(8,128)S(1)}, f32[2,64,512]{2,1,0:T(8,128)S(1)}, u32[]{:S(2)}, u32[]{:S(2)}) collective-permute-start(f32[2,64,512]{2,1,0:T(8,128)S(1)} %get-tuple-element.31), channel_id=1, source_target_pairs={{0,1},{1,0},{2,3},{3,2},{4,5},{5,4},{6,7},{7,6},{8,9},{9,8},{10,11... | collective-permute-start | bytes 786440 | tf_op jit(solution)/shard_map/ppermute | solution.py:311
  39.2 5.2 %collective-permute-start.13 = (bf16[16,4096]{1,0:T(8,128)(2,1)S(1)}, bf16[16,4096]{1,0:T(8,128)(2,1)S(1)}, u32[]{:S(2)}, u32[]{:S(2)}) collective-permute-start(bf16[16,4096]{1,0:T(8,128)(2,1)S(1)} %get-tuple-element.33), channel_id=1, source_target_pairs={{0,2},{1,3},{2,0},{3,1},{4,6},{5,7},{6,4},{7,5},{8,10},{9,11},{10,... | collective-permute-start | bytes 393224 | tf_op jit(solution)/shard_map/ppermute | solution.py:311
  40.3 7.3 %collective-permute-start.12 = (bf16[16,4096]{1,0:T(8,128)(2,1)S(1)}, bf16[16,4096]{1,0:T(8,128)(2,1)S(1)}, u32[]{:S(2)}, u32[]{:S(2)}) collective-permute-start(bf16[16,4096]{1,0:T(8,128)(2,1)S(1)} %get-tuple-element.36), channel_id=1, source_target_pairs={{0,4},{1,5},{2,6},{3,7},{4,0},{5,1},{6,2},{7,3},{8,12},{9,13},{10,... | collective-permute-start | bytes 393224 | tf_op jit(solution)/shard_map/ppermute | solution.py:311
  44.5 7.3 %collective-permute-start.14 = (bf16[8,4096]{1,0:T(8,128)(2,1)S(1)}, bf16[8,4096]{1,0:T(8,128)(2,1)S(1)}, u32[]{:S(2)}, u32[]{:S(2)}) collective-permute-start(bf16[8,4096]{1,0:T(8,128)(2,1)S(1)} %get-tuple-element.39), channel_id=1, source_target_pairs={{0,8},{1,9},{2,10},{3,11},{4,12},{5,13},{6,14},{7,15},{8,0},{9,1},... | collective-permute-start | bytes 196616 | tf_op jit(solution)/shard_map/ppermute | solution.py:311
  45.3 6.4 %collective-permute-start.15 = (bf16[8,4096]{1,0:T(8,128)(2,1)S(1)}, bf16[8,4096]{1,0:T(8,128)(2,1)S(1)}, u32[]{:S(2)}, u32[]{:S(2)}) collective-permute-start(bf16[8,4096]{1,0:T(8,128)(2,1)S(1)} %get-tuple-element.40), channel_id=1, source_target_pairs={{0,12},{1,13},{2,14},{3,15},{4,8},{5,9},{6,10},{7,11},{8,4},{9,5},... | collective-permute-start | bytes 196616 | tf_op jit(solution)/shard_map/ppermute | solution.py:311
  47.7 4.3 %collective-permute-start.16 = (bf16[8,4096]{1,0:T(8,128)(2,1)S(1)}, bf16[8,4096]{1,0:T(8,128)(2,1)S(1)}, u32[]{:S(2)}, u32[]{:S(2)}) collective-permute-start(bf16[8,4096]{1,0:T(8,128)(2,1)S(1)} %slice.30), channel_id=1, source_target_pairs={{0,2},{1,3},{2,0},{3,1},{4,6},{5,7},{6,4},{7,5},{8,10},{9,11},{10,... | collective-permute-start | bytes 196616 | tf_op jit(solution)/shard_map/ppermute | solution.py:311
